TPU v7x, 32 devices: a whole 2x2x4 slice. The times are simulated.
32 devices in a mesh: series: 8 (over z, y), tm: 4 (over x, core).
Axes of the slice: x: 2, y: 2, z: 4, core: 2. Of those that a mesh axis runs over, the one named last changes fastest.
Arguments:
- observed: bfloat16 [131072, 2048], P('series', 'tm'), may hold values from -6 to 6
- flags: int32 [131072, 16], P('series', 'tm'), may hold values 0 or 1
- factors: bfloat16 [131072, 64], P('series'), may hold values from -0.75 to 0.75
- basis: float32 [64, 2048], P(None, 'tm'), may hold values from -6 to 6
- tcn_weights: float32 [4, 64, 64], replicated, may hold values from -0.5 to 0.5
- tcn_bias: float32 [2, 64], replicated, may hold values from -3 to 3
- dilations: int32 [2], replicated, may hold values from 1 to 64, as said below
Outputs:
- new_basis: float32 [64, 2048], P(None, 'tm')
- new_factors: bfloat16 [131072, 64], P('series')
Inputs may be any that keep to these rules, and one draw needn't show every extreme that they name: `dilations`: each dilation is between 1 and 64, and at least one of the two equals 64.
All inputs are finite; a program needn't handle non-finite values. No bound on the sum of `flags` on one device may be relied on, other than what follows from the above.
Results may differ from a plain program's by a relative error of at most 0.002.
The roundings to bfloat16 on the way count: a program that leaves them out, or rounds other values in their place, can miss the bound.
Values may be sent and summed in bfloat16 or wider, within the bound.
No kernel may reach another device: no remote copies, remote signals or barrier semaphores. Data moves between devices by JAX's collectives and lax.ppermute only.
A program may use at most 192 MiB of HBM per device.

v0:
```python
import math

import jax
import jax.numpy as jnp
from jax import lax
from jax.sharding import PartitionSpec as P

DMAX = 64
BLK = 128
ITERS = 3


def for_sending(x):
    return jax.tree.map(lambda a: a.astype(jnp.bfloat16) if a.dtype == jnp.float32 else a, x)


def shifted_2(x, axis, by):
    count = lax.axis_size(axis)
    pairs = [(i, i + by) for i in range(count) if 0 <= i + by < count]
    return lax.ppermute(x, axis, pairs)


def delay(field, steps):
    padded = jnp.pad(field, ((0, 0), (DMAX, 0)))
    return lax.dynamic_slice_in_dim(padded, DMAX - steps, field.shape[1], 1)


def mix(weight, field):
    return jnp.dot(weight, field, precision=lax.Precision.HIGHEST)


def tcn_error(padded, tcn_weights, tcn_bias, dilations, keep):
    shifted = delay(padded, jnp.int32(1))
    hidden = jax.nn.relu(
        mix(tcn_weights[0], delay(shifted, dilations[0]))
        + mix(tcn_weights[1], shifted)
        + tcn_bias[0][:, None]
    )
    output = (
        mix(tcn_weights[2], delay(hidden, dilations[1]))
        + mix(tcn_weights[3], hidden)
        + tcn_bias[1][:, None]
    )
    return (padded - shifted - output)[:, -keep:]


def resid_block(factors, observed, flags, basis_b):
    pred = jnp.dot(factors, basis_b, preferred_element_type=jnp.float32)
    diff = (pred - observed.astype(jnp.float32)).reshape(factors.shape[0], -1, BLK) * flags[
        :, :, None
    ].astype(jnp.float32)
    return diff.reshape(factors.shape[0], -1).astype(jnp.bfloat16)


def reg_gradient(current, tcn_weights, tcn_bias, dilations):
    width = 1 + 2 * DMAX
    local_cols = current.shape[1]
    earlier = shifted_2(for_sending(current[:, local_cols - width :]), "tm", 1)
    padded = jnp.concatenate([earlier, current], axis=1)
    error, pull = jax.vjp(
        lambda v: tcn_error(v, tcn_weights, tcn_bias, dilations, local_cols), padded
    )
    grad_pad = pull(0.1 * error)[0]
    later = shifted_2(for_sending(grad_pad[:, :width]), "tm", -1)
    own = grad_pad[:, width:]
    return own.at[:, local_cols - width :].add(later)


def shards(observed, flags, factors, basis, tcn_weights, tcn_bias, dilations):
    local_rows = factors.shape[0]
    local_cols = basis.shape[1]
    rank = basis.shape[0]
    series_count = lax.axis_size("series")
    time_count = lax.axis_size("tm")
    data_scale = 1.0 / math.sqrt(local_rows * series_count)
    entries = rank * local_cols * time_count
    current = basis
    for step in range(ITERS):
        basis_b = current.astype(jnp.bfloat16)
        resid = resid_block(factors, observed, flags, basis_b)
        local_grad = lax.dot_general(
            factors, resid, (((0,), (0,)), ((), ())), preferred_element_type=jnp.float32
        )
        reg_grad = reg_gradient(current, tcn_weights, tcn_bias, dilations)
        data_grad = lax.psum(local_grad, "series")
        grad = data_grad * data_scale + reg_grad
        total = lax.psum(jnp.sum(grad * grad), "tm")
        current = current - 0.1 * grad / jnp.sqrt(total / entries + 1e-06)
    basis_b = current.astype(jnp.bfloat16)
    resid = resid_block(factors, observed, flags, basis_b)
    coef = 0.1 / math.sqrt(local_cols * time_count)
    share_rows = local_rows // time_count
    fgrad_rows = lax.psum_scatter(
        lax.dot_general(
            resid, basis_b, (((1,), (1,)), ((), ())), preferred_element_type=jnp.float32
        ),
        "tm",
        scatter_dimension=0,
        tiled=True,
    )
    own_rows = lax.dynamic_slice_in_dim(factors, lax.axis_index("tm") * share_rows, share_rows, 0)
    updated = (own_rows.astype(jnp.float32) - coef * fgrad_rows).astype(jnp.bfloat16)
    new_factors = lax.all_gather(updated, "tm", axis=0, tiled=True)
    return (current, new_factors)


def solution(mesh):
    return jax.shard_map(
        shards,
        mesh=mesh,
        in_specs=(
            P("series", "tm"),
            P("series", "tm"),
            P("series", None),
            P(None, "tm"),
            P(),
            P(),
            P(),
        ),
        out_specs=(P(None, "tm"), P("series", None)),
        check_vma=False,
    )
```

profile of v0, /device:TPU:0, one launch (start us, length us, event | category | flops | bytes accessed | tf_op | source)
XLA Modules:
  0.0 524.1 jit_solution(65079634500645742)
XLA Ops:
  8.2 2.3 collective-permute-start
  11.3 1.3 fusion.145
  16.2 5.0 copy.9
  22.4 1.2 fusion.51
  23.6 1.2 fusion.20
  24.7 1.2 fusion.48
  28.1 1.2 convolution_bitcast_fusion.10
  30.1 1.2 fusion.32
  33.6 1.1 fusion.30
  34.9 1.9 collective-permute-start.1
  36.9 31.4 %mul.77 = f32[16384,4,128]{2,1,0:T(4,128)} broadcast(f32[16384,4]{1,0:T(8,128)} %copy.9), dimensions={0,1} | broadcast | bytes 33816576 | tf_op jit(solution)/shard_map/mul | solution.py:49
  68.3 26.6 %fusion.35 = f32[64,512]{1,0:T(8,128)} fusion(bf16[16384,64]{0,1:T(8,128)(2,1)S(1)} %copy-done, bf16[16384,512]{1,0:T(8,128)(2,1)} %param.13, f32[2048,8,4,128]{3,2,1,0:T(4,128)} %bitcast.184, bf16[64,512]{1,0:T(8,128)(2,1)S(1)} %convert_element_type.77), kind=kOutput, calls=%fused_computation.57 | convolution fusion | flops 2181038080 | bytes 52625408 | tf_op jit(solution)/shard_map/dot_general | solution.py:81
  95.7 73.6 %all-reduce.19.cloned.1.call-done = f32[64,512]{1,0:T(8,128)} async-done(((f32[64,512]{1,0:T(8,128)}), f32[64,512]{1,0:T(8,128)}) %all-reduce.19.cloned.1.call-update) | async-done | bytes 131088 | tf_op jit(solution)/shard_map/psum | solution.py:85
  169.3 1.5 multiply_reduce_fusion.2
  170.9 6.3 %psum.43 = f32[]{:T(128)} all-reduce(f32[]{:T(128)} %multiply_reduce_fusion.2), channel_id=1, replica_groups=mesh['series'=8,'tm'=4] {'tm'}, use_global_device_ids=true, to_apply=%region_2.3 | all-reduce | flops 1 | bytes 8 | tf_op jit(solution)/shard_map/psum | solution.py:87
  178.9 1.8 collective-permute-start.2
  187.3 1.5 collective-permute-start.3
  188.8 26.5 %fusion.33 = f32[64,512]{1,0:T(8,128)} fusion(bf16[16384,64]{0,1:T(8,128)(2,1)S(1)} %copy-done, bf16[16384,512]{1,0:T(8,128)(2,1)} %param.13, f32[2048,8,4,128]{3,2,1,0:T(4,128)} %bitcast.185, bf16[64,512]{1,0:T(8,128)(2,1)S(1)} %get-tuple-element.40), kind=kOutput, calls=%fused_computation.55 | convolution fusion | flops 2181038080 | bytes 52625408 | tf_op jit(solution)/shard_map/dot_general | solution.py:81
  216.0 71.9 %all-reduce.21.cloned.1.call-done = f32[64,512]{1,0:T(8,128)} async-done(((f32[64,512]{1,0:T(8,128)}), f32[64,512]{1,0:T(8,128)}) %all-reduce.21.cloned.1.call-update) | async-done | bytes 131088 | tf_op jit(solution)/shard_map/psum | solution.py:85
  288.0 1.5 multiply_reduce_fusion.1
  289.5 6.3 %psum.45 = f32[]{:T(128)} all-reduce(f32[]{:T(128)} %multiply_reduce_fusion.1), channel_id=1, replica_groups=mesh['series'=8,'tm'=4] {'tm'}, use_global_device_ids=true, to_apply=%region_5.6 | all-reduce | flops 1 | bytes 8 | tf_op jit(solution)/shard_map/psum | solution.py:87
  297.5 1.8 collective-permute-start.4
  305.9 1.5 collective-permute-start.5
  307.4 26.5 %fusion.34 = f32[64,512]{1,0:T(8,128)} fusion(bf16[16384,64]{0,1:T(8,128)(2,1)S(1)} %copy-done, bf16[16384,512]{1,0:T(8,128)(2,1)} %param.13, f32[2048,8,4,128]{3,2,1,0:T(4,128)} %bitcast.186, bf16[64,512]{1,0:T(8,128)(2,1)S(1)} %get-tuple-element.38), kind=kOutput, calls=%fused_computation.56 | convolution fusion | flops 2181038080 | bytes 52625408 | tf_op jit(solution)/shard_map/dot_general | solution.py:81
  334.6 71.9 %all-reduce.23.cloned.1.call-done = f32[64,512]{1,0:T(8,128)} async-done(((f32[64,512]{1,0:T(8,128)}), f32[64,512]{1,0:T(8,128)}) %all-reduce.23.cloned.1.call-update) | async-done | bytes 131088 | tf_op jit(solution)/shard_map/psum | solution.py:85
  406.6 1.5 multiply_reduce_fusion
  408.1 6.5 %psum.47 = f32[]{:T(128)} all-reduce(f32[]{:T(128)} %multiply_reduce_fusion), channel_id=1, replica_groups=mesh['series'=8,'tm'=4] {'tm'}, use_global_device_ids=true, to_apply=%region_8.9 | all-reduce | flops 1 | bytes 8 | tf_op jit(solution)/shard_map/psum | solution.py:87
  416.3 28.8 %fusion.9 = f32[16384,64]{0,1:T(8,128)} fusion(bf16[16384,512]{1,0:T(8,128)(2,1)} %param.13, f32[2048,8,4,128]{3,2,1,0:T(4,128)} %bitcast.187, bf16[16384,64]{0,1:T(8,128)(2,1)S(1)} %copy-done, f32[64,512]{1,0:T(8,128)S(1)} %divide_subtract_fusion), kind=kOutput, calls=%fused_computation.13 | convolution fusion | flops 2181103616 | bytes 56754176 | tf_op jit(solution)/shard_map/dot_general | solution.py:94
  445.2 44.1 %reduce-scatter.2.cloned.1.call-done = f32[4096,64]{0,1:T(8,128)} async-done(((f32[16384,64]{0,1:T(8,128)}), f32[4096,64]{0,1:T(8,128)}) %reduce-scatter.2.cloned.1.call-update) | async-done | bytes 1048592 | tf_op jit(solution)/shard_map/reduce_scatter | solution.py:93
  489.3 2.1 subtract_convert_fusion
  491.5 22.7 %all-gather.2.cloned.1.call-done = bf16[16384,64]{0,1:T(8,128)(2,1)} async-done(((bf16[4096,64]{0,1:T(8,128)(2,1)}), bf16[16384,64]{0,1:T(8,128)(2,1)}) %all-gather.2.cloned.1.call-update) | async-done | bytes 2097168 | tf_op jit(solution)/shard_map/all_gather | solution.py:103
  514.2 3.0 copy.42
  (93 shorter events, 27.7 us)
Async XLA Ops:
  7.2 162.2 %all-reduce.19.cloned.1.call-start = ((), (), s32[]{:S(2)}) async-start(), calls=%async_computation.1 | async-start | bytes 262144 | tf_op jit(solution)/shard_map/psum | solution.py:85
  8.2 13.0 %collective-permute-start = (bf16[64,129]{1,0:T(8,128)(2,1)S(1)}, bf16[64,129]{1,0:T(8,128)(2,1)S(1)}, u32[]{:S(2)}, u32[]{:S(2)}) collective-permute-start(bf16[64,129]{1,0:T(8,128)(2,1)S(1)} %slice.174), channel_id=1, source_target_pairs={{0,1},{1,2},{2,3},{4,5},{5,6},{6,7},{8,9},{9,10},{10,11},{12,13},{... | collective-permute-start | bytes 49544 | tf_op jit(solution)/shard_map/ppermute | solution.py:20
  34.9 33.3 %copy-start = (bf16[16384,64]{0,1:T(8,128)(2,1)S(1)}, bf16[16384,64]{0,1:T(8,128)(2,1)}, u32[]{:S(2)}) copy-start(bf16[16384,64]{0,1:T(8,128)(2,1)} %param.15) | copy-start | bytes 6291460
  34.9 60.2 %collective-permute-start.1 = (bf16[64,129]{1,0:T(8,128)(2,1)S(1)}, bf16[64,129]{1,0:T(8,128)(2,1)S(1)}, u32[]{:S(2)}, u32[]{:S(2)}) collective-permute-start(bf16[64,129]{1,0:T(8,128)(2,1)S(1)} %slice.346), channel_id=1, source_target_pairs={{1,0},{2,1},{3,2},{5,4},{6,5},{7,6},{9,8},{10,9},{11,10},{13,12},{... | collective-permute-start | bytes 49544 | tf_op jit(solution)/shard_map/ppermute | solution.py:20
  68.3 109.6 %copy-start.3 = (f32[64,512]{1,0:T(8,128)S(1)}, f32[64,512]{1,0:T(8,128)}, u32[]{:S(2)}) copy-start(f32[64,512]{1,0:T(8,128)} %param.16) | copy-start | bytes 393220
  68.3 113.4 %copy-start.1 = (f32[4,64,64]{2,1,0:T(8,128)S(1)}, f32[4,64,64]{2,1,0:T(8,128)}, u32[]{:S(2)}) copy-start(f32[4,64,64]{2,1,0:T(8,128)} %param.17) | copy-start | bytes 196612
  94.9 193.0 %all-reduce.21.cloned.1.call-start = ((), (), s32[]{:S(2)}) async-start(), calls=%async_computation.2 | async-start | bytes 262144 | tf_op jit(solution)/shard_map/psum | solution.py:85
  178.9 2.6 collective-permute-start.2
  187.3 28.1 %collective-permute-start.3 = (bf16[64,129]{1,0:T(8,128)(2,1)S(1)}, bf16[64,129]{1,0:T(8,128)(2,1)S(1)}, u32[]{:S(2)}, u32[]{:S(2)}) collective-permute-start(bf16[64,129]{1,0:T(8,128)(2,1)S(1)} %slice.345), channel_id=1, source_target_pairs={{1,0},{2,1},{3,2},{5,4},{6,5},{7,6},{9,8},{10,9},{11,10},{13,12},{... | collective-permute-start | bytes 49544 | tf_op jit(solution)/shard_map/ppermute | solution.py:20
  215.2 191.3 %all-reduce.23.cloned.1.call-start = ((), (), s32[]{:S(2)}) async-start(), calls=%async_computation.3 | async-start | bytes 262144 | tf_op jit(solution)/shard_map/psum | solution.py:85
  297.5 2.6 collective-permute-start.4
  305.9 28.2 %collective-permute-start.5 = (bf16[64,129]{1,0:T(8,128)(2,1)S(1)}, bf16[64,129]{1,0:T(8,128)(2,1)S(1)}, u32[]{:S(2)}, u32[]{:S(2)}) collective-permute-start(bf16[64,129]{1,0:T(8,128)(2,1)S(1)} %slice.344), channel_id=1, source_target_pairs={{1,0},{2,1},{3,2},{5,4},{6,5},{7,6},{9,8},{10,9},{11,10},{13,12},{... | collective-permute-start | bytes 49544 | tf_op jit(solution)/shard_map/ppermute | solution.py:20
  333.9 155.4 %reduce-scatter.2.cloned.1.call-start = ((), (), s32[]{:S(2)}) async-start(), calls=%async_computation.4 | async-start | bytes 5242880 | tf_op jit(solution)/shard_map/reduce_scatter | solution.py:93
  416.3 28.8 %copy-start.2 = (f32[64,512]{1,0:T(8,128)}, f32[64,512]{1,0:T(8,128)S(1)}, u32[]{:S(2)}) copy-start(f32[64,512]{1,0:T(8,128)S(1)} %divide_subtract_fusion) | copy-start | bytes 393220
  445.1 69.1 %all-gather.2.cloned.1.call-start = ((), (), s32[]{:S(2)}) async-start(), calls=%async_computation.5 | async-start | bytes 2621440 | tf_op jit(solution)/shard_map/all_gather | solution.py:103
Sparse Core Ops, SparseCore 0:
  95.1 74.2 all-reduce.18
  215.4 72.5 all-reduce.20
  334.0 72.5 all-reduce.22
  445.2 44.0 reduce-scatter.1
  491.6 22.5 all-gather.1
where the time goes:
time: 529 us; the launch traced here: 524 us
  waiting for transfers between devices  286 us (54%)
  matrix products  124 us (23%)
  local copies, waits for them, and re-layouts  50.2 us (9%)
  between operations  19.3 us (4%)
  blocking collectives  19 us (4%)
  other arithmetic  14.6 us (3%)
  starting transfers between devices  11 us (2%)
    psum x3, waiting for transfers between devices, shards(): data_grad = lax.psum(local_grad, 'series')  218 us
    dot_general x3, matrix products, shards(): lax.dot_general(factors, resid, (((0,), (0,)), ((), ())), preferred_eleme...  79.6 us
    reduce_scatter x1, waiting for transfers between devices, shards(): lax.psum_scatter(lax.dot_general(resid, basis_b, (((1,), (1,)), ((), ()))...  44.1 us
    mul x1, local copies, waits for them, and re-layouts, resid_block(): (pred - observed.astype(jnp.float32)).reshape(factors.shape[0], -1, BLK)  31.4 us
    dot_general x1, matrix products, shards(): lax.dot_general(resid, basis_b, (((1,), (1,)), ((), ())), preferred_eleme...  28.8 us
    all_gather x1, waiting for transfers between devices, shards(): new_factors = lax.all_gather(updated, 'tm', axis=0, tiled=True)  22.7 us
    psum x3, blocking collectives, shards(): total = lax.psum(jnp.sum(grad * grad), 'tm')  19 us
    dot_general x24, matrix products, mix(): return jnp.dot(weight, field, precision=lax.Precision.HIGHEST)  15.4 us
  transfers between devices with their start and end apart: 11, of which 7 were waited for; matrix products, arithmetic and copies ran while one was open for 23% of the time, Pallas kernels for 0%

commit v1 on v0

v1 whole, which is shorter than its diff:
```python
import math

import jax
import jax.numpy as jnp
from jax import lax
from jax.experimental import pallas as pl
from jax.experimental.pallas import tpu as pltpu
from jax.sharding import PartitionSpec as P

BLK = 128
LANES = 128
ITERS = 3
F32 = jnp.float32
BF16 = jnp.bfloat16
VMEM_BYTES = 48 << 20


def nt_dot(a, b):
    return lax.dot_general(a, b, (((1,), (1,)), ((), ())), preferred_element_type=F32)


def tn_dot(a, b):
    return lax.dot_general(a, b, (((0,), (0,)), ((), ())), preferred_element_type=F32)


def gram_kernel(obs_ref, fac_ref, flg_ref, out_ref):
    rank = fac_ref.shape[0]
    blocks = flg_ref.shape[0]
    fac = fac_ref[...]
    flg = flg_ref[...].astype(F32).astype(BF16)
    masked = jnp.concatenate([fac * flg[b : b + 1, :] for b in range(blocks)], axis=0)
    parts = []
    for b in range(0, blocks, 2):
        both = jnp.dot(
            masked[b * rank : (b + 2) * rank],
            obs_ref[:, b * BLK : (b + 2) * BLK],
            preferred_element_type=F32,
        )
        parts += [both[:rank, :BLK], both[rank:, BLK:]]
    new = jnp.concatenate(parts + [nt_dot(fac, masked)], axis=1)

    @pl.when(pl.program_id(0) == 0)
    def _():
        out_ref[...] = new

    @pl.when(pl.program_id(0) > 0)
    def _():
        out_ref[...] += new


def gram(observed, fac_t, flg_t, rows):
    series, cols = observed.shape
    rank, blocks = fac_t.shape[0], flg_t.shape[0]
    width = cols + blocks * rank
    return pl.pallas_call(
        gram_kernel,
        grid=(series // rows,),
        in_specs=[
            pl.BlockSpec((rows, cols), lambda i: (i, 0)),
            pl.BlockSpec((rank, rows), lambda i: (0, i)),
            pl.BlockSpec((blocks, rows), lambda i: (0, i)),
        ],
        out_specs=pl.BlockSpec((rank, width), lambda i: (0, 0)),
        out_shape=jax.ShapeDtypeStruct((rank, width), F32),
        compiler_params=pltpu.CompilerParams(vmem_limit_bytes=VMEM_BYTES),
        name="gram",
    )(observed, fac_t, flg_t)


def split(x):
    high = x.astype(BF16)
    return high, (x - high.astype(F32)).astype(BF16)


def later(x, steps, fill):
    lane = lax.broadcasted_iota(jnp.int32, (x.shape[0], LANES), 1)
    before = jnp.broadcast_to(fill, (x.shape[0], LANES))
    out = []
    for j in range(0, x.shape[1], LANES):
        rolled = pltpu.roll(x[:, j : j + LANES], steps, 1)
        out.append(jnp.where(lane < steps, before, rolled))
        before = rolled
    return jnp.concatenate(out, axis=1)


def earlier(x, steps):
    lane = lax.broadcasted_iota(jnp.int32, (x.shape[0], LANES), 1)
    rolled = [
        pltpu.roll(x[:, j : j + LANES], LANES - steps, 1) for j in range(0, x.shape[1], LANES)
    ]
    rolled.append(jnp.zeros((x.shape[0], LANES), F32))
    out = [jnp.where(lane < LANES - steps, a, b) for a, b in zip(rolled[:-1], rolled[1:])]
    return jnp.concatenate(out, axis=1)


def taps(first, second):
    fh, fl = split(first)
    sh, sl = split(second)
    zero = jnp.zeros_like(fh)
    top = jnp.concatenate([fh, sh, fh, sh], axis=1)
    bottom = jnp.concatenate([fl, sl, zero, zero], axis=1)
    return jnp.concatenate([top, bottom], axis=0)


def pair_dot(weights, a, b):
    ah, al = split(a)
    bh, bl = split(b)
    both = jnp.dot(
        weights, jnp.concatenate([ah, bh, al, bl], axis=0), preferred_element_type=F32
    )
    rank = a.shape[0]
    return both[:rank] + both[rank:]


def steps_kernel(
    dil_ref, place_ref, sums_ref, basis_ref, w_ref, bias_ref, basis_out, basis_b_out, x_ref,
    *, data_scale, entries
):
    rank, total = basis_ref.shape
    cols = basis_out.shape[1]
    slabs = total // cols
    d0, d1 = dil_ref[0], dil_ref[1]
    b0, b1 = bias_ref[:, 0:1], bias_ref[:, 1:2]
    w = [w_ref[i] for i in range(4)]
    layer1 = taps(w[0], w[1])
    layer2 = taps(w[2], w[3])
    back2 = taps(w[2].T, w[3].T)
    back1 = taps(w[0].T, w[1].T)
    x_ref[...] = basis_ref[...]

    def body(i, carry):
        x = x_ref[...]
        z = later(x, 1, 0.0)
        pre = pair_dot(layer1, later(z, d0, 0.0), z) + b0
        hidden = jnp.maximum(pre, 0.0)
        shown = later(hidden, d1, jnp.maximum(b0, 0.0))
        error = 0.1 * (x - z - pair_dot(layer2, shown, hidden) - b1)
        pull = -pair_dot(back2, earlier(error, d1), error)
        pull = jnp.where(pre > 0.0, pull, 0.0)
        reg = error + earlier(pair_dot(back1, earlier(pull, d0), pull) - error, 1)
        xb = x.astype(BF16)
        data = []
        for s in range(slabs):
            for b in range(0, cols // BLK, 2):
                at = s * cols + b * BLK
                pair = sums_ref[s, :, cols + b * rank : cols + (b + 2) * rank]
                high, rest = split(pair)
                mid = rest
                low = (pair - high.astype(F32) - mid.astype(F32)).astype(BF16)
                zero = jnp.zeros((rank, BLK), BF16)
                right = jnp.concatenate(
                    [
                        jnp.concatenate([xb[:, at : at + BLK], zero], axis=1),
                        jnp.concatenate([zero, xb[:, at + BLK : at + 2 * BLK]], axis=1),
                    ],
                    axis=0,
                )
                got = jnp.dot(
                    jnp.concatenate([high, mid, low], axis=0), right, preferred_element_type=F32
                )
                got = got[:rank] + (got[rank : 2 * rank] + got[2 * rank :])
                data.append(got - sums_ref[s, :, b * BLK : (b + 2) * BLK])
        grad = jnp.concatenate(data, axis=1) * data_scale + reg
        square = jnp.sum(grad * grad)
        x_ref[...] = x - grad * (0.1 * lax.rsqrt(jnp.full((1, 1), square) / entries + 1e-06))
        return carry

    lax.fori_loop(0, ITERS, body, 0)
    start = pl.multiple_of(place_ref[0] * cols, LANES)
    mine = x_ref[:, pl.ds(start, cols)]
    basis_out[...] = mine
    basis_b_out[...] = mine.astype(BF16)


def basis_steps(dilations, place, sums, basis_all, weights, bias_t, cols, data_scale):
    rank, total = basis_all.shape
    smem = pl.BlockSpec(memory_space=pltpu.SMEM)
    vmem = pl.BlockSpec(memory_space=pltpu.VMEM)
    return pl.pallas_call(
        lambda *refs: steps_kernel(*refs, data_scale=data_scale, entries=float(rank * total)),
        in_specs=[smem, smem, vmem, vmem, vmem, vmem],
        out_specs=[vmem, vmem],
        out_shape=[
            jax.ShapeDtypeStruct((rank, cols), F32),
            jax.ShapeDtypeStruct((rank, cols), BF16),
        ],
        scratch_shapes=[pltpu.VMEM((rank, total), F32)],
        compiler_params=pltpu.CompilerParams(vmem_limit_bytes=VMEM_BYTES),
        name="basis_steps",
    )(dilations, place, sums, basis_all, weights, bias_t)


def pull_kernel(obs_ref, fac_ref, flg_ref, basis_ref, out_ref):
    basis = basis_ref[...]
    flg = flg_ref[...].astype(F32)
    pred = tn_dot(fac_ref[...], basis)
    resid = (pred - obs_ref[...].astype(F32)).astype(BF16)
    total = None
    for b in range(flg.shape[0]):
        cut = slice(b * BLK, (b + 1) * BLK)
        term = nt_dot(basis[:, cut], resid[:, cut]) * flg[b : b + 1, :]
        total = term if total is None else total + term
    out_ref[...] = total


def factor_pull(observed, fac_t, flg_t, basis_b, first, series, rows):
    cols = observed.shape[1]
    rank, blocks = fac_t.shape[0], flg_t.shape[0]
    skip = first // rows
    return pl.pallas_call(
        pull_kernel,
        grid=(series // rows,),
        in_specs=[
            pl.BlockSpec((rows, cols), lambda i: (i + skip, 0)),
            pl.BlockSpec((rank, rows), lambda i: (0, i + skip)),
            pl.BlockSpec((blocks, rows), lambda i: (0, i + skip)),
            pl.BlockSpec((rank, cols), lambda i: (0, 0)),
        ],
        out_specs=pl.BlockSpec((rank, rows), lambda i: (0, i)),
        out_shape=jax.ShapeDtypeStruct((rank, series), F32),
        compiler_params=pltpu.CompilerParams(vmem_limit_bytes=VMEM_BYTES),
        name="factor_pull",
    )(observed, fac_t, flg_t, basis_b)


def swap(x, axis, bit):
    count = lax.axis_size(axis)
    return lax.ppermute(x, axis, [(i, i ^ bit) for i in range(count)])


def sum_over(x, axis):
    count = lax.axis_size(axis)
    if count & (count - 1):
        return lax.psum(x, axis)
    bit = 1
    while bit < count:
        x = x + swap(x, axis, bit)
        bit *= 2
    return x


def gather_over(x, axis):
    return lax.all_gather(x, axis, axis=0, tiled=False)


def shards(observed, flags, factors, basis, tcn_weights, tcn_bias, dilations):
    series, cols = observed.shape
    rank = basis.shape[0]
    time_count = lax.axis_size("tm")
    place = lax.axis_index("tm")
    fac_t, flg_t = factors.T, flags.T
    data_scale = 1.0 / math.sqrt(series * lax.axis_size("series"))
    coef = 0.1 / math.sqrt(cols * time_count)

    basis_all = gather_over(basis, "tm").transpose(1, 0, 2).reshape(rank, cols * time_count)
    sums = gather_over(sum_over(gram(observed, fac_t, flg_t, 2048), "series"), "tm")
    new_basis, basis_b = basis_steps(
        dilations, place.astype(jnp.int32).reshape(1), sums, basis_all,
        tcn_weights, tcn_bias.T, cols, data_scale,
    )

    chunks = 4
    width = series // chunks
    half = width // 2
    core = place % 2
    done = []
    for c in range(chunks):
        first = c * width
        pull = factor_pull(observed, fac_t, flg_t, basis_b, first, width, 2048) * coef
        low, high = pull[:, :half], pull[:, half:]
        own = jnp.where(core == 0, low, high)
        other = jnp.where(core == 0, high, low)
        own = (own + swap(other, "tm", 1)).astype(jnp.float16)
        both = own.astype(F32) + swap(own, "tm", 2).astype(F32)
        mine = lax.dynamic_slice_in_dim(fac_t, first + core * half, half, 1)
        new = (mine.astype(F32) - both).astype(BF16)
        theirs = swap(new, "tm", 1)
        done.append(jnp.where(core == 0, new, theirs))
        done.append(jnp.where(core == 0, theirs, new))
    return new_basis, jnp.concatenate(done, axis=1).T


def solution(mesh):
    return jax.shard_map(
        shards,
        mesh=mesh,
        in_specs=(
            P("series", "tm"),
            P("series", "tm"),
            P("series", None),
            P(None, "tm"),
            P(),
            P(),
            P(),
        ),
        out_specs=(P(None, "tm"), P("series", None)),
        check_vma=False,
    )
```

time: 529 us -> 106 us (0.20)
  waiting for transfers between devices: 286 us -> 31.6 us
  matrix products: 124 us -> 0 us
  local copies, waits for them, and re-layouts: 50.2 us -> 4.48 us
  Pallas kernels: 0 us -> 35.8 us
  between operations: 19.3 us -> 0.9 us
  other arithmetic: 14.6 us -> 3.21 us
    psum x3 -> x0, waiting for transfers between devices: 218 us -> none  [shards(): data_grad = lax.psum(local_grad, 'series')]
    dot_general x28 -> x0, matrix products: 124 us -> none  [the longest x3 79.6 us: shards(): lax.dot_general(factors, resid, (((0,), (0,)), ((), ())), preferred_eleme...]
    reduce_scatter x1 -> x0, waiting for transfers between devices: 44.1 us -> none  [shards(): lax.psum_scatter(lax.dot_general(resid, basis_b, (((1,), (1,)), ((), ()))...]
    pallas_call x0 -> x6, Pallas kernels: none -> 35.8 us  [the longest x4 17.2 us: factor_pull(): pl.pallas_call(pull_kernel, grid=(series // rows,), in_specs=[pl.BlockSpe...]
    mul x1 -> x0, local copies, waits for them, and re-layouts: 31.4 us -> none  [resid_block(): (pred - observed.astype(jnp.float32)).reshape(factors.shape[0], -1, BLK)]
    ppermute x6 -> x15, waiting for transfers between devices: 1.69 us -> 31.6 us  [swap(): return lax.ppermute(x, axis, [(i, i ^ bit) for i in range(count)])]
    all_gather x1 -> x0, waiting for transfers between devices: 22.7 us -> none  [shards(): new_factors = lax.all_gather(updated, 'tm', axis=0, tiled=True)]
    psum x3 -> x0, blocking collectives: 19 us -> none  [shards(): total = lax.psum(jnp.sum(grad * grad), 'tm')]
  transfers between devices with their start and end apart: 11 -> 15, of which waited for: 7 -> 11; matrix products, arithmetic and copies ran while one was open for 23% -> 2% of each run, Pallas kernels for 0% -> 0%
where the time goes in v1:
time: 106 us
  Pallas kernels  35.8 us (34%)
  waiting for transfers between devices  31.6 us (30%)
  blocking collectives  16 us (15%)
  starting transfers between devices  14.1 us (13%)
  local copies, waits for them, and re-layouts  4.48 us (4%)
  other arithmetic  3.21 us (3%)
    ppermute x15, waiting for transfers between devices, swap(): return lax.ppermute(x, axis, [(i, i ^ bit) for i in range(count)])  31.6 us
    pallas_call x4, Pallas kernels, factor_pull(): pl.pallas_call(pull_kernel, grid=(series // rows,), in_specs=[pl.BlockSpe...  17.2 us
    all_gather x2, blocking collectives, gather_over(): return lax.all_gather(x, axis, axis=0, tiled=False)  16 us
    ppermute x15, starting transfers between devices, swap(): return lax.ppermute(x, axis, [(i, i ^ bit) for i in range(count)])  14.1 us
    pallas_call x1, Pallas kernels, gram(): pl.pallas_call(gram_kernel, grid=(series // rows,), in_specs=[pl.BlockSpe...  10.8 us
    pallas_call x1, Pallas kernels, basis_steps(): pl.pallas_call(lambda *refs: steps_kernel(*refs, data_scale=data_scale, e...  7.81 us
    unnamed x20, local copies, waits for them, and re-layouts  4.14 us
  transfers between devices with their start and end apart: 15, of which 11 were waited for; matrix products, arithmetic and copies ran while one was open for 2% of the time, Pallas kernels for 0%

profile of v1, /device:TPU:0, one launch (start us, length us, event | category | flops | bytes accessed | tf_op | source)
XLA Modules:
  0.0 106.1 jit_solution(9391021728550163752)
XLA Ops:
  0.6 1.6 %copy-done = bf16[16384,64]{0,1:T(8,128)(2,1)S(1)} copy-done((bf16[16384,64]{0,1:T(8,128)(2,1)S(1)}, bf16[16384,64]{0,1:T(8,128)(2,1)}, u32[]{:S(2)}) %copy-start) | copy-done | bytes 2097176
  2.2 0.9 copy-done.2
  3.2 10.8 %gram.1 = f32[64,768]{1,0:T(8,128)S(1)} custom-call(bf16[16384,512]{1,0:T(8,128)(2,1)} %obs_ref.9, bf16[64,16384]{1,0:T(8,128)(2,1)S(1)} %bitcast.26, s32[4,16384]{1,0:T(4,128)S(1)} %bitcast.31), custom_call_target="tpu_custom_call" | custom-call | tf_op jit(solution)/shard_map/gram/pallas_call | solution.py:55
  14.0 3.0 %collective-permute-start = (f32[64,768]{1,0:T(8,128)S(1)}, f32[64,768]{1,0:T(8,128)S(1)}, u32[]{:S(2)}, u32[]{:S(2)}) collective-permute-start(f32[64,768]{1,0:T(8,128)S(1)} %gram.1), channel_id=1, source_target_pairs={{0,4},{4,0},{8,12},{12,8},{16,20},{20,16},{24,28},{28,24},{1,5},{5... | collective-permute-start | bytes 589832 | tf_op jit(solution)/shard_map/ppermute | solution.py:228
  17.0 4.9 %collective-permute-done = f32[64,768]{1,0:T(8,128)S(1)} collective-permute-done((f32[64,768]{1,0:T(8,128)S(1)}, f32[64,768]{1,0:T(8,128)S(1)}, u32[]{:S(2)}, u32[]{:S(2)}) %collective-permute-start) | collective-permute-done | bytes 196640 | tf_op jit(solution)/shard_map/ppermute | solution.py:228
  21.9 1.9 %collective-permute-start.1 = (f32[64,768]{1,0:T(8,128)S(1)}, f32[64,768]{1,0:T(8,128)S(1)}, u32[]{:S(2)}, u32[]{:S(2)}) collective-permute-start(f32[64,768]{1,0:T(8,128)S(1)} %add.55), channel_id=1, source_target_pairs={{0,8},{4,12},{8,0},{12,4},{16,24},{20,28},{24,16},{28,20},{1,9},{5... | collective-permute-start | bytes 589832 | tf_op jit(solution)/shard_map/ppermute | solution.py:228
  23.8 4.3 %collective-permute-done.1 = f32[64,768]{1,0:T(8,128)S(1)} collective-permute-done((f32[64,768]{1,0:T(8,128)S(1)}, f32[64,768]{1,0:T(8,128)S(1)}, u32[]{:S(2)}, u32[]{:S(2)}) %collective-permute-start.1) | collective-permute-done | bytes 196640 | tf_op jit(solution)/shard_map/ppermute | solution.py:228
  28.1 2.5 %collective-permute-start.2 = (f32[64,768]{1,0:T(8,128)S(1)}, f32[64,768]{1,0:T(8,128)S(1)}, u32[]{:S(2)}, u32[]{:S(2)}) collective-permute-start(f32[64,768]{1,0:T(8,128)S(1)} %add.56), channel_id=1, source_target_pairs={{0,16},{4,20},{8,24},{12,28},{16,0},{20,4},{24,8},{28,12},{1,17},{... | collective-permute-start | bytes 589832 | tf_op jit(solution)/shard_map/ppermute | solution.py:228
  30.6 7.2 %all-gather.1 = f32[256,512]{1,0:T(8,128)S(1)} all-gather(f32[64,512]{1,0:T(8,128)S(1)} %copy-done.6), channel_id=3, replica_groups=mesh['series'=8,'tm'=4] {'tm'}, dimensions={0}, use_global_device_ids=true | all-gather | bytes 655360 | tf_op jit(solution)/shard_map/all_gather | solution.py:243
  37.8 0.3 copy.9
  38.5 8.9 %all-gather = f32[256,768]{1,0:T(8,128)S(1)} all-gather(f32[64,768]{1,0:T(8,128)S(1)} %add.57), channel_id=2, replica_groups=mesh['series'=8,'tm'=4] {'tm'}, dimensions={0}, use_global_device_ids=true | all-gather | bytes 983040 | tf_op jit(solution)/shard_map/all_gather | solution.py:243
  47.4 7.8 %basis_steps.1 = (f32[64,512]{1,0:T(8,128)}, bf16[64,512]{1,0:T(8,128)(2,1)S(1)}) custom-call(s32[2]{0:T(128)S(1)} %copy-done.5, s32[1]{0:T(128)} %bitcast.refs_1_, f32[4,64,768]{2,1,0:T(8,128)S(1)} %bitcast.36, f32[64,2048]{1,0:T(8,128)S(1)} %bitcast.37, f32[4,64,64]{2,1,0:T(8,128)S(1)} %copy-done.4, f32[64,2]{1,0:T(8,128)S(1)} %bitcast.38), custom_call_target="tpu_custom_call" | custom-call | tf_op jit(solution)/shard_map/basis_steps/pallas_call | solution.py:179
  55.2 4.3 %factor_pull.7 = f32[64,4096]{1,0:T(8,128)S(1)} custom-call(bf16[16384,512]{1,0:T(8,128)(2,1)} %obs_ref.9, bf16[64,16384]{1,0:T(8,128)(2,1)S(1)} %bitcast.27, s32[4,16384]{1,0:T(4,128)S(1)} %bitcast.32, bf16[64,512]{1,0:T(8,128)(2,1)S(1)} %get-tuple-element.5.basis_ref), custom_call_target="tpu_custom_call" | custom-call | tf_op jit(solution)/shard_map/factor_pull/pallas_call | solution.py:210
  59.5 4.3 %factor_pull.5 = f32[64,4096]{1,0:T(8,128)S(1)} custom-call(bf16[16384,512]{1,0:T(8,128)(2,1)} %obs_ref.9, bf16[64,16384]{1,0:T(8,128)(2,1)S(1)} %bitcast.28, s32[4,16384]{1,0:T(4,128)S(1)} %bitcast.33, bf16[64,512]{1,0:T(8,128)(2,1)S(1)} %get-tuple-element.5.basis_ref), custom_call_target="tpu_custom_call" | custom-call | tf_op jit(solution)/shard_map/factor_pull/pallas_call | solution.py:210
  63.8 4.3 %factor_pull.4 = f32[64,4096]{1,0:T(8,128)S(1)} custom-call(bf16[16384,512]{1,0:T(8,128)(2,1)} %obs_ref.9, bf16[64,16384]{1,0:T(8,128)(2,1)S(1)} %bitcast.29, s32[4,16384]{1,0:T(4,128)S(1)} %bitcast.34, bf16[64,512]{1,0:T(8,128)(2,1)S(1)} %get-tuple-element.5.basis_ref), custom_call_target="tpu_custom_call" | custom-call | tf_op jit(solution)/shard_map/factor_pull/pallas_call | solution.py:210
  68.1 4.3 %factor_pull.6 = f32[64,4096]{1,0:T(8,128)S(1)} custom-call(bf16[16384,512]{1,0:T(8,128)(2,1)} %obs_ref.9, bf16[64,16384]{1,0:T(8,128)(2,1)S(1)} %bitcast.30, s32[4,16384]{1,0:T(4,128)S(1)} %bitcast.35, bf16[64,512]{1,0:T(8,128)(2,1)S(1)} %get-tuple-element.5.basis_ref), custom_call_target="tpu_custom_call" | custom-call | tf_op jit(solution)/shard_map/factor_pull/pallas_call | solution.py:210
  72.6 0.4 collective-permute-start.12
  73.5 0.4 collective-permute-start.3
  74.6 0.9 collective-permute-start.13
  75.6 1.3 %collective-permute-start.7 = (f16[64,2048]{1,0:T(8,128)(2,1)S(1)}, f16[64,2048]{1,0:T(8,128)(2,1)}, u32[]{:S(2)}, u32[]{:S(2)}) collective-permute-start(f16[64,2048]{1,0:T(8,128)(2,1)S(1)} %add_convert_fusion.2), channel_id=1, source_target_pairs={{0,2},{1,3},{2,0},{3,1},{4,6},{5,7},{6,4},{7,5},{8,10},{9,11},{10,... | collective-permute-start | bytes 786440 | tf_op jit(solution)/shard_map/ppermute | solution.py:228
  77.0 0.9 collective-permute-start.4
  78.0 1.3 %collective-permute-start.10 = (f16[64,2048]{1,0:T(8,128)(2,1)S(1)}, f16[64,2048]{1,0:T(8,128)(2,1)}, u32[]{:S(2)}, u32[]{:S(2)}) collective-permute-start(f16[64,2048]{1,0:T(8,128)(2,1)S(1)} %add_convert_fusion.1), channel_id=1, source_target_pairs={{0,2},{1,3},{2,0},{3,1},{4,6},{5,7},{6,4},{7,5},{8,10},{9,11},{10,... | collective-permute-start | bytes 786440 | tf_op jit(solution)/shard_map/ppermute | solution.py:228
  79.2 4.6 %collective-permute-done.13 = f16[64,2048]{1,0:T(8,128)(2,1)S(1)} collective-permute-done((f16[64,2048]{1,0:T(8,128)(2,1)S(1)}, f16[64,2048]{1,0:T(8,128)(2,1)S(1)}, u32[]{:S(2)}, u32[]{:S(2)}) %collective-permute-start.13) | collective-permute-done | bytes 262176 | tf_op jit(solution)/shard_map/ppermute | solution.py:228
  83.8 5.7 %collective-permute-done.7 = f16[64,2048]{1,0:T(8,128)(2,1)} collective-permute-done((f16[64,2048]{1,0:T(8,128)(2,1)S(1)}, f16[64,2048]{1,0:T(8,128)(2,1)}, u32[]{:S(2)}, u32[]{:S(2)}) %collective-permute-start.7) | collective-permute-done | bytes 262176 | tf_op jit(solution)/shard_map/ppermute | solution.py:228
  89.6 5.6 %collective-permute-done.4 = f16[64,2048]{1,0:T(8,128)(2,1)} collective-permute-done((f16[64,2048]{1,0:T(8,128)(2,1)S(1)}, f16[64,2048]{1,0:T(8,128)(2,1)}, u32[]{:S(2)}, u32[]{:S(2)}) %collective-permute-start.4) | collective-permute-done | bytes 262176 | tf_op jit(solution)/shard_map/ppermute | solution.py:228
  95.2 5.1 %collective-permute-done.10 = f16[64,2048]{1,0:T(8,128)(2,1)} collective-permute-done((f16[64,2048]{1,0:T(8,128)(2,1)S(1)}, f16[64,2048]{1,0:T(8,128)(2,1)}, u32[]{:S(2)}, u32[]{:S(2)}) %collective-permute-start.10) | collective-permute-done | bytes 262176 | tf_op jit(solution)/shard_map/ppermute | solution.py:228
  100.2 1.7 %fusion = (bf16[64,2048]{1,0:T(8,128)(2,1)S(1)}, bf16[64,2048]{1,0:T(8,128)(2,1)S(1)}, bf16[64,2048]{1,0:T(8,128)(2,1)S(1)}, bf16[64,2048]{1,0:T(8,128)(2,1)S(1)}) fusion(f16[64,2048]{1,0:T(8,128)(2,1)S(1)} %collective-permute-done.13, f16[64,2048]{1,0:T(8,128)(2,1)S(1)} %add_convert_fusion, bf16[16384,64]{0,1:T(8,128)(2,1)S(1)} %copy-done.1, ...), kind=kLoop, calls=%fused_computation.1 | loop fusion | flops 3145728 | bytes 4194320 | tf_op jit(solution)/shard_map/convert_element_type | solution.py:276
  102.0 0.5 collective-permute-start.8
  102.6 0.4 collective-permute-start.14
  103.0 0.5 collective-permute-done.5
  103.7 0.2 collective-permute-done.8
  104.8 1.3 %copy-done.7 = bf16[64,16384]{1,0:T(8,128)(2,1)} copy-done((bf16[64,16384]{1,0:T(8,128)(2,1)}, bf16[64,16384]{1,0:T(8,128)(2,1)S(1)}, u32[]{:S(2)}) %copy-start.7) | copy-done | bytes 2097176
  (51 shorter events, 3.1 us)
Async XLA Ops:
  0.6 1.6 %copy-start = (bf16[16384,64]{0,1:T(8,128)(2,1)S(1)}, bf16[16384,64]{0,1:T(8,128)(2,1)}, u32[]{:S(2)}) copy-start(bf16[16384,64]{0,1:T(8,128)(2,1)} %param.9) | copy-start | bytes 6291460
  2.2 0.9 copy-start.2
  3.2 27.5 %copy-start.6 = (f32[64,512]{1,0:T(8,128)S(1)}, f32[64,512]{1,0:T(8,128)}, u32[]{:S(2)}) copy-start(f32[64,512]{1,0:T(8,128)} %param.10) | copy-start | bytes 393220
  13.9 24.4 %copy-start.8 = (f32[2,64]{1,0:T(2,128)S(1)}, f32[2,64]{1,0:T(2,128)}, u32[]{:S(2)}) copy-start(f32[2,64]{1,0:T(2,128)} %param.12) | copy-start | bytes 1540
  14.0 7.9 %collective-permute-start = (f32[64,768]{1,0:T(8,128)S(1)}, f32[64,768]{1,0:T(8,128)S(1)}, u32[]{:S(2)}, u32[]{:S(2)}) collective-permute-start(f32[64,768]{1,0:T(8,128)S(1)} %gram.1), channel_id=1, source_target_pairs={{0,4},{4,0},{8,12},{12,8},{16,20},{20,16},{24,28},{28,24},{1,5},{5... | collective-permute-start | bytes 589832 | tf_op jit(solution)/shard_map/ppermute | solution.py:228
  21.9 6.1 %collective-permute-start.1 = (f32[64,768]{1,0:T(8,128)S(1)}, f32[64,768]{1,0:T(8,128)S(1)}, u32[]{:S(2)}, u32[]{:S(2)}) collective-permute-start(f32[64,768]{1,0:T(8,128)S(1)} %add.55), channel_id=1, source_target_pairs={{0,8},{4,12},{8,0},{12,4},{16,24},{20,28},{24,16},{28,20},{1,9},{5... | collective-permute-start | bytes 589832 | tf_op jit(solution)/shard_map/ppermute | solution.py:228
  28.1 19.3 %copy-start.4 = (f32[4,64,64]{2,1,0:T(8,128)S(1)}, f32[4,64,64]{2,1,0:T(8,128)}, u32[]{:S(2)}) copy-start(f32[4,64,64]{2,1,0:T(8,128)} %refs_4_.1) | copy-start | bytes 196612
  28.1 19.3 %copy-start.5 = (s32[2]{0:T(128)S(1)}, s32[2]{0:T(128)}, u32[]{:S(2)}) copy-start(s32[2]{0:T(128)} %refs_0_.1) | copy-start | bytes 28
  28.1 10.4 %collective-permute-start.2 = (f32[64,768]{1,0:T(8,128)S(1)}, f32[64,768]{1,0:T(8,128)S(1)}, u32[]{:S(2)}, u32[]{:S(2)}) collective-permute-start(f32[64,768]{1,0:T(8,128)S(1)} %add.56), channel_id=1, source_target_pairs={{0,16},{4,20},{8,24},{12,28},{16,0},{20,4},{24,8},{28,12},{1,17},{... | collective-permute-start | bytes 589832 | tf_op jit(solution)/shard_map/ppermute | solution.py:228
  38.2 17.0 %copy-start.1 = (bf16[16384,64]{0,1:T(8,128)(2,1)S(1)}, bf16[16384,64]{0,1:T(8,128)(2,1)}, u32[]{:S(2)}) copy-start(bf16[16384,64]{0,1:T(8,128)(2,1)} %param.9) | copy-start | bytes 6291460
  38.2 17.0 %copy-start.3 = (s32[16384,4]{0,1:T(4,128)S(1)}, s32[16384,4]{0,1:T(4,128)}, u32[]{:S(2)}) copy-start(s32[16384,4]{0,1:T(4,128)} %param.8) | copy-start | bytes 786436
  72.6 2.0 %collective-permute-start.12 = (f32[64,2048]{1,0:T(8,128)S(1)}, f32[64,2048]{1,0:T(8,128)S(1)}, u32[]{:S(2)}, u32[]{:S(2)}) collective-permute-start(f32[64,2048]{1,0:T(8,128)S(1)} %slice_select_fusion), channel_id=1, source_target_pairs={{0,1},{1,0},{2,3},{3,2},{4,5},{5,4},{6,7},{7,6},{8,9},{9,8},{10,11... | collective-permute-start | bytes 1572872 | tf_op jit(solution)/shard_map/ppermute | solution.py:228
  73.2 2.4 %collective-permute-start.6 = (f32[64,2048]{1,0:T(8,128)S(1)}, f32[64,2048]{1,0:T(8,128)S(1)}, u32[]{:S(2)}, u32[]{:S(2)}) collective-permute-start(f32[64,2048]{1,0:T(8,128)S(1)} %slice_select_fusion.2), channel_id=1, source_target_pairs={{0,1},{1,0},{2,3},{3,2},{4,5},{5,4},{6,7},{7,6},{8,9},{9,8},{10,11... | collective-permute-start | bytes 1572872 | tf_op jit(solution)/shard_map/ppermute | solution.py:228
  73.5 3.3 %collective-permute-start.3 = (f32[64,2048]{1,0:T(8,128)S(1)}, f32[64,2048]{1,0:T(8,128)S(1)}, u32[]{:S(2)}, u32[]{:S(2)}) collective-permute-start(f32[64,2048]{1,0:T(8,128)S(1)} %slice_select_fusion.3), channel_id=1, source_target_pairs={{0,1},{1,0},{2,3},{3,2},{4,5},{5,4},{6,7},{7,6},{8,9},{9,8},{10,11... | collective-permute-start | bytes 1572872 | tf_op jit(solution)/shard_map/ppermute | solution.py:228
  74.1 3.8 %collective-permute-start.9 = (f32[64,2048]{1,0:T(8,128)S(1)}, f32[64,2048]{1,0:T(8,128)S(1)}, u32[]{:S(2)}, u32[]{:S(2)}) collective-permute-start(f32[64,2048]{1,0:T(8,128)S(1)} %slice_select_fusion.1), channel_id=1, source_target_pairs={{0,1},{1,0},{2,3},{3,2},{4,5},{5,4},{6,7},{7,6},{8,9},{9,8},{10,11... | collective-permute-start | bytes 1572872 | tf_op jit(solution)/shard_map/ppermute | solution.py:228
  74.6 9.2 %collective-permute-start.13 = (f16[64,2048]{1,0:T(8,128)(2,1)S(1)}, f16[64,2048]{1,0:T(8,128)(2,1)S(1)}, u32[]{:S(2)}, u32[]{:S(2)}) collective-permute-start(f16[64,2048]{1,0:T(8,128)(2,1)S(1)} %add_convert_fusion), channel_id=1, source_target_pairs={{0,2},{1,3},{2,0},{3,1},{4,6},{5,7},{6,4},{7,5},{8,10},{9,11},{10,... | collective-permute-start | bytes 786440 | tf_op jit(solution)/shard_map/ppermute | solution.py:228
  75.6 13.9 %collective-permute-start.7 = (f16[64,2048]{1,0:T(8,128)(2,1)S(1)}, f16[64,2048]{1,0:T(8,128)(2,1)}, u32[]{:S(2)}, u32[]{:S(2)}) collective-permute-start(f16[64,2048]{1,0:T(8,128)(2,1)S(1)} %add_convert_fusion.2), channel_id=1, source_target_pairs={{0,2},{1,3},{2,0},{3,1},{4,6},{5,7},{6,4},{7,5},{8,10},{9,11},{10,... | collective-permute-start | bytes 786440 | tf_op jit(solution)/shard_map/ppermute | solution.py:228
  77.0 18.2 %collective-permute-start.4 = (f16[64,2048]{1,0:T(8,128)(2,1)S(1)}, f16[64,2048]{1,0:T(8,128)(2,1)}, u32[]{:S(2)}, u32[]{:S(2)}) collective-permute-start(f16[64,2048]{1,0:T(8,128)(2,1)S(1)} %add_convert_fusion.3), channel_id=1, source_target_pairs={{0,2},{1,3},{2,0},{3,1},{4,6},{5,7},{6,4},{7,5},{8,10},{9,11},{10,... | collective-permute-start | bytes 786440 | tf_op jit(solution)/shard_map/ppermute | solution.py:228
  78.0 22.3 %collective-permute-start.10 = (f16[64,2048]{1,0:T(8,128)(2,1)S(1)}, f16[64,2048]{1,0:T(8,128)(2,1)}, u32[]{:S(2)}, u32[]{:S(2)}) collective-permute-start(f16[64,2048]{1,0:T(8,128)(2,1)S(1)} %add_convert_fusion.1), channel_id=1, source_target_pairs={{0,2},{1,3},{2,0},{3,1},{4,6},{5,7},{6,4},{7,5},{8,10},{9,11},{10,... | collective-permute-start | bytes 786440 | tf_op jit(solution)/shard_map/ppermute | solution.py:228
  101.9 1.6 %collective-permute-start.5 = (bf16[64,2048]{1,0:T(8,128)(2,1)S(1)}, bf16[64,2048]{1,0:T(8,128)(2,1)S(1)}, u32[]{:S(2)}, u32[]{:S(2)}) collective-permute-start(bf16[64,2048]{1,0:T(8,128)(2,1)S(1)} %get-tuple-element.8), channel_id=1, source_target_pairs={{0,1},{1,0},{2,3},{3,2},{4,5},{5,4},{6,7},{7,6},{8,9},{9,8},{10,11... | collective-permute-start | bytes 786440 | tf_op jit(solution)/shard_map/ppermute | solution.py:228
  102.0 1.9 %collective-permute-start.8 = (bf16[64,2048]{1,0:T(8,128)(2,1)S(1)}, bf16[64,2048]{1,0:T(8,128)(2,1)S(1)}, u32[]{:S(2)}, u32[]{:S(2)}) collective-permute-start(bf16[64,2048]{1,0:T(8,128)(2,1)S(1)} %get-tuple-element.7), channel_id=1, source_target_pairs={{0,1},{1,0},{2,3},{3,2},{4,5},{5,4},{6,7},{7,6},{8,9},{9,8},{10,11... | collective-permute-start | bytes 786440 | tf_op jit(solution)/shard_map/ppermute | solution.py:228
  102.5 1.8 %collective-permute-start.11 = (bf16[64,2048]{1,0:T(8,128)(2,1)S(1)}, bf16[64,2048]{1,0:T(8,128)(2,1)S(1)}, u32[]{:S(2)}, u32[]{:S(2)}) collective-permute-start(bf16[64,2048]{1,0:T(8,128)(2,1)S(1)} %get-tuple-element.9), channel_id=1, source_target_pairs={{0,1},{1,0},{2,3},{3,2},{4,5},{5,4},{6,7},{7,6},{8,9},{9,8},{10,11... | collective-permute-start | bytes 786440 | tf_op jit(solution)/shard_map/ppermute | solution.py:228
  102.6 2.1 %collective-permute-start.14 = (bf16[64,2048]{1,0:T(8,128)(2,1)S(1)}, bf16[64,2048]{1,0:T(8,128)(2,1)S(1)}, u32[]{:S(2)}, u32[]{:S(2)}) collective-permute-start(bf16[64,2048]{1,0:T(8,128)(2,1)S(1)} %get-tuple-element.6), channel_id=1, source_target_pairs={{0,1},{1,0},{2,3},{3,2},{4,5},{5,4},{6,7},{7,6},{8,9},{9,8},{10,11... | collective-permute-start | bytes 786440 | tf_op jit(solution)/shard_map/ppermute | solution.py:228
  104.8 1.3 %copy-start.7 = (bf16[64,16384]{1,0:T(8,128)(2,1)}, bf16[64,16384]{1,0:T(8,128)(2,1)S(1)}, u32[]{:S(2)}) copy-start(bf16[64,16384]{1,0:T(8,128)(2,1)S(1)} %select_dynamic-update-slice_fusion) | copy-start | bytes 6291460

commit v2 on v1

v2 whole, which is shorter than its diff:
```python
import functools
import math

import jax
import jax.numpy as jnp
from jax import lax
from jax.experimental import pallas as pl
from jax.experimental.pallas import tpu as pltpu
from jax.sharding import PartitionSpec as P

BLK = 128
LANES = 128
ITERS = 3
VMEM_BYTES = 40 << 20
SMALL_BYTES = 24 << 20
PULL_ROWS = 1024
CHUNKS = (3, 5)
F32 = jnp.float32
BF16 = jnp.bfloat16


def nt_dot(a, b):
    return lax.dot_general(a, b, (((1,), (1,)), ((), ())), preferred_element_type=F32)


def tn_dot(a, b):
    return lax.dot_general(a, b, (((0,), (0,)), ((), ())), preferred_element_type=F32)


def kernel_cost(seconds):
    return pl.CostEstimate(flops=0, bytes_accessed=int(seconds * 3.69e12), transcendentals=0)


def gram_kernel(
    core_ref, obs_hbm, fac_hbm, flg_hbm, out_ref, send_hbm, obs_ref, fac_ref, flg_ref, sems,
    send_sems, *, rows
):
    series = obs_ref.shape[0]
    half = send_hbm.shape[0]
    rank, blocks = fac_ref.shape[0], flg_ref.shape[0]
    flg_copy = pltpu.make_async_copy(flg_hbm, flg_ref, sems.at[0])
    fac_copy = pltpu.make_async_copy(fac_hbm, fac_ref, sems.at[1])
    flg_copy.start()
    fac_copy.start()
    first = (1 - core_ref[0]) * half
    cuts, copies, sends = [], [], []
    for i in range(series // rows):
        at = i * rows
        at = first + at if at < half else half - first + (at - half)
        cuts.append(pl.ds(pl.multiple_of(at, rows), rows))
        copies.append(
            pltpu.make_async_copy(obs_hbm.at[cuts[i]], obs_ref.at[cuts[i]], sems.at[2 + i])
        )
        copies[i].start()
    flg_copy.wait()
    fac_copy.wait()
    for i, (cut, copy) in enumerate(zip(cuts, copies)):
        fac = fac_ref[:, cut]
        flg = flg_ref[:, cut].astype(F32).astype(BF16)
        masked = jnp.concatenate([fac * flg[b : b + 1, :] for b in range(blocks)], axis=0)
        gram_part = nt_dot(fac, masked)
        copy.wait()
        if i * rows < half:
            sends.append(
                pltpu.make_async_copy(
                    obs_ref.at[cut], send_hbm.at[pl.ds(i * rows, rows)], send_sems.at[i]
                )
            )
            sends[i].start()
        parts = []
        for b in range(0, blocks, 2):
            both = jnp.dot(
                masked[b * rank : (b + 2) * rank],
                obs_ref[cut, b * BLK : (b + 2) * BLK],
                preferred_element_type=F32,
            )
            parts += [both[:rank, :BLK], both[rank:, BLK:]]
        new = jnp.concatenate(parts + [gram_part], axis=1)
        if i == 0:
            out_ref[...] = new
        else:
            out_ref[...] += new
    for send in sends:
        send.wait()


def in_hbm(x):
    return pltpu.with_memory_space_constraint(x, pltpu.HBM)


def gram(core, observed, fac_t, flg_t, rows):
    series, cols = observed.shape
    rank, blocks = fac_t.shape[0], flg_t.shape[0]
    width = cols + blocks * rank
    half = series // 2
    hbm = pl.BlockSpec(memory_space=pltpu.HBM)
    return pl.pallas_call(
        functools.partial(gram_kernel, rows=rows),
        in_specs=[pl.BlockSpec(memory_space=pltpu.SMEM), hbm, hbm, hbm],
        out_specs=[pl.BlockSpec(memory_space=pltpu.VMEM), hbm],
        out_shape=[
            jax.ShapeDtypeStruct((rank, width), F32),
            pltpu.HBM((half, cols), BF16),
        ],
        scratch_shapes=[
            pltpu.VMEM((series, cols), BF16),
            pltpu.VMEM(fac_t.shape, BF16),
            pltpu.VMEM(flg_t.shape, jnp.int32),
            pltpu.SemaphoreType.DMA((2 + series // rows,)),
            pltpu.SemaphoreType.DMA((half // rows,)),
        ],
        compiler_params=pltpu.CompilerParams(vmem_limit_bytes=32 << 20),
        cost_estimate=kernel_cost(8e-6),
        name="gram",
    )(core, in_hbm(observed), in_hbm(fac_t), in_hbm(flg_t))


def split(x):
    high = x.astype(BF16)
    return high, (x - high.astype(F32)).astype(BF16)


def split3(x):
    high, mid = split(x)
    return high, mid, (x - high.astype(F32) - mid.astype(F32)).astype(BF16)


def later(x, steps, fill):
    lane = lax.broadcasted_iota(jnp.int32, (x.shape[0], LANES), 1)
    before = jnp.broadcast_to(fill, (x.shape[0], LANES))
    out = []
    for j in range(0, x.shape[1], LANES):
        rolled = pltpu.roll(x[:, j : j + LANES], steps, 1)
        out.append(jnp.where(lane < steps, before, rolled))
        before = rolled
    return jnp.concatenate(out, axis=1)


def earlier(x, steps):
    lane = lax.broadcasted_iota(jnp.int32, (x.shape[0], LANES), 1)
    rolled = [
        pltpu.roll(x[:, j : j + LANES], LANES - steps, 1) for j in range(0, x.shape[1], LANES)
    ]
    rolled.append(jnp.zeros((x.shape[0], LANES), F32))
    out = [jnp.where(lane < LANES - steps, a, b) for a, b in zip(rolled[:-1], rolled[1:])]
    return jnp.concatenate(out, axis=1)


def taps(first, second):
    fh, fl = split(first)
    sh, sl = split(second)
    zero = jnp.zeros_like(fh)
    top = jnp.concatenate([fh, sh, fh, sh], axis=1)
    bottom = jnp.concatenate([fl, sl, zero, zero], axis=1)
    return jnp.concatenate([top, bottom], axis=0)


def pair_dot(weights, a, b):
    ah, al = split(a)
    bh, bl = split(b)
    both = jnp.dot(
        weights, jnp.concatenate([ah, bh, al, bl], axis=0), preferred_element_type=F32
    )
    rank = a.shape[0]
    return both[:rank] + both[rank:]


def column(row):
    shape = (row.shape[1], row.shape[1])
    same = lax.broadcasted_iota(jnp.int32, shape, 0) == lax.broadcasted_iota(jnp.int32, shape, 1)
    return jnp.sum(jnp.where(same, jnp.broadcast_to(row, shape), 0.0), axis=1, keepdims=True)


def reg_gradient(x, dil_ref, w_ref, bias_ref):
    d0, d1 = dil_ref[0], dil_ref[1]
    b0, b1 = column(bias_ref[0:1, :]), column(bias_ref[1:2, :])
    w = [w_ref[i] for i in range(4)]
    z = later(x, 1, 0.0)
    pre = pair_dot(taps(w[0], w[1]), later(z, d0, 0.0), z) + b0
    hidden = jnp.maximum(pre, 0.0)
    shown = later(hidden, d1, jnp.maximum(b0, 0.0))
    error = 0.1 * (x - z - pair_dot(taps(w[2], w[3]), shown, hidden) - b1)
    pull = -pair_dot(taps(w[2].T, w[3].T), earlier(error, d1), error)
    pull = jnp.where(pre > 0.0, pull, 0.0)
    back = pair_dot(taps(w[0].T, w[1].T), earlier(pull, d0), pull)
    return error + earlier(back - error, 1)


def steps_kernel(
    dil_ref, place_ref, w_hbm, bias_hbm, *refs, slabs, data_scale, entries, series
):
    sums_hbm, basis_hbm = refs[:slabs], refs[slabs : 2 * slabs]
    own_hbm, sib_hbm, fac_hbm, own_flg_hbm, sib_flg_hbm = refs[2 * slabs : 2 * slabs + 5]
    basis_out, own_b_out, sib_b_out, pull_ref = refs[2 * slabs + 5 : 2 * slabs + 9]
    x_ref, xb_ref, data_ref, sums_ref, w_ref, bias_ref, fac_ref, flg_ref, sems = refs[
        2 * slabs + 9 : -2
    ]
    pull_scratch = refs[-2:]
    core = place_ref[0] % 2
    rank, cols = basis_out.shape
    starts = [pl.multiple_of((place_ref[0] ^ m) * cols, cols) for m in range(slabs)]
    mine = pl.ds(pl.multiple_of(core * (fac_hbm.shape[1] // 2), series), series)
    pairs = [(basis_hbm[m], x_ref.at[:, pl.ds(starts[m], cols)]) for m in range(slabs)]
    pairs += [(w_hbm, w_ref), (bias_hbm, bias_ref)]
    pairs += [(sums_hbm[m], sums_ref.at[m]) for m in range(slabs)]
    late = [
        (fac_hbm.at[:, mine], fac_ref),
        (own_flg_hbm.at[:, mine], flg_ref.at[0]),
        (sib_flg_hbm.at[:, mine], flg_ref.at[1]),
    ]
    loads = [
        pltpu.make_async_copy(source, target, sems.at[i])
        for i, (source, target) in enumerate(pairs + late)
    ]
    for load in loads:
        load.start()
    copies = pull_copies(core, own_hbm, sib_hbm, pull_scratch, 0, 0, series)
    for load in loads[: len(pairs)]:
        load.wait()

    def step(i, carry):
        reg = reg_gradient(x_ref[...], dil_ref, w_ref, bias_ref)
        xb_ref[...] = x_ref[...].astype(BF16)
        for m in range(slabs):
            for b in range(0, cols // BLK, 2):
                high, mid, low = split3(sums_ref[m, :, cols + b * rank : cols + (b + 2) * rank])
                at = pl.multiple_of(starts[m] + b * BLK, 2 * BLK)
                xb = xb_ref[:, pl.ds(at, 2 * BLK)]
                zero = jnp.zeros((rank, BLK), BF16)
                right = jnp.concatenate(
                    [
                        jnp.concatenate([xb[:, :BLK], zero], axis=1),
                        jnp.concatenate([zero, xb[:, BLK:]], axis=1),
                    ],
                    axis=0,
                )
                got = jnp.dot(
                    jnp.concatenate([high, mid, low], axis=0), right, preferred_element_type=F32
                )
                got = got[:rank] + (got[rank : 2 * rank] + got[2 * rank :])
                data_ref[:, pl.ds(at, 2 * BLK)] = got - sums_ref[m, :, b * BLK : (b + 2) * BLK]
        grad = data_ref[...] * data_scale + reg
        square = jnp.sum(grad * grad)
        x_ref[...] -= grad * (0.1 * lax.rsqrt(jnp.full((1, 1), square) / entries + 1e-06))
        return carry

    lax.fori_loop(0, ITERS, step, 0)
    basis_out[...] = x_ref[:, pl.ds(starts[0], cols)]
    own_b = x_ref[:, pl.ds(starts[0], cols)].astype(BF16)
    sib_b = x_ref[:, pl.ds(starts[1], cols)].astype(BF16)
    own_b_out[...] = own_b
    sib_b_out[...] = sib_b
    for load in loads[len(pairs) :]:
        load.wait()
    pull_chunk(
        0, copies, pull_scratch, fac_ref, flg_ref.at[0], flg_ref.at[1], own_b, sib_b, pull_ref
    )


def basis_steps(
    dilations, place, weights, bias, basis, sums, observed, sibling, fac_t, flags, data_scale,
    series
):
    slabs = len(sums)
    rank, cols = basis[0].shape
    total = slabs * cols
    smem = pl.BlockSpec(memory_space=pltpu.SMEM)
    vmem = pl.BlockSpec(memory_space=pltpu.VMEM)
    operands = [weights, bias, *sums, *basis, observed, sibling, fac_t, *flags]
    kernel = functools.partial(
        steps_kernel, slabs=slabs, data_scale=data_scale, entries=float(rank * total),
        series=series,
    )
    return pl.pallas_call(
        kernel,
        in_specs=[smem, smem] + [pl.BlockSpec(memory_space=pltpu.HBM)] * len(operands),
        out_specs=[vmem] * 4,
        out_shape=[
            jax.ShapeDtypeStruct((rank, cols), F32),
            jax.ShapeDtypeStruct((rank, cols), BF16),
            jax.ShapeDtypeStruct((rank, cols), BF16),
            jax.ShapeDtypeStruct((rank, series), F32),
        ],
        scratch_shapes=[
            pltpu.VMEM((rank, total), F32),
            pltpu.VMEM((rank, total), BF16),
            pltpu.VMEM((rank, total), F32),
            pltpu.VMEM((slabs, *sums[0].shape), F32),
            pltpu.VMEM(weights.shape, F32),
            pltpu.VMEM(bias.shape, F32),
            pltpu.VMEM((rank, series), BF16),
            pltpu.VMEM((2, flags[0].shape[0], series), jnp.int32),
            pltpu.SemaphoreType.DMA((2 * slabs + 5,)),
        ]
        + pull_scratch_shapes(cols, series),
        compiler_params=pltpu.CompilerParams(vmem_limit_bytes=32 << 20),
        cost_estimate=kernel_cost(8e-6),
        name="basis_steps",
    )(dilations, place, *[in_hbm(x) for x in operands])


def pull_rows(obs, fac, flg, basis):
    pred = tn_dot(fac, basis)
    resid = (pred - obs.astype(F32)).astype(BF16)
    total = None
    for b in range(flg.shape[0]):
        block = slice(b * BLK, (b + 1) * BLK)
        term = nt_dot(basis[:, block], resid[:, block]) * flg[b : b + 1, :].astype(F32)
        total = term if total is None else total + term
    return total


def pull_scratch_shapes(cols, series):
    return [
        pltpu.VMEM((2, series, cols), BF16),
        pltpu.SemaphoreType.DMA((-(-series // PULL_ROWS), 2)),
    ]


def pull_copies(core, own_hbm, sib_hbm, scratch, first, sib_first, series):
    obs_ref, sems = scratch
    base = core * (own_hbm.shape[0] // 2) + first
    rows = min(series, PULL_ROWS)
    copies = []
    for i in range(series // rows):
        here = pl.ds(i * rows, rows)
        own = pl.ds(pl.multiple_of(base + i * rows, rows), rows)
        copies.append(
            [
                pltpu.make_async_copy(own_hbm.at[own], obs_ref.at[0, here], sems.at[i, 0]),
                pltpu.make_async_copy(
                    sib_hbm.at[pl.ds(sib_first + i * rows, rows)], obs_ref.at[1, here], sems.at[i, 1]
                ),
            ]
        )
        for copy in copies[i]:
            copy.start()
    return copies


def pull_chunk(
    base, copies, scratch, fac_ref, own_flg_ref, sib_flg_ref, own_basis, sib_basis, out_ref
):
    obs_ref = scratch[0]
    rows = out_ref.shape[1] // len(copies)
    for i, pair in enumerate(copies):
        here = pl.ds(i * rows, rows)
        own = pl.ds(pl.multiple_of(base + i * rows, rows), rows)
        fac = fac_ref[:, own]
        pair[0].wait()
        pair[1].wait()
        out_ref[:, here] = pull_rows(
            obs_ref[0, here, :], fac, own_flg_ref[:, own], own_basis
        ) + pull_rows(obs_ref[1, here, :], fac, sib_flg_ref[:, own], sib_basis)


def pull_kernel(
    core_ref, own_hbm, sib_hbm, fac_ref, own_flg_ref, sib_flg_ref, own_basis_ref, sib_basis_ref,
    out_ref, *scratch, first, sib_first
):
    copies = pull_copies(
        core_ref[0], own_hbm, sib_hbm, scratch, first, sib_first, out_ref.shape[1]
    )
    pull_chunk(
        core_ref[0] * (fac_ref.shape[1] // 2) + first, copies, scratch, fac_ref, own_flg_ref,
        sib_flg_ref, own_basis_ref[...], sib_basis_ref[...], out_ref,
    )


def factor_pull(core, observed, sibling, fac_t, flags, basis_b, first, sib_first, series):
    vmem = pl.BlockSpec(memory_space=pltpu.VMEM)
    hbm = pl.BlockSpec(memory_space=pltpu.HBM)
    return pl.pallas_call(
        functools.partial(pull_kernel, first=first, sib_first=sib_first),
        in_specs=[pl.BlockSpec(memory_space=pltpu.SMEM), hbm, hbm] + [vmem] * 5,
        out_specs=vmem,
        out_shape=jax.ShapeDtypeStruct((fac_t.shape[0], series), F32),
        scratch_shapes=pull_scratch_shapes(observed.shape[1], series),
        compiler_params=pltpu.CompilerParams(vmem_limit_bytes=24 << 20),
        cost_estimate=kernel_cost(2e-6 * series / 1024),
        name="factor_pull",
    )(core, in_hbm(observed), in_hbm(sibling), fac_t, *flags, *basis_b)


def put_kernel(core_ref, *refs, places):
    pieces, (out, sems) = refs[: 2 * len(places)], refs[-2:]
    half = out.shape[1] // 2
    copies = []
    for i, ref in enumerate(pieces):
        side = core_ref[0] if i % 2 == 0 else 1 - core_ref[0]
        at = pl.multiple_of(side * half + places[i // 2], LANES)
        copies.append(
            pltpu.make_async_copy(ref, out.at[:, pl.ds(at, ref.shape[1])], sems.at[i])
        )
        copies[-1].start()
    for copy in copies:
        copy.wait()


def put(core, pieces, places, out, shape):
    old = [] if out is None else [in_hbm(out)]
    return pl.pallas_call(
        functools.partial(put_kernel, places=places),
        in_specs=[pl.BlockSpec(memory_space=pltpu.SMEM)]
        + [pl.BlockSpec(memory_space=pltpu.VMEM)] * len(pieces)
        + [pl.BlockSpec(memory_space=pltpu.HBM)] * len(old),
        out_specs=pl.BlockSpec(memory_space=pltpu.HBM),
        out_shape=pltpu.HBM(shape, BF16),
        scratch_shapes=[pltpu.SemaphoreType.DMA((len(pieces),))],
        input_output_aliases={1 + len(pieces): 0} if old else {},
        compiler_params=pltpu.CompilerParams(vmem_limit_bytes=4 << 20),
        cost_estimate=kernel_cost(1e-6),
        name="put",
    )(core, *pieces, *old)


def swap(x, axis, bit):
    count = lax.axis_size(axis)
    return lax.ppermute(x, axis, [(i, i ^ bit) for i in range(count)])


def sum_over(x, axis):
    count = lax.axis_size(axis)
    if count & (count - 1):
        return lax.psum(x, axis)
    bit = 1
    while bit < count:
        x = x + swap(x, axis, bit)
        bit *= 2
    return x


def gather_over(x, axis):
    bit = lax.axis_size(axis) // 2
    pieces, order = [x], [0]
    while bit:
        pieces += [swap(p, axis, bit) for p in pieces]
        order += [m ^ bit for m in order]
        bit //= 2
    return [p for _, p in sorted(zip(order, pieces), key=lambda pair: pair[0])]


def after(x, *others):
    return lax.optimization_barrier((x, *others))[0]


def shards(observed, flags, factors, basis, tcn_weights, tcn_bias, dilations):
    series, cols = observed.shape
    half = series // 2
    time_count = lax.axis_size("tm")
    place = lax.axis_index("tm")
    core = (place % 2).astype(jnp.int32).reshape(1)
    fac_t, flg_t = factors.T, flags.T
    data_scale = 1.0 / math.sqrt(series * lax.axis_size("series"))
    coef = 0.1 / math.sqrt(cols * time_count)

    place = place.astype(jnp.int32).reshape(1)
    unit = half // sum(CHUNKS)

    sums, send = gram(core, observed, fac_t, flg_t, 1024)
    sibling = swap(send, "tm", 1)
    far = swap(after(basis, sums), "tm", 2)
    slabs = [basis, swap(basis, "tm", 1), far, swap(far, "tm", 1)]
    sums = sum_over(sums, "series")
    flags = (flg_t, swap(flg_t, "tm", 1))
    new_basis, own_b, sib_b, pull = basis_steps(
        dilations, place, tcn_weights, tcn_bias, slabs, gather_over(sums, "tm"),
        observed, sibling, fac_t, flags, data_scale, CHUNKS[0] * unit,
    )
    sent, arrived, pieces, firsts = [], [], [], [0]
    for c, chunk in enumerate(CHUNKS):
        first, width = firsts[c], chunk * unit
        if c > 0:
            own_b = after(own_b, *sent)
            pull = factor_pull(
                core, observed, sibling, fac_t, flags, (own_b, sib_b), first, first, width
            )
        own = (pull * coef).astype(jnp.float16)
        sent.append(after(own, *arrived) if arrived else own)
        arrived.append(swap(sent[-1], "tm", 2))
        firsts.append(first + width)
    for c, (own, got) in enumerate(zip(sent, arrived)):
        if c == len(sent) - 1:
            new_factors = put(core, pieces, firsts[:c], None, fac_t.shape)
            got = after(got, new_factors)
            pieces = []
        both = own.astype(F32) + got.astype(F32)
        mine = lax.dynamic_slice_in_dim(fac_t, core[0] * half + firsts[c], own.shape[1], 1)
        new = (mine.astype(F32) - both).astype(BF16)
        pieces += [new, swap(new, "tm", 1)]
    new_factors = put(core, pieces, firsts[-2:-1], new_factors, fac_t.shape)
    return new_basis, new_factors.T


def solution(mesh):
    return jax.shard_map(
        shards,
        mesh=mesh,
        in_specs=(
            P("series", "tm"),
            P("series", "tm"),
            P("series", None),
            P(None, "tm"),
            P(),
            P(),
            P(),
        ),
        out_specs=(P(None, "tm"), P("series", None)),
        check_vma=False,
    )
```

time: 106 us -> 95.6 us (0.902)
  blocking collectives: 16 us -> 0 us
  waiting for transfers between devices: 31.6 us -> 42.9 us
  local copies, waits for them, and re-layouts: 4.48 us -> 0.84 us
  other arithmetic: 3.21 us -> 1.76 us
    all_gather x2 -> x0, blocking collectives: 16 us -> none  [gather_over(): return lax.all_gather(x, axis, axis=0, tiled=False)]
    ppermute x15, waiting for transfers between devices: 31.6 us -> 42.9 us  [swap(): return lax.ppermute(x, axis, [(i, i ^ bit) for i in range(count)])]
    unnamed x20 -> x28, local copies, waits for them, and re-layouts: 4.14 us -> 0.84 us
    pallas_call x6 -> x5, Pallas kernels: 35.8 us -> 35.4 us  [the longest x1 14.1 us: basis_steps(): pl.pallas_call(kernel, in_specs=[smem, smem] + [pl.BlockSpec(memory_space...]
  transfers between devices with their start and end apart: 15 -> 15, of which waited for: 11 -> 9; matrix products, arithmetic and copies ran while one was open for 2% -> 0% of each run, Pallas kernels for 0% -> 10%
where the time goes in v2:
time: 95.6 us; the launch traced here: 95.4 us
  waiting for transfers between devices  42.9 us (45%)
  Pallas kernels  35.4 us (37%)
  starting transfers between devices  13.4 us (14%)
  other arithmetic  1.76 us (2%)
  between operations  1.03 us (1%)
    ppermute x15, waiting for transfers between devices, swap(): return lax.ppermute(x, axis, [(i, i ^ bit) for i in range(count)])  42.9 us
    pallas_call x1, Pallas kernels, basis_steps(): pl.pallas_call(kernel, in_specs=[smem, smem] + [pl.BlockSpec(memory_space...  14.1 us
    ppermute x15, starting transfers between devices, swap(): return lax.ppermute(x, axis, [(i, i ^ bit) for i in range(count)])  13.4 us
    pallas_call x1, Pallas kernels, gram(): pl.pallas_call(functools.partial(gram_kernel, rows=rows), in_specs=[pl.Bl...  10.3 us
    pallas_call x1, Pallas kernels, factor_pull(): pl.pallas_call(functools.partial(pull_kernel, first=first, sib_first=sib_...  9.04 us
    pallas_call x2, Pallas kernels, put(): pl.pallas_call(functools.partial(put_kernel, places=places), in_specs=[pl...  1.96 us
  transfers between devices with their start and end apart: 15, of which 9 were waited for; matrix products, arithmetic and copies ran while one was open for 0% of the time, Pallas kernels for 10%

profile of v2, /device:TPU:0, one launch (start us, length us, event | category | flops | bytes accessed | tf_op | source)
XLA Modules:
  0.0 95.4 jit_solution(13400678243616803183)
XLA Ops:
  0.6 10.3 %gram.1 = (f32[64,768]{1,0:T(8,128)S(1)}, bf16[8192,512]{1,0:T(8,128)(2,1)}) custom-call(s32[1]{0:T(128)} %bitcast.1.core_ref, bf16[16384,512]{1,0:T(8,128)(2,1)} %own_hbm.1, bf16[64,16384]{1,0:T(8,128)(2,1)} %bitcast.13, s32[4,16384]{1,0:T(4,128)} %bitcast.16), custom_call_target="tpu_custom_call" | custom-call | bytes 29520000 | tf_op jit(solution)/shard_map/gram/pallas_call | solution.py:97
  11.0 0.5 collective-permute-start.9
  11.6 2.6 %collective-permute-start = (f32[64,768]{1,0:T(8,128)S(1)}, f32[64,768]{1,0:T(8,128)S(1)}, u32[]{:S(2)}, u32[]{:S(2)}) collective-permute-start(f32[64,768]{1,0:T(8,128)S(1)} %get-tuple-element.12), channel_id=1, source_target_pairs={{0,4},{4,0},{8,12},{12,8},{16,20},{20,16},{24,28},{28,24},{1,5},{5... | collective-permute-start | bytes 589832 | tf_op jit(solution)/shard_map/ppermute | solution.py:419
  14.1 5.5 %collective-permute-done = f32[64,768]{1,0:T(8,128)S(1)} collective-permute-done((f32[64,768]{1,0:T(8,128)S(1)}, f32[64,768]{1,0:T(8,128)S(1)}, u32[]{:S(2)}, u32[]{:S(2)}) %collective-permute-start) | collective-permute-done | bytes 196640 | tf_op jit(solution)/shard_map/ppermute | solution.py:419
  19.7 1.9 %collective-permute-start.1 = (f32[64,768]{1,0:T(8,128)S(1)}, f32[64,768]{1,0:T(8,128)S(1)}, u32[]{:S(2)}, u32[]{:S(2)}) collective-permute-start(f32[64,768]{1,0:T(8,128)S(1)} %add.31), channel_id=1, source_target_pairs={{0,8},{4,12},{8,0},{12,4},{16,24},{20,28},{24,16},{28,20},{1,9},{5... | collective-permute-start | bytes 589832 | tf_op jit(solution)/shard_map/ppermute | solution.py:419
  21.5 4.8 %collective-permute-done.1 = f32[64,768]{1,0:T(8,128)S(1)} collective-permute-done((f32[64,768]{1,0:T(8,128)S(1)}, f32[64,768]{1,0:T(8,128)S(1)}, u32[]{:S(2)}, u32[]{:S(2)}) %collective-permute-start.1) | collective-permute-done | bytes 196640 | tf_op jit(solution)/shard_map/ppermute | solution.py:419
  26.4 2.7 %collective-permute-start.2 = (f32[64,768]{1,0:T(8,128)S(1)}, f32[64,768]{1,0:T(8,128)S(1)}, u32[]{:S(2)}, u32[]{:S(2)}) collective-permute-start(f32[64,768]{1,0:T(8,128)S(1)} %add.32), channel_id=1, source_target_pairs={{0,16},{4,20},{8,24},{12,28},{16,0},{20,4},{24,8},{28,12},{1,17},{... | collective-permute-start | bytes 589832 | tf_op jit(solution)/shard_map/ppermute | solution.py:419
  29.1 8.3 %collective-permute-done.2 = f32[64,768]{1,0:T(8,128)S(1)} collective-permute-done((f32[64,768]{1,0:T(8,128)S(1)}, f32[64,768]{1,0:T(8,128)S(1)}, u32[]{:S(2)}, u32[]{:S(2)}) %collective-permute-start.2) | collective-permute-done | bytes 196640 | tf_op jit(solution)/shard_map/ppermute | solution.py:419
  37.4 1.4 %collective-permute-start.4 = (f32[64,768]{1,0:T(8,128)S(1)}, f32[64,768]{1,0:T(8,128)S(1)}, u32[]{:S(2)}, u32[]{:S(2)}) collective-permute-start(f32[64,768]{1,0:T(8,128)S(1)} %add.33.refs_0_), channel_id=1, source_target_pairs={{0,2},{1,3},{2,0},{3,1},{4,6},{5,7},{6,4},{7,5},{8,10},{9,11},{10,... | collective-permute-start | bytes 589832 | tf_op jit(solution)/shard_map/ppermute | solution.py:419
  38.8 0.7 collective-permute-start.7
  39.5 0.5 collective-permute-start.10
  40.0 6.2 %collective-permute-done.7.refs_6_ = f32[64,512]{1,0:T(8,128)S(1)} collective-permute-done((f32[64,512]{1,0:T(8,128)S(1)}, f32[64,512]{1,0:T(8,128)S(1)}, u32[]{:S(2)}, u32[]{:S(2)}) %collective-permute-start.7) | collective-permute-done | bytes 131104 | tf_op jit(solution)/shard_map/ppermute | solution.py:419
  46.2 0.5 collective-permute-start.5
  46.7 0.1 collective-permute-start.8
  46.8 1.3 %collective-permute-done.8.refs_7_ = f32[64,512]{1,0:T(8,128)S(1)} collective-permute-done((f32[64,512]{1,0:T(8,128)S(1)}, f32[64,512]{1,0:T(8,128)S(1)}, u32[]{:S(2)}, u32[]{:S(2)}) %collective-permute-start.8) | collective-permute-done | bytes 131104 | tf_op jit(solution)/shard_map/ppermute | solution.py:419
  48.2 0.5 copy-done.13
  48.8 0.1 copy-done.3
  48.9 0.1 copy-done.9
  49.0 14.1 %basis_steps.1 = (f32[64,512]{1,0:T(8,128)}, bf16[64,512]{1,0:T(8,128)(2,1)S(1)}, bf16[64,512]{1,0:T(8,128)(2,1)S(1)}, f32[64,3072]{1,0:T(8,128)S(1)}) custom-call(s32[2]{0:T(128)S(1)} %copy-done.5, s32[1]{0:T(128)} %bitcast.place_ref, f32[4,64,64]{2,1,0:T(8,128)} %w_hbm.1, f32[2,64]{1,0:T(2,128)} %bias_hbm.1, f32[64,768]{1,0:T(8,128)} %copy-done.6, ...), custom_call_target="tpu_custom_call" | custom-call | bytes 29520000 | tf_op jit(solution)/shard_map/basis_steps/pallas_call | solution.py:274
  63.1 0.1 multiply_convert_fusion.1
  63.2 1.2 %collective-permute-start.11 = (f16[64,3072]{1,0:T(8,128)(2,1)S(1)}, f16[64,3072]{1,0:T(8,128)(2,1)S(1)}, u32[]{:S(2)}, u32[]{:S(2)}) collective-permute-start(f16[64,3072]{1,0:T(8,128)(2,1)S(1)} %multiply_convert_fusion.1), channel_id=1, source_target_pairs={{0,2},{1,3},{2,0},{3,1},{4,6},{5,7},{6,4},{7,5},{8,10},{9,11},{10,... | collective-permute-start | bytes 1179656 | tf_op jit(solution)/shard_map/ppermute | solution.py:419
  64.4 9.0 %factor_pull.1 = f32[64,5120]{1,0:T(8,128)S(1)} custom-call(s32[1]{0:T(128)} %bitcast.1.core_ref, bf16[16384,512]{1,0:T(8,128)(2,1)} %own_hbm.1, bf16[8192,512]{1,0:T(8,128)(2,1)} %collective-permute-done.9.refs_9_.sib_hbm, bf16[64,16384]{1,0:T(8,128)(2,1)S(1)} %bitcast.15, s32[4,16384]{1,0:T(4,128)S(1)} %bitcast.19, s32[4,16384]{1,0:T(4,128)S(1)} %copy-done.4, ...), custom_call_target="tpu_custom_call" | custom-call | bytes 36900000 | tf_op jit(solution)/shard_map/factor_pull/pallas_call | solution.py:373
  73.5 0.1 multiply_convert_fusion
  73.6 0.9 collective-permute-done.11
  74.5 1.2 %collective-permute-start.12 = (f16[64,5120]{1,0:T(8,128)(2,1)S(1)}, f16[64,5120]{1,0:T(8,128)(2,1)}, u32[]{:S(2)}, u32[]{:S(2)}) collective-permute-start(f16[64,5120]{1,0:T(8,128)(2,1)S(1)} %multiply_convert_fusion), channel_id=1, source_target_pairs={{0,2},{1,3},{2,0},{3,1},{4,6},{5,7},{6,4},{7,5},{8,10},{9,11},{10,... | collective-permute-start | bytes 1966088 | tf_op jit(solution)/shard_map/ppermute | solution.py:419
  75.7 0.2 fusion.1.refs_0_
  75.9 1.7 %collective-permute-done.13.refs_1_ = bf16[64,3072]{1,0:T(8,128)(2,1)S(1)} collective-permute-done((bf16[64,3072]{1,0:T(8,128)(2,1)S(1)}, bf16[64,3072]{1,0:T(8,128)(2,1)S(1)}, u32[]{:S(2)}, u32[]{:S(2)}) %collective-permute-start.13) | collective-permute-done | bytes 393248 | tf_op jit(solution)/shard_map/ppermute | solution.py:419
  77.6 0.9 put.2.refs_2_
  78.5 12.1 %collective-permute-done.12 = f16[64,5120]{1,0:T(8,128)(2,1)} collective-permute-done((f16[64,5120]{1,0:T(8,128)(2,1)S(1)}, f16[64,5120]{1,0:T(8,128)(2,1)}, u32[]{:S(2)}, u32[]{:S(2)}) %collective-permute-start.12) | collective-permute-done | bytes 655392 | tf_op jit(solution)/shard_map/ppermute | solution.py:419
  90.7 1.3 %fusion.refs_0_ = bf16[64,5120]{1,0:T(8,128)(2,1)S(1)} fusion(f16[64,5120]{1,0:T(8,128)(2,1)} %collective-permute-done.12, f16[64,5120]{1,0:T(8,128)(2,1)S(1)} %multiply_convert_fusion, bf16[16384,64]{0,1:T(8,128)(2,1)S(1)} %copy-done, s32[]{:T(128)S(6)} %select_n.14), kind=kLoop, calls=%fused_computation.1 | loop fusion | flops 1966080 | bytes 2621444 | tf_op jit(solution)/shard_map/convert_element_type | solution.py:489
  92.1 2.1 %collective-permute-done.14.refs_1_ = bf16[64,5120]{1,0:T(8,128)(2,1)S(1)} collective-permute-done((bf16[64,5120]{1,0:T(8,128)(2,1)S(1)}, bf16[64,5120]{1,0:T(8,128)(2,1)S(1)}, u32[]{:S(2)}, u32[]{:S(2)}) %collective-permute-start.14) | collective-permute-done | bytes 655392 | tf_op jit(solution)/shard_map/ppermute | solution.py:419
  94.2 1.1 %put.3 = bf16[64,16384]{1,0:T(8,128)(2,1)} custom-call(s32[1]{0:T(128)} %bitcast.1.core_ref, bf16[64,5120]{1,0:T(8,128)(2,1)S(1)} %fusion.refs_0_, bf16[64,5120]{1,0:T(8,128)(2,1)S(1)} %collective-permute-done.14.refs_1_, bf16[64,16384]{1,0:T(8,128)(2,1)} %put.2.refs_2_), custom_call_target="tpu_custom_call", output_to_operand_aliasing={{}: (3, {})} | custom-call | bytes 3690000 | tf_op jit(solution)/shard_map/put/pallas_call | solution.py:402
  (38 shorter events, 0.4 us)
Async XLA Ops:
  11.0 27.8 %copy-start.10 = (f32[64,512]{1,0:T(8,128)S(1)}, f32[64,512]{1,0:T(8,128)}, u32[]{:S(2)}) copy-start(f32[64,512]{1,0:T(8,128)} %refs_4_.1) | copy-start | bytes 393220
  11.0 28.5 %copy-start.1 = (s32[16384,4]{0,1:T(4,128)S(1)}, s32[16384,4]{0,1:T(4,128)}, u32[]{:S(2)}) copy-start(s32[16384,4]{0,1:T(4,128)} %param.8) | copy-start | bytes 786436
  11.0 38.0 %copy-start.5 = (s32[2]{0:T(128)S(1)}, s32[2]{0:T(128)}, u32[]{:S(2)}) copy-start(s32[2]{0:T(128)} %dil_ref.1) | copy-start | bytes 28
  11.0 37.1 %collective-permute-start.9 = (bf16[8192,512]{1,0:T(8,128)(2,1)}, bf16[8192,512]{1,0:T(8,128)(2,1)}, u32[]{:S(2)}, u32[]{:S(2)}) collective-permute-start(bf16[8192,512]{1,0:T(8,128)(2,1)} %get-tuple-element.14), channel_id=1, source_target_pairs={{0,1},{1,0},{2,3},{3,2},{4,5},{5,4},{6,7},{7,6},{8,9},{9,8},{10,11... | collective-permute-start | bytes 25165832 | tf_op jit(solution)/shard_map/ppermute | solution.py:419
  11.6 8.1 %collective-permute-start = (f32[64,768]{1,0:T(8,128)S(1)}, f32[64,768]{1,0:T(8,128)S(1)}, u32[]{:S(2)}, u32[]{:S(2)}) collective-permute-start(f32[64,768]{1,0:T(8,128)S(1)} %get-tuple-element.12), channel_id=1, source_target_pairs={{0,4},{4,0},{8,12},{12,8},{16,20},{20,16},{24,28},{28,24},{1,5},{5... | collective-permute-start | bytes 589832 | tf_op jit(solution)/shard_map/ppermute | solution.py:419
  19.7 6.7 %collective-permute-start.1 = (f32[64,768]{1,0:T(8,128)S(1)}, f32[64,768]{1,0:T(8,128)S(1)}, u32[]{:S(2)}, u32[]{:S(2)}) collective-permute-start(f32[64,768]{1,0:T(8,128)S(1)} %add.31), channel_id=1, source_target_pairs={{0,8},{4,12},{8,0},{12,4},{16,24},{20,28},{24,16},{28,20},{1,9},{5... | collective-permute-start | bytes 589832 | tf_op jit(solution)/shard_map/ppermute | solution.py:419
  26.4 11.0 %collective-permute-start.2 = (f32[64,768]{1,0:T(8,128)S(1)}, f32[64,768]{1,0:T(8,128)S(1)}, u32[]{:S(2)}, u32[]{:S(2)}) collective-permute-start(f32[64,768]{1,0:T(8,128)S(1)} %add.32), channel_id=1, source_target_pairs={{0,16},{4,20},{8,24},{12,28},{16,0},{20,4},{24,8},{28,12},{1,17},{... | collective-permute-start | bytes 589832 | tf_op jit(solution)/shard_map/ppermute | solution.py:419
  37.4 10.8 %copy-start.6 = (f32[64,768]{1,0:T(8,128)}, f32[64,768]{1,0:T(8,128)S(1)}, u32[]{:S(2)}) copy-start(f32[64,768]{1,0:T(8,128)S(1)} %add.33.refs_0_) | copy-start | bytes 589828
  37.4 8.8 %collective-permute-start.4 = (f32[64,768]{1,0:T(8,128)S(1)}, f32[64,768]{1,0:T(8,128)S(1)}, u32[]{:S(2)}, u32[]{:S(2)}) collective-permute-start(f32[64,768]{1,0:T(8,128)S(1)} %add.33.refs_0_), channel_id=1, source_target_pairs={{0,2},{1,3},{2,0},{3,1},{4,6},{5,7},{6,4},{7,5},{8,10},{9,11},{10,... | collective-permute-start | bytes 589832 | tf_op jit(solution)/shard_map/ppermute | solution.py:419
  38.8 7.4 %collective-permute-start.7 = (f32[64,512]{1,0:T(8,128)S(1)}, f32[64,512]{1,0:T(8,128)S(1)}, u32[]{:S(2)}, u32[]{:S(2)}) collective-permute-start(f32[64,512]{1,0:T(8,128)S(1)} %copy-done.10), channel_id=1, source_target_pairs={{0,2},{1,3},{2,0},{3,1},{4,6},{5,7},{6,4},{7,5},{8,10},{9,11},{10,... | collective-permute-start | bytes 393224 | tf_op jit(solution)/shard_map/ppermute | solution.py:419
  39.5 7.2 %collective-permute-start.6 = (f32[64,512]{1,0:T(8,128)S(1)}, f32[64,512]{1,0:T(8,128)S(1)}, u32[]{:S(2)}, u32[]{:S(2)}) collective-permute-start(f32[64,512]{1,0:T(8,128)S(1)} %copy-done.10), channel_id=1, source_target_pairs={{0,1},{1,0},{2,3},{3,2},{4,5},{5,4},{6,7},{7,6},{8,9},{9,8},{10,11... | collective-permute-start | bytes 393224 | tf_op jit(solution)/shard_map/ppermute | solution.py:419
  39.5 8.6 %collective-permute-start.10 = (s32[4,16384]{1,0:T(4,128)S(1)}, s32[4,16384]{1,0:T(4,128)S(1)}, u32[]{:S(2)}, u32[]{:S(2)}) collective-permute-start(s32[4,16384]{1,0:T(4,128)S(1)} %bitcast.18), channel_id=1, source_target_pairs={{0,1},{1,0},{2,3},{3,2},{4,5},{5,4},{6,7},{7,6},{8,9},{9,8},{10,11... | collective-permute-start | bytes 786440 | tf_op jit(solution)/shard_map/ppermute | solution.py:419
  46.2 2.0 %copy-start.11 = (f32[64,512]{1,0:T(8,128)}, f32[64,512]{1,0:T(8,128)S(1)}, u32[]{:S(2)}) copy-start(f32[64,512]{1,0:T(8,128)S(1)} %collective-permute-done.7.refs_6_) | copy-start | bytes 393220
  46.2 1.9 %collective-permute-start.3 = (f32[64,768]{1,0:T(8,128)S(1)}, f32[64,768]{1,0:T(8,128)S(1)}, u32[]{:S(2)}, u32[]{:S(2)}) collective-permute-start(f32[64,768]{1,0:T(8,128)S(1)} %add.33.refs_0_), channel_id=1, source_target_pairs={{0,1},{1,0},{2,3},{3,2},{4,5},{5,4},{6,7},{7,6},{8,9},{9,8},{10,11... | collective-permute-start | bytes 589832 | tf_op jit(solution)/shard_map/ppermute | solution.py:419
  46.2 2.0 %copy-start.7 = (f32[64,768]{1,0:T(8,128)}, f32[64,768]{1,0:T(8,128)S(1)}, u32[]{:S(2)}) copy-start(f32[64,768]{1,0:T(8,128)S(1)} %collective-permute-done.4.refs_2_) | copy-start | bytes 589828
  46.2 1.9 %collective-permute-start.5 = (f32[64,768]{1,0:T(8,128)S(1)}, f32[64,768]{1,0:T(8,128)S(1)}, u32[]{:S(2)}, u32[]{:S(2)}) collective-permute-start(f32[64,768]{1,0:T(8,128)S(1)} %collective-permute-done.4.refs_2_), channel_id=1, source_target_pairs={{0,1},{1,0},{2,3},{3,2},{4,5},{5,4},{6,7},{7,6},{8,9},{9,8},{10,11... | collective-permute-start | bytes 589832 | tf_op jit(solution)/shard_map/ppermute | solution.py:419
  46.7 1.5 %copy-start.12 = (f32[64,512]{1,0:T(8,128)}, f32[64,512]{1,0:T(8,128)S(1)}, u32[]{:S(2)}) copy-start(f32[64,512]{1,0:T(8,128)S(1)} %collective-permute-done.6.refs_5_) | copy-start | bytes 393220
  46.7 1.4 %collective-permute-start.8 = (f32[64,512]{1,0:T(8,128)S(1)}, f32[64,512]{1,0:T(8,128)S(1)}, u32[]{:S(2)}, u32[]{:S(2)}) collective-permute-start(f32[64,512]{1,0:T(8,128)S(1)} %collective-permute-done.7.refs_6_), channel_id=1, source_target_pairs={{0,1},{1,0},{2,3},{3,2},{4,5},{5,4},{6,7},{7,6},{8,9},{9,8},{10,11... | collective-permute-start | bytes 393224 | tf_op jit(solution)/shard_map/ppermute | solution.py:419
  48.1 0.6 copy-start.13
  48.1 0.7 copy-start.3
  48.1 0.8 copy-start.8
  48.2 0.8 copy-start.9
  49.0 15.4 %copy-start = (bf16[16384,64]{0,1:T(8,128)(2,1)S(1)}, bf16[16384,64]{0,1:T(8,128)(2,1)}, u32[]{:S(2)}) copy-start(bf16[16384,64]{0,1:T(8,128)(2,1)} %param.9) | copy-start | bytes 6291460
  63.1 1.3 %copy-start.2 = (s32[16384,4]{0,1:T(4,128)S(1)}, s32[16384,4]{0,1:T(4,128)}, u32[]{:S(2)}) copy-start(s32[16384,4]{0,1:T(4,128)} %param.8) | copy-start | bytes 786436
  63.1 1.3 %copy-start.4 = (s32[4,16384]{1,0:T(4,128)S(1)}, s32[4,16384]{1,0:T(4,128)}, u32[]{:S(2)}) copy-start(s32[4,16384]{1,0:T(4,128)} %copy-done.3) | copy-start | bytes 786436
  63.2 11.3 %collective-permute-start.11 = (f16[64,3072]{1,0:T(8,128)(2,1)S(1)}, f16[64,3072]{1,0:T(8,128)(2,1)S(1)}, u32[]{:S(2)}, u32[]{:S(2)}) collective-permute-start(f16[64,3072]{1,0:T(8,128)(2,1)S(1)} %multiply_convert_fusion.1), channel_id=1, source_target_pairs={{0,2},{1,3},{2,0},{3,1},{4,6},{5,7},{6,4},{7,5},{8,10},{9,11},{10,... | collective-permute-start | bytes 1179656 | tf_op jit(solution)/shard_map/ppermute | solution.py:419
  74.5 16.2 %collective-permute-start.12 = (f16[64,5120]{1,0:T(8,128)(2,1)S(1)}, f16[64,5120]{1,0:T(8,128)(2,1)}, u32[]{:S(2)}, u32[]{:S(2)}) collective-permute-start(f16[64,5120]{1,0:T(8,128)(2,1)S(1)} %multiply_convert_fusion), channel_id=1, source_target_pairs={{0,2},{1,3},{2,0},{3,1},{4,6},{5,7},{6,4},{7,5},{8,10},{9,11},{10,... | collective-permute-start | bytes 1966088 | tf_op jit(solution)/shard_map/ppermute | solution.py:419
  75.8 1.8 %collective-permute-start.13 = (bf16[64,3072]{1,0:T(8,128)(2,1)S(1)}, bf16[64,3072]{1,0:T(8,128)(2,1)S(1)}, u32[]{:S(2)}, u32[]{:S(2)}) collective-permute-start(bf16[64,3072]{1,0:T(8,128)(2,1)S(1)} %fusion.1.refs_0_), channel_id=1, source_target_pairs={{0,1},{1,0},{2,3},{3,2},{4,5},{5,4},{6,7},{7,6},{8,9},{9,8},{10,11... | collective-permute-start | bytes 1179656 | tf_op jit(solution)/shard_map/ppermute | solution.py:419
  92.0 2.2 %collective-permute-start.14 = (bf16[64,5120]{1,0:T(8,128)(2,1)S(1)}, bf16[64,5120]{1,0:T(8,128)(2,1)S(1)}, u32[]{:S(2)}, u32[]{:S(2)}) collective-permute-start(bf16[64,5120]{1,0:T(8,128)(2,1)S(1)} %fusion.refs_0_), channel_id=1, source_target_pairs={{0,1},{1,0},{2,3},{3,2},{4,5},{5,4},{6,7},{7,6},{8,9},{9,8},{10,11... | collective-permute-start | bytes 1966088 | tf_op jit(solution)/shard_map/ppermute | solution.py:419

commit v3 on v2

--- a/solution.py
+++ b/solution.py
@@ -14,7 +14,8 @@
 VMEM_BYTES = 40 << 20
 SMALL_BYTES = 24 << 20
 PULL_ROWS = 1024
-CHUNKS = (3, 5)
+CHUNKS = (4, 4)
+CUTS = ((2, 2), (3, 1))
 F32 = jnp.float32
 BF16 = jnp.bfloat16
 
@@ -186,23 +187,70 @@
     return error + earlier(back - error, 1)
 
 
+def network_kernel(dil_ref, place_ref, w_hbm, bias_hbm, *refs, slabs):
+    basis_hbm, (x_hbm, reg_hbm, x_ref, reg_ref, w_ref, bias_ref, sems) = refs[:slabs], refs[slabs:]
+    cols = basis_hbm[0].shape[1]
+    pairs = [(w_hbm, w_ref), (bias_hbm, bias_ref)]
+    for m in range(slabs):
+        start = pl.multiple_of((place_ref[0] ^ m) * cols, cols)
+        pairs.append((basis_hbm[m], x_ref.at[:, pl.ds(start, cols)]))
+    loads = [
+        pltpu.make_async_copy(source, target, sems.at[i])
+        for i, (source, target) in enumerate(pairs)
+    ]
+    for load in loads:
+        load.start()
+    for load in loads:
+        load.wait()
+    x_store = pltpu.make_async_copy(x_ref, x_hbm, sems.at[slabs + 2])
+    reg_store = pltpu.make_async_copy(reg_ref, reg_hbm, sems.at[slabs + 3])
+    x_store.start()
+    reg_ref[...] = reg_gradient(x_ref[...], dil_ref, w_ref, bias_ref)
+    reg_store.start()
+    x_store.wait()
+    reg_store.wait()
+
+
+def network_start(dilations, place, weights, bias, basis):
+    slabs = len(basis)
+    rank, cols = basis[0].shape
+    smem = pl.BlockSpec(memory_space=pltpu.SMEM)
+    hbm = pl.BlockSpec(memory_space=pltpu.HBM)
+    whole = (rank, slabs * cols)
+    return pl.pallas_call(
+        functools.partial(network_kernel, slabs=slabs),
+        in_specs=[smem, smem] + [hbm] * (2 + slabs),
+        out_specs=[hbm, hbm],
+        out_shape=[pltpu.HBM(whole, F32), pltpu.HBM(whole, F32)],
+        scratch_shapes=[
+            pltpu.VMEM(whole, F32),
+            pltpu.VMEM(whole, F32),
+            pltpu.VMEM(weights.shape, F32),
+            pltpu.VMEM(bias.shape, F32),
+            pltpu.SemaphoreType.DMA((slabs + 4,)),
+        ],
+        compiler_params=pltpu.CompilerParams(vmem_limit_bytes=16 << 20),
+        cost_estimate=kernel_cost(3e-6),
+        name="network_start",
+    )(dilations, place, *[in_hbm(x) for x in (weights, bias, *basis)])
+
+
 def steps_kernel(
     dil_ref, place_ref, w_hbm, bias_hbm, *refs, slabs, data_scale, entries, series
 ):
-    sums_hbm, basis_hbm = refs[:slabs], refs[slabs : 2 * slabs]
-    own_hbm, sib_hbm, fac_hbm, own_flg_hbm, sib_flg_hbm = refs[2 * slabs : 2 * slabs + 5]
-    basis_out, own_b_out, sib_b_out, pull_ref = refs[2 * slabs + 5 : 2 * slabs + 9]
-    x_ref, xb_ref, data_ref, sums_ref, w_ref, bias_ref, fac_ref, flg_ref, sems = refs[
-        2 * slabs + 9 : -2
+    sums_hbm, x_hbm, reg_hbm = refs[:slabs], refs[slabs], refs[slabs + 1]
+    own_hbm, sib_hbm, fac_hbm, own_flg_hbm, sib_flg_hbm = refs[slabs + 2 : slabs + 7]
+    basis_out, own_b_out, sib_b_out, pull_ref = refs[slabs + 7 : slabs + 11]
+    x_ref, reg_ref, xb_ref, data_ref, sums_ref, w_ref, bias_ref, fac_ref, flg_ref, sems = refs[
+        slabs + 11 : -2
     ]
     pull_scratch = refs[-2:]
     core = place_ref[0] % 2
     rank, cols = basis_out.shape
     starts = [pl.multiple_of((place_ref[0] ^ m) * cols, cols) for m in range(slabs)]
     mine = pl.ds(pl.multiple_of(core * (fac_hbm.shape[1] // 2), series), series)
-    pairs = [(basis_hbm[m], x_ref.at[:, pl.ds(starts[m], cols)]) for m in range(slabs)]
-    pairs += [(w_hbm, w_ref), (bias_hbm, bias_ref)]
-    pairs += [(sums_hbm[m], sums_ref.at[m]) for m in range(slabs)]
+    pairs = [(x_hbm, x_ref)] + [(sums_hbm[m], sums_ref.at[m]) for m in range(slabs)]
+    pairs += [(reg_hbm, reg_ref), (w_hbm, w_ref), (bias_hbm, bias_ref)]
     late = [
         (fac_hbm.at[:, mine], fac_ref),
         (own_flg_hbm.at[:, mine], flg_ref.at[0]),
@@ -214,12 +262,12 @@
     ]
     for load in loads:
         load.start()
-    copies = pull_copies(core, own_hbm, sib_hbm, pull_scratch, 0, 0, series)
+    tiles = pull_tiles(series, True)
+    copies = pull_copies(core, own_hbm, sib_hbm, pull_scratch, 0, tiles)
     for load in loads[: len(pairs)]:
         load.wait()
 
-    def step(i, carry):
-        reg = reg_gradient(x_ref[...], dil_ref, w_ref, bias_ref)
+    def step():
         xb_ref[...] = x_ref[...].astype(BF16)
         for m in range(slabs):
             for b in range(0, cols // BLK, 2):
@@ -239,12 +287,17 @@
                 )
                 got = got[:rank] + (got[rank : 2 * rank] + got[2 * rank :])
                 data_ref[:, pl.ds(at, 2 * BLK)] = got - sums_ref[m, :, b * BLK : (b + 2) * BLK]
-        grad = data_ref[...] * data_scale + reg
+        grad = data_ref[...] * data_scale + reg_ref[...]
         square = jnp.sum(grad * grad)
         x_ref[...] -= grad * (0.1 * lax.rsqrt(jnp.full((1, 1), square) / entries + 1e-06))
+
+    def body(i, carry):
+        reg_ref[...] = reg_gradient(x_ref[...], dil_ref, w_ref, bias_ref)
+        step()
         return carry
 
-    lax.fori_loop(0, ITERS, step, 0)
+    step()
+    lax.fori_loop(1, ITERS, body, 0)
     basis_out[...] = x_ref[:, pl.ds(starts[0], cols)]
     own_b = x_ref[:, pl.ds(starts[0], cols)].astype(BF16)
     sib_b = x_ref[:, pl.ds(starts[1], cols)].astype(BF16)
@@ -253,20 +306,21 @@
     for load in loads[len(pairs) :]:
         load.wait()
     pull_chunk(
-        0, copies, pull_scratch, fac_ref, flg_ref.at[0], flg_ref.at[1], own_b, sib_b, pull_ref
+        0, tiles, copies, pull_scratch, fac_ref, flg_ref.at[0], flg_ref.at[1], own_b, sib_b,
+        pull_ref,
     )
 
 
 def basis_steps(
-    dilations, place, weights, bias, basis, sums, observed, sibling, fac_t, flags, data_scale,
+    dilations, place, weights, bias, start, sums, observed, sibling, fac_t, flags, data_scale,
     series
 ):
     slabs = len(sums)
-    rank, cols = basis[0].shape
-    total = slabs * cols
+    rank, total = start[0].shape
+    cols = total // slabs
     smem = pl.BlockSpec(memory_space=pltpu.SMEM)
     vmem = pl.BlockSpec(memory_space=pltpu.VMEM)
-    operands = [weights, bias, *sums, *basis, observed, sibling, fac_t, *flags]
+    operands = [weights, bias, *sums, *start, observed, sibling, fac_t, *flags]
     kernel = functools.partial(
         steps_kernel, slabs=slabs, data_scale=data_scale, entries=float(rank * total),
         series=series,
@@ -283,6 +337,7 @@
         ],
         scratch_shapes=[
             pltpu.VMEM((rank, total), F32),
+            pltpu.VMEM((rank, total), F32),
             pltpu.VMEM((rank, total), BF16),
             pltpu.VMEM((rank, total), F32),
             pltpu.VMEM((slabs, *sums[0].shape), F32),
@@ -290,9 +345,9 @@
             pltpu.VMEM(bias.shape, F32),
             pltpu.VMEM((rank, series), BF16),
             pltpu.VMEM((2, flags[0].shape[0], series), jnp.int32),
-            pltpu.SemaphoreType.DMA((2 * slabs + 5,)),
+            pltpu.SemaphoreType.DMA((slabs + 7,)),
         ]
-        + pull_scratch_shapes(cols, series),
+        + pull_scratch_shapes(cols, series, pull_tiles(series, True)),
         compiler_params=pltpu.CompilerParams(vmem_limit_bytes=32 << 20),
         cost_estimate=kernel_cost(8e-6),
         name="basis_steps",
@@ -310,26 +365,34 @@
     return total
 
 
-def pull_scratch_shapes(cols, series):
+def pull_tiles(series, ready):
+    first = series if ready or series <= PULL_ROWS else PULL_ROWS
+    tiles, at = [(0, first)], first
+    while at < series:
+        tiles.append((at, min(3 * PULL_ROWS, series - at)))
+        at += tiles[-1][1]
+    return tiles
+
+
+def pull_scratch_shapes(cols, series, tiles):
     return [
         pltpu.VMEM((2, series, cols), BF16),
-        pltpu.SemaphoreType.DMA((-(-series // PULL_ROWS), 2)),
+        pltpu.SemaphoreType.DMA((len(tiles), 2)),
     ]
 
 
-def pull_copies(core, own_hbm, sib_hbm, scratch, first, sib_first, series):
+def pull_copies(core, own_hbm, sib_hbm, scratch, first, tiles):
     obs_ref, sems = scratch
     base = core * (own_hbm.shape[0] // 2) + first
-    rows = min(series, PULL_ROWS)
     copies = []
-    for i in range(series // rows):
-        here = pl.ds(i * rows, rows)
-        own = pl.ds(pl.multiple_of(base + i * rows, rows), rows)
+    for i, (at, rows) in enumerate(tiles):
+        here = pl.ds(at, rows)
+        own = pl.ds(pl.multiple_of(base + at, PULL_ROWS), rows)
         copies.append(
             [
                 pltpu.make_async_copy(own_hbm.at[own], obs_ref.at[0, here], sems.at[i, 0]),
                 pltpu.make_async_copy(
-                    sib_hbm.at[pl.ds(sib_first + i * rows, rows)], obs_ref.at[1, here], sems.at[i, 1]
+                    sib_hbm.at[pl.ds(first + at, rows)], obs_ref.at[1, here], sems.at[i, 1]
                 ),
             ]
         )
@@ -339,43 +402,43 @@
 
 
 def pull_chunk(
-    base, copies, scratch, fac_ref, own_flg_ref, sib_flg_ref, own_basis, sib_basis, out_ref
+    base, tiles, copies, scratch, fac_ref, own_flg_ref, sib_flg_ref, own_basis, sib_basis, out_ref
 ):
     obs_ref = scratch[0]
-    rows = out_ref.shape[1] // len(copies)
-    for i, pair in enumerate(copies):
-        here = pl.ds(i * rows, rows)
-        own = pl.ds(pl.multiple_of(base + i * rows, rows), rows)
-        fac = fac_ref[:, own]
+    for (first, height), pair in zip(tiles, copies):
         pair[0].wait()
         pair[1].wait()
-        out_ref[:, here] = pull_rows(
-            obs_ref[0, here, :], fac, own_flg_ref[:, own], own_basis
-        ) + pull_rows(obs_ref[1, here, :], fac, sib_flg_ref[:, own], sib_basis)
+        for at in range(first, first + height, 2 * PULL_ROWS):
+            rows = min(2 * PULL_ROWS, first + height - at)
+            here = pl.ds(at, rows)
+            own = pl.ds(pl.multiple_of(base + at, PULL_ROWS), rows)
+            fac = fac_ref[:, own]
+            out_ref[:, here] = pull_rows(
+                obs_ref[0, here, :], fac, own_flg_ref[:, own], own_basis
+            ) + pull_rows(obs_ref[1, here, :], fac, sib_flg_ref[:, own], sib_basis)
 
 
 def pull_kernel(
     core_ref, own_hbm, sib_hbm, fac_ref, own_flg_ref, sib_flg_ref, own_basis_ref, sib_basis_ref,
-    out_ref, *scratch, first, sib_first
+    out_ref, *scratch, first, tiles
 ):
-    copies = pull_copies(
-        core_ref[0], own_hbm, sib_hbm, scratch, first, sib_first, out_ref.shape[1]
-    )
+    copies = pull_copies(core_ref[0], own_hbm, sib_hbm, scratch, first, tiles)
     pull_chunk(
-        core_ref[0] * (fac_ref.shape[1] // 2) + first, copies, scratch, fac_ref, own_flg_ref,
+        core_ref[0] * (fac_ref.shape[1] // 2) + first, tiles, copies, scratch, fac_ref, own_flg_ref,
         sib_flg_ref, own_basis_ref[...], sib_basis_ref[...], out_ref,
     )
 
 
-def factor_pull(core, observed, sibling, fac_t, flags, basis_b, first, sib_first, series):
+def factor_pull(core, observed, sibling, fac_t, flags, basis_b, first, series):
     vmem = pl.BlockSpec(memory_space=pltpu.VMEM)
     hbm = pl.BlockSpec(memory_space=pltpu.HBM)
+    tiles = pull_tiles(series, False)
     return pl.pallas_call(
-        functools.partial(pull_kernel, first=first, sib_first=sib_first),
+        functools.partial(pull_kernel, first=first, tiles=tiles),
         in_specs=[pl.BlockSpec(memory_space=pltpu.SMEM), hbm, hbm] + [vmem] * 5,
         out_specs=vmem,
         out_shape=jax.ShapeDtypeStruct((fac_t.shape[0], series), F32),
-        scratch_shapes=pull_scratch_shapes(observed.shape[1], series),
+        scratch_shapes=pull_scratch_shapes(observed.shape[1], series, tiles),
         compiler_params=pltpu.CompilerParams(vmem_limit_bytes=24 << 20),
         cost_estimate=kernel_cost(2e-6 * series / 1024),
         name="factor_pull",
@@ -419,25 +482,20 @@
     return lax.ppermute(x, axis, [(i, i ^ bit) for i in range(count)])
 
 
-def sum_over(x, axis):
+def sum_over(x, axis, beside):
     count = lax.axis_size(axis)
     if count & (count - 1):
         return lax.psum(x, axis)
     bit = 1
     while bit < count:
-        x = x + swap(x, axis, bit)
+        other = swap(x, axis, bit)
+        if beside:
+            done = beside.pop(0)(x)
+            x = after(x + other, *done)
+        else:
+            x = x + other
         bit *= 2
     return x
-
-
-def gather_over(x, axis):
-    bit = lax.axis_size(axis) // 2
-    pieces, order = [x], [0]
-    while bit:
-        pieces += [swap(p, axis, bit) for p in pieces]
-        order += [m ^ bit for m in order]
-        bit //= 2
-    return [p for _, p in sorted(zip(order, pieces), key=lambda pair: pair[0])]
 
 
 def after(x, *others):
@@ -459,36 +517,69 @@
 
     sums, send = gram(core, observed, fac_t, flg_t, 1024)
     sibling = swap(send, "tm", 1)
-    far = swap(after(basis, sums), "tm", 2)
-    slabs = [basis, swap(basis, "tm", 1), far, swap(far, "tm", 1)]
-    sums = sum_over(sums, "series")
-    flags = (flg_t, swap(flg_t, "tm", 1))
+    slabs = {0: basis}
+
+    def beside_1(now):
+        slabs[2] = swap(after(basis, now), "tm", 2)
+        return [slabs[2]]
+
+    def beside_2(now):
+        return []
+
+    def beside_3(now):
+        slabs[1] = swap(after(basis, now), "tm", 1)
+        slabs[3] = swap(after(slabs[2], now), "tm", 1)
+        slabs["flags"] = swap(after(flg_t, now), "tm", 1)
+        return [slabs[1], slabs[3]]
+
+    beside = [beside_1, beside_2, beside_3]
+    sums = sum_over(sums, "series", beside)
+    for work in beside:
+        work(sums)
+    flags = (flg_t, slabs["flags"])
+    start = network_start(
+        dilations, after(place, sums), tcn_weights, tcn_bias, [slabs[m] for m in range(time_count)]
+    )
+    far = after(swap(sums, "tm", 2), start[1])
+    sums = [sums, swap(sums, "tm", 1), far, swap(far, "tm", 1)]
     new_basis, own_b, sib_b, pull = basis_steps(
-        dilations, place, tcn_weights, tcn_bias, slabs, gather_over(sums, "tm"),
+        dilations, place, tcn_weights, tcn_bias, start, sums,
         observed, sibling, fac_t, flags, data_scale, CHUNKS[0] * unit,
     )
-    sent, arrived, pieces, firsts = [], [], [], [0]
+    sent, arrived, pieces, firsts = [], [], [], []
+    first = 0
     for c, chunk in enumerate(CHUNKS):
-        first, width = firsts[c], chunk * unit
+        width = chunk * unit
         if c > 0:
             own_b = after(own_b, *sent)
             pull = factor_pull(
-                core, observed, sibling, fac_t, flags, (own_b, sib_b), first, first, width
+                core, observed, sibling, fac_t, flags, (own_b, sib_b), first, width
             )
         own = (pull * coef).astype(jnp.float16)
-        sent.append(after(own, *arrived) if arrived else own)
-        arrived.append(swap(sent[-1], "tm", 2))
-        firsts.append(first + width)
+        at = 0
+        for cut in CUTS[c]:
+            piece = own[:, at * unit : (at + cut) * unit]
+            if c > 0:
+                piece = after(piece, arrived[0])
+            sent.append(piece)
+            arrived.append(swap(piece, "tm", 2))
+            firsts.append(first + at * unit)
+            at += cut
+        first += width
+    early = len(CUTS[0])
     for c, (own, got) in enumerate(zip(sent, arrived)):
-        if c == len(sent) - 1:
-            new_factors = put(core, pieces, firsts[:c], None, fac_t.shape)
+        if c < early:
+            got = after(got, *sent[early:])
+        if c == early:
+            new_factors = put(core, pieces, firsts[:early], None, fac_t.shape)
+            pieces = []
+        if c >= early:
             got = after(got, new_factors)
-            pieces = []
         both = own.astype(F32) + got.astype(F32)
         mine = lax.dynamic_slice_in_dim(fac_t, core[0] * half + firsts[c], own.shape[1], 1)
         new = (mine.astype(F32) - both).astype(BF16)
         pieces += [new, swap(new, "tm", 1)]
-    new_factors = put(core, pieces, firsts[-2:-1], new_factors, fac_t.shape)
+    new_factors = put(core, pieces, firsts[early:], new_factors, fac_t.shape)
     return new_basis, new_factors.T
 
 

time: 95.6 us -> 87.6 us (0.916)
  waiting for transfers between devices: 42.9 us -> 30 us
  starting transfers between devices: 13.4 us -> 16 us
    ppermute x15 -> x19, waiting for transfers between devices: 42.9 us -> 30 us  [swap(): return lax.ppermute(x, axis, [(i, i ^ bit) for i in range(count)])]
    ppermute x15 -> x19, starting transfers between devices: 13.4 us -> 16 us  [swap(): return lax.ppermute(x, axis, [(i, i ^ bit) for i in range(count)])]
    pallas_call x1 -> x2, Pallas kernels: 9.04 us -> 11.6 us  [the longest x1 7.19 us: factor_pull(): pl.pallas_call(functools.partial(pull_kernel, first=first, tiles=tiles),...]
    pallas_call x1, Pallas kernels: 14.1 us -> 12.2 us  [basis_steps(): pl.pallas_call(kernel, in_specs=[smem, smem] + [pl.BlockSpec(memory_space...]
    convert_element_type x2 -> x3, other arithmetic: 1.5 us -> 2.41 us  [shards(): new = (mine.astype(F32) - both).astype(BF16)]
  transfers between devices with their start and end apart: 15 -> 19, of which waited for: 9 -> 10; matrix products, arithmetic and copies ran while one was open for 0% -> 4% of each run, Pallas kernels for 10% -> 14%
where the time goes in v3:
time: 87.6 us; the launch traced here: 87.4 us
  Pallas kernels  36.1 us (41%)
  waiting for transfers between devices  30 us (34%)
  starting transfers between devices  16 us (18%)
  other arithmetic  2.66 us (3%)
  local copies, waits for them, and re-layouts  1.55 us (2%)
  between operations  1.12 us (1%)
    ppermute x19, waiting for transfers between devices, swap(): return lax.ppermute(x, axis, [(i, i ^ bit) for i in range(count)])  30 us
    ppermute x19, starting transfers between devices, swap(): return lax.ppermute(x, axis, [(i, i ^ bit) for i in range(count)])  16 us
    pallas_call x1, Pallas kernels, basis_steps(): pl.pallas_call(kernel, in_specs=[smem, smem] + [pl.BlockSpec(memory_space...  12.2 us
    pallas_call x1, Pallas kernels, gram(): pl.pallas_call(functools.partial(gram_kernel, rows=rows), in_specs=[pl.Bl...  10.4 us
    pallas_call x1, Pallas kernels, factor_pull(): pl.pallas_call(functools.partial(pull_kernel, first=first, tiles=tiles),...  7.19 us
    pallas_call x1, Pallas kernels, network_start(): pl.pallas_call(functools.partial(network_kernel, slabs=slabs), in_specs=[...  4.37 us
    convert_element_type x3, other arithmetic, shards(): new = (mine.astype(F32) - both).astype(BF16)  2.41 us
    pallas_call x2, Pallas kernels, put(): pl.pallas_call(functools.partial(put_kernel, places=places), in_specs=[pl...  1.99 us
  transfers between devices with their start and end apart: 19, of which 10 were waited for; matrix products, arithmetic and copies ran while one was open for 4% of the time, Pallas kernels for 14%

profile of v3, /device:TPU:0, one launch (start us, length us, event | category | flops | bytes accessed | tf_op | source)
XLA Modules:
  0.0 87.4 jit_solution(12613285664436800346)
XLA Ops:
  0.7 10.4 %gram.1 = (f32[64,768]{1,0:T(8,128)S(1)}, bf16[8192,512]{1,0:T(8,128)(2,1)}) custom-call(s32[1]{0:T(128)} %bitcast.1.core_ref, bf16[16384,512]{1,0:T(8,128)(2,1)} %own_hbm.1, bf16[64,16384]{1,0:T(8,128)(2,1)} %bitcast.21, s32[4,16384]{1,0:T(4,128)} %bitcast.24), custom_call_target="tpu_custom_call" | custom-call | bytes 29520000 | tf_op jit(solution)/shard_map/gram/pallas_call | solution.py:98
  11.1 0.5 collective-permute-start.9
  11.6 2.6 %collective-permute-start = (f32[64,768]{1,0:T(8,128)S(1)}, f32[64,768]{1,0:T(8,128)S(1)}, u32[]{:S(2)}, u32[]{:S(2)}) collective-permute-start(f32[64,768]{1,0:T(8,128)S(1)} %get-tuple-element.25), channel_id=1, source_target_pairs={{0,4},{4,0},{8,12},{12,8},{16,20},{20,16},{24,28},{28,24},{1,5},{5... | collective-permute-start | bytes 589832 | tf_op jit(solution)/shard_map/ppermute | solution.py:482
  14.2 1.5 %collective-permute-start.1 = (f32[64,512]{1,0:T(8,128)S(1)}, f32[64,512]{1,0:T(8,128)S(1)}, u32[]{:S(2)}, u32[]{:S(2)}) collective-permute-start(f32[64,512]{1,0:T(8,128)S(1)} %copy-done.10), channel_id=1, source_target_pairs={{0,2},{1,3},{2,0},{3,1},{4,6},{5,7},{6,4},{7,5},{8,10},{9,11},{10,... | collective-permute-start | bytes 393224 | tf_op jit(solution)/shard_map/ppermute | solution.py:482
  15.7 4.0 %collective-permute-done = f32[64,768]{1,0:T(8,128)S(1)} collective-permute-done((f32[64,768]{1,0:T(8,128)S(1)}, f32[64,768]{1,0:T(8,128)S(1)}, u32[]{:S(2)}, u32[]{:S(2)}) %collective-permute-start) | collective-permute-done | bytes 196640 | tf_op jit(solution)/shard_map/ppermute | solution.py:482
  19.8 1.9 %collective-permute-start.2 = (f32[64,768]{1,0:T(8,128)S(1)}, f32[64,768]{1,0:T(8,128)S(1)}, u32[]{:S(2)}, u32[]{:S(2)}) collective-permute-start(f32[64,768]{1,0:T(8,128)S(1)} %add.53), channel_id=1, source_target_pairs={{0,8},{4,12},{8,0},{12,4},{16,24},{20,28},{24,16},{28,20},{1,9},{5... | collective-permute-start | bytes 589832 | tf_op jit(solution)/shard_map/ppermute | solution.py:482
  21.6 4.8 %collective-permute-done.2 = f32[64,768]{1,0:T(8,128)S(1)} collective-permute-done((f32[64,768]{1,0:T(8,128)S(1)}, f32[64,768]{1,0:T(8,128)S(1)}, u32[]{:S(2)}, u32[]{:S(2)}) %collective-permute-start.2) | collective-permute-done | bytes 196640 | tf_op jit(solution)/shard_map/ppermute | solution.py:482
  26.5 2.7 %collective-permute-start.3 = (f32[64,768]{1,0:T(8,128)S(1)}, f32[64,768]{1,0:T(8,128)S(1)}, u32[]{:S(2)}, u32[]{:S(2)}) collective-permute-start(f32[64,768]{1,0:T(8,128)S(1)} %add.54), channel_id=1, source_target_pairs={{0,16},{4,20},{8,24},{12,28},{16,0},{20,4},{24,8},{28,12},{1,17},{... | collective-permute-start | bytes 589832 | tf_op jit(solution)/shard_map/ppermute | solution.py:482
  29.2 0.5 collective-permute-start.5
  29.7 7.8 %collective-permute-done.3 = f32[64,768]{1,0:T(8,128)S(1)} collective-permute-done((f32[64,768]{1,0:T(8,128)S(1)}, f32[64,768]{1,0:T(8,128)S(1)}, u32[]{:S(2)}, u32[]{:S(2)}) %collective-permute-start.3) | collective-permute-done | bytes 196640 | tf_op jit(solution)/shard_map/ppermute | solution.py:482
  37.5 1.4 %collective-permute-start.7 = (f32[64,768]{1,0:T(8,128)S(1)}, f32[64,768]{1,0:T(8,128)S(1)}, u32[]{:S(2)}, u32[]{:S(2)}) collective-permute-start(f32[64,768]{1,0:T(8,128)S(1)} %add.55.refs_0_), channel_id=1, source_target_pairs={{0,2},{1,3},{2,0},{3,1},{4,6},{5,7},{6,4},{7,5},{8,10},{9,11},{10,... | collective-permute-start | bytes 589832 | tf_op jit(solution)/shard_map/ppermute | solution.py:482
  38.9 0.5 collective-permute-start.6
  39.4 4.4 %network_start.1 = (f32[64,2048]{1,0:T(8,128)}, f32[64,2048]{1,0:T(8,128)}) custom-call(s32[2]{0:T(128)S(1)} %copy-done.5, s32[1]{0:T(128)} %bitcast.place_ref, f32[4,64,64]{2,1,0:T(8,128)} %w_hbm.3, f32[2,64]{1,0:T(2,128)} %bias_hbm.3, f32[64,512]{1,0:T(8,128)} %refs_0_.1, f32[64,512]{1,0:T(8,128)} %copy-done.12, f32[64,512]{1,0:T(8,128)} %copy-done.11, ...), custom_call_target="tpu_custom_call" | custom-call | bytes 11070000 | tf_op jit(solution)/shard_map/network_start/pallas_call | solution.py:220
  44.0 1.4 %collective-permute-done.8.refs_3_ = f32[64,768]{1,0:T(8,128)S(1)} collective-permute-done((f32[64,768]{1,0:T(8,128)S(1)}, f32[64,768]{1,0:T(8,128)S(1)}, u32[]{:S(2)}, u32[]{:S(2)}) %collective-permute-start.8) | collective-permute-done | bytes 196640 | tf_op jit(solution)/shard_map/ppermute | solution.py:482
  45.4 0.6 copy-done.9
  46.0 12.2 %basis_steps.1 = (f32[64,512]{1,0:T(8,128)}, bf16[64,512]{1,0:T(8,128)(2,1)S(1)}, bf16[64,512]{1,0:T(8,128)(2,1)S(1)}, f32[64,4096]{1,0:T(8,128)S(1)}) custom-call(s32[2]{0:T(128)S(1)} %copy-done.5, s32[1]{0:T(128)} %bitcast.place_ref, f32[4,64,64]{2,1,0:T(8,128)} %w_hbm.3, f32[2,64]{1,0:T(2,128)} %bias_hbm.3, f32[64,768]{1,0:T(8,128)} %copy-done.6, ...), custom_call_target="tpu_custom_call" | custom-call | bytes 29520000 | tf_op jit(solution)/shard_map/basis_steps/pallas_call | solution.py:328
  58.4 0.8 collective-permute-start.11
  59.2 1.3 %collective-permute-start.14 = (f16[64,2048]{1,0:T(8,128)(2,1)S(1)}, f16[64,2048]{1,0:T(8,128)(2,1)S(1)}, u32[]{:S(2)}, u32[]{:S(2)}) collective-permute-start(f16[64,2048]{1,0:T(8,128)(2,1)S(1)} %get-tuple-element.50), channel_id=1, source_target_pairs={{0,2},{1,3},{2,0},{3,1},{4,6},{5,7},{6,4},{7,5},{8,10},{9,11},{10,... | collective-permute-start | bytes 786440 | tf_op jit(solution)/shard_map/ppermute | solution.py:482
  60.5 7.2 %factor_pull.1 = f32[64,4096]{1,0:T(8,128)S(1)} custom-call(s32[1]{0:T(128)} %bitcast.1.core_ref, bf16[16384,512]{1,0:T(8,128)(2,1)} %own_hbm.1, bf16[8192,512]{1,0:T(8,128)(2,1)} %collective-permute-done.9.refs_7_.sib_hbm, bf16[64,16384]{1,0:T(8,128)(2,1)S(1)} %bitcast.23, s32[4,16384]{1,0:T(4,128)S(1)} %bitcast.27, s32[4,16384]{1,0:T(4,128)S(1)} %copy-done.4, ...), custom_call_target="tpu_custom_call" | custom-call | bytes 29520000 | tf_op jit(solution)/shard_map/factor_pull/pallas_call | solution.py:436
  67.9 0.7 slice.19
  68.6 0.8 collective-permute-start.12
  69.3 3.9 %collective-permute-done.14 = f16[64,2048]{1,0:T(8,128)(2,1)S(1)} collective-permute-done((f16[64,2048]{1,0:T(8,128)(2,1)S(1)}, f16[64,2048]{1,0:T(8,128)(2,1)S(1)}, u32[]{:S(2)}, u32[]{:S(2)}) %collective-permute-start.14) | collective-permute-done | bytes 262176 | tf_op jit(solution)/shard_map/ppermute | solution.py:482
  73.6 0.5 collective-permute-start.15
  74.1 0.8 collective-permute-start.17
  75.1 0.4 collective-permute-done.15.refs_3_
  75.5 1.0 %put.2.refs_4_ = bf16[64,16384]{1,0:T(8,128)(2,1)} custom-call(s32[1]{0:T(128)} %bitcast.1.core_ref, bf16[64,2048]{1,0:T(8,128)(2,1)S(1)} %get-tuple-element.49.refs_0_, bf16[64,2048]{1,0:T(8,128)(2,1)S(1)} %collective-permute-done.13.refs_1_, bf16[64,2048]{1,0:T(8,128)(2,1)S(1)} %get-tuple-element.48.refs_2_, ...), custom_call_target="tpu_custom_call" | custom-call | bytes 3690000 | tf_op jit(solution)/shard_map/put/pallas_call | solution.py:465
  76.5 5.3 %collective-permute-done.12 = f16[64,3072]{1,0:T(8,128)(2,1)} collective-permute-done((f16[64,3072]{1,0:T(8,128)(2,1)S(1)}, f16[64,3072]{1,0:T(8,128)(2,1)}, u32[]{:S(2)}, u32[]{:S(2)}) %collective-permute-start.12) | collective-permute-done | bytes 393248 | tf_op jit(solution)/shard_map/ppermute | solution.py:482
  81.8 1.1 %fusion.refs_0_ = bf16[64,3072]{1,0:T(8,128)(2,1)S(1)} fusion(f16[64,3072]{1,0:T(8,128)(2,1)} %collective-permute-done.12, f16[64,3072]{1,0:T(8,128)(2,1)S(1)} %slice.18, bf16[16384,64]{0,1:T(8,128)(2,1)S(1)} %copy-done, s32[]{:T(128)S(6)} %select_n.20), kind=kLoop, calls=%fused_computation.3 | loop fusion | flops 1179648 | bytes 1572868 | tf_op jit(solution)/shard_map/convert_element_type | solution.py:580
  83.0 0.8 collective-permute-done.17
  83.8 1.0 %fusion.3.refs_2_ = bf16[64,1024]{1,0:T(8,128)(2,1)S(1)} fusion(f16[64,1024]{1,0:T(8,128)(2,1)} %collective-permute-done.17, f16[64,1024]{1,0:T(8,128)(2,1)} %slice.19, bf16[16384,64]{0,1:T(8,128)(2,1)S(1)} %copy-done, s32[]{:T(128)S(6)} %select_n.23), kind=kLoop, calls=%fused_computation.9 | loop fusion | flops 393216 | bytes 524292 | tf_op jit(solution)/shard_map/convert_element_type | solution.py:580
  84.9 1.3 %collective-permute-done.18.refs_3_ = bf16[64,1024]{1,0:T(8,128)(2,1)S(1)} collective-permute-done((bf16[64,1024]{1,0:T(8,128)(2,1)S(1)}, bf16[64,1024]{1,0:T(8,128)(2,1)S(1)}, u32[]{:S(2)}, u32[]{:S(2)}) %collective-permute-start.18) | collective-permute-done | bytes 131104 | tf_op jit(solution)/shard_map/ppermute | solution.py:482
  86.2 1.0 %put.3 = bf16[64,16384]{1,0:T(8,128)(2,1)} custom-call(s32[1]{0:T(128)} %bitcast.1.core_ref, bf16[64,3072]{1,0:T(8,128)(2,1)S(1)} %fusion.refs_0_, bf16[64,3072]{1,0:T(8,128)(2,1)S(1)} %collective-permute-done.16.refs_1_, bf16[64,1024]{1,0:T(8,128)(2,1)S(1)} %fusion.3.refs_2_, ...), custom_call_target="tpu_custom_call", output_to_operand_aliasing={{}: (5, {})} | custom-call | bytes 3690000 | tf_op jit(solution)/shard_map/put/pallas_call | solution.py:465
  (51 shorter events, 1.4 us)
Async XLA Ops:
  0.6 13.5 %copy-start.10 = (f32[64,512]{1,0:T(8,128)S(1)}, f32[64,512]{1,0:T(8,128)}, u32[]{:S(2)}) copy-start(f32[64,512]{1,0:T(8,128)} %refs_0_.1) | copy-start | bytes 393220
  0.7 38.3 %copy-start.1 = (s32[16384,4]{0,1:T(4,128)S(1)}, s32[16384,4]{0,1:T(4,128)}, u32[]{:S(2)}) copy-start(s32[16384,4]{0,1:T(4,128)} %param.8) | copy-start | bytes 786436
  0.7 38.8 %copy-start.5 = (s32[2]{0:T(128)S(1)}, s32[2]{0:T(128)}, u32[]{:S(2)}) copy-start(s32[2]{0:T(128)} %dil_ref.3) | copy-start | bytes 28
  11.1 34.3 %collective-permute-start.9 = (bf16[8192,512]{1,0:T(8,128)(2,1)}, bf16[8192,512]{1,0:T(8,128)(2,1)}, u32[]{:S(2)}, u32[]{:S(2)}) collective-permute-start(bf16[8192,512]{1,0:T(8,128)(2,1)} %get-tuple-element.35), channel_id=1, source_target_pairs={{0,1},{1,0},{2,3},{3,2},{4,5},{5,4},{6,7},{7,6},{8,9},{9,8},{10,11... | collective-permute-start | bytes 25165832 | tf_op jit(solution)/shard_map/ppermute | solution.py:482
  11.6 8.1 %collective-permute-start = (f32[64,768]{1,0:T(8,128)S(1)}, f32[64,768]{1,0:T(8,128)S(1)}, u32[]{:S(2)}, u32[]{:S(2)}) collective-permute-start(f32[64,768]{1,0:T(8,128)S(1)} %get-tuple-element.25), channel_id=1, source_target_pairs={{0,4},{4,0},{8,12},{12,8},{16,20},{20,16},{24,28},{28,24},{1,5},{5... | collective-permute-start | bytes 589832 | tf_op jit(solution)/shard_map/ppermute | solution.py:482
  14.2 5.6 %collective-permute-start.1 = (f32[64,512]{1,0:T(8,128)S(1)}, f32[64,512]{1,0:T(8,128)S(1)}, u32[]{:S(2)}, u32[]{:S(2)}) collective-permute-start(f32[64,512]{1,0:T(8,128)S(1)} %copy-done.10), channel_id=1, source_target_pairs={{0,2},{1,3},{2,0},{3,1},{4,6},{5,7},{6,4},{7,5},{8,10},{9,11},{10,... | collective-permute-start | bytes 393224 | tf_op jit(solution)/shard_map/ppermute | solution.py:482
  19.7 19.7 %copy-start.11 = (f32[64,512]{1,0:T(8,128)}, f32[64,512]{1,0:T(8,128)S(1)}, u32[]{:S(2)}) copy-start(f32[64,512]{1,0:T(8,128)S(1)} %collective-permute-done.1.refs_2_) | copy-start | bytes 393220
  19.8 6.7 %collective-permute-start.2 = (f32[64,768]{1,0:T(8,128)S(1)}, f32[64,768]{1,0:T(8,128)S(1)}, u32[]{:S(2)}, u32[]{:S(2)}) collective-permute-start(f32[64,768]{1,0:T(8,128)S(1)} %add.53), channel_id=1, source_target_pairs={{0,8},{4,12},{8,0},{12,4},{16,24},{20,28},{24,16},{28,20},{1,9},{5... | collective-permute-start | bytes 589832 | tf_op jit(solution)/shard_map/ppermute | solution.py:482
  26.5 11.0 %collective-permute-start.3 = (f32[64,768]{1,0:T(8,128)S(1)}, f32[64,768]{1,0:T(8,128)S(1)}, u32[]{:S(2)}, u32[]{:S(2)}) collective-permute-start(f32[64,768]{1,0:T(8,128)S(1)} %add.54), channel_id=1, source_target_pairs={{0,16},{4,20},{8,24},{12,28},{16,0},{20,4},{24,8},{28,12},{1,17},{... | collective-permute-start | bytes 589832 | tf_op jit(solution)/shard_map/ppermute | solution.py:482
  29.2 8.3 %collective-permute-start.4 = (f32[64,512]{1,0:T(8,128)S(1)}, f32[64,512]{1,0:T(8,128)S(1)}, u32[]{:S(2)}, u32[]{:S(2)}) collective-permute-start(f32[64,512]{1,0:T(8,128)S(1)} %copy-done.10), channel_id=1, source_target_pairs={{0,1},{1,0},{2,3},{3,2},{4,5},{5,4},{6,7},{7,6},{8,9},{9,8},{10,11... | collective-permute-start | bytes 393224 | tf_op jit(solution)/shard_map/ppermute | solution.py:482
  29.2 8.3 %collective-permute-start.5 = (f32[64,512]{1,0:T(8,128)S(1)}, f32[64,512]{1,0:T(8,128)S(1)}, u32[]{:S(2)}, u32[]{:S(2)}) collective-permute-start(f32[64,512]{1,0:T(8,128)S(1)} %collective-permute-done.1.refs_2_), channel_id=1, source_target_pairs={{0,1},{1,0},{2,3},{3,2},{4,5},{5,4},{6,7},{7,6},{8,9},{9,8},{10,11... | collective-permute-start | bytes 393224 | tf_op jit(solution)/shard_map/ppermute | solution.py:482
  37.5 7.9 %copy-start.6 = (f32[64,768]{1,0:T(8,128)}, f32[64,768]{1,0:T(8,128)S(1)}, u32[]{:S(2)}) copy-start(f32[64,768]{1,0:T(8,128)S(1)} %add.55.refs_0_) | copy-start | bytes 589828
  37.5 1.9 %copy-start.12 = (f32[64,512]{1,0:T(8,128)}, f32[64,512]{1,0:T(8,128)S(1)}, u32[]{:S(2)}) copy-start(f32[64,512]{1,0:T(8,128)S(1)} %collective-permute-done.4.refs_1_) | copy-start | bytes 393220
  37.5 1.9 %copy-start.13 = (f32[64,512]{1,0:T(8,128)}, f32[64,512]{1,0:T(8,128)S(1)}, u32[]{:S(2)}) copy-start(f32[64,512]{1,0:T(8,128)S(1)} %collective-permute-done.5.refs_3_) | copy-start | bytes 393220
  37.5 6.3 %collective-permute-start.7 = (f32[64,768]{1,0:T(8,128)S(1)}, f32[64,768]{1,0:T(8,128)S(1)}, u32[]{:S(2)}, u32[]{:S(2)}) collective-permute-start(f32[64,768]{1,0:T(8,128)S(1)} %add.55.refs_0_), channel_id=1, source_target_pairs={{0,2},{1,3},{2,0},{3,1},{4,6},{5,7},{6,4},{7,5},{8,10},{9,11},{10,... | collective-permute-start | bytes 589832 | tf_op jit(solution)/shard_map/ppermute | solution.py:482
  38.9 5.0 %collective-permute-start.10 = (s32[4,16384]{1,0:T(4,128)S(1)}, s32[4,16384]{1,0:T(4,128)S(1)}, u32[]{:S(2)}, u32[]{:S(2)}) collective-permute-start(s32[4,16384]{1,0:T(4,128)S(1)} %bitcast.26), channel_id=1, source_target_pairs={{0,1},{1,0},{2,3},{3,2},{4,5},{5,4},{6,7},{7,6},{8,9},{9,8},{10,11... | collective-permute-start | bytes 786440 | tf_op jit(solution)/shard_map/ppermute | solution.py:482
  38.9 5.0 %collective-permute-start.6 = (f32[64,768]{1,0:T(8,128)S(1)}, f32[64,768]{1,0:T(8,128)S(1)}, u32[]{:S(2)}, u32[]{:S(2)}) collective-permute-start(f32[64,768]{1,0:T(8,128)S(1)} %add.55.refs_0_), channel_id=1, source_target_pairs={{0,1},{1,0},{2,3},{3,2},{4,5},{5,4},{6,7},{7,6},{8,9},{9,8},{10,11... | collective-permute-start | bytes 589832 | tf_op jit(solution)/shard_map/ppermute | solution.py:482
  43.8 1.5 %copy-start.7 = (f32[64,768]{1,0:T(8,128)}, f32[64,768]{1,0:T(8,128)S(1)}, u32[]{:S(2)}) copy-start(f32[64,768]{1,0:T(8,128)S(1)} %collective-permute-done.7.refs_2_) | copy-start | bytes 589828
  43.8 1.5 %collective-permute-start.8 = (f32[64,768]{1,0:T(8,128)S(1)}, f32[64,768]{1,0:T(8,128)S(1)}, u32[]{:S(2)}, u32[]{:S(2)}) collective-permute-start(f32[64,768]{1,0:T(8,128)S(1)} %collective-permute-done.7.refs_2_), channel_id=1, source_target_pairs={{0,1},{1,0},{2,3},{3,2},{4,5},{5,4},{6,7},{7,6},{8,9},{9,8},{10,11... | collective-permute-start | bytes 589832 | tf_op jit(solution)/shard_map/ppermute | solution.py:482
  43.9 1.4 %copy-start.3 = (s32[4,16384]{1,0:T(4,128)}, s32[4,16384]{1,0:T(4,128)S(1)}, u32[]{:S(2)}) copy-start(s32[4,16384]{1,0:T(4,128)S(1)} %collective-permute-done.10.refs_10_.sib_flg_ref) | copy-start | bytes 786436
  43.9 1.4 %copy-start.8 = (f32[64,768]{1,0:T(8,128)}, f32[64,768]{1,0:T(8,128)S(1)}, u32[]{:S(2)}) copy-start(f32[64,768]{1,0:T(8,128)S(1)} %collective-permute-done.6.refs_1_) | copy-start | bytes 589828
  58.2 2.4 %copy-start = (bf16[16384,64]{0,1:T(8,128)(2,1)S(1)}, bf16[16384,64]{0,1:T(8,128)(2,1)}, u32[]{:S(2)}) copy-start(bf16[16384,64]{0,1:T(8,128)(2,1)} %param.9) | copy-start | bytes 6291460
  58.2 2.3 %copy-start.2 = (s32[16384,4]{0,1:T(4,128)S(1)}, s32[16384,4]{0,1:T(4,128)}, u32[]{:S(2)}) copy-start(s32[16384,4]{0,1:T(4,128)} %param.8) | copy-start | bytes 786436
  58.2 2.3 %copy-start.4 = (s32[4,16384]{1,0:T(4,128)S(1)}, s32[4,16384]{1,0:T(4,128)}, u32[]{:S(2)}) copy-start(s32[4,16384]{1,0:T(4,128)} %copy-done.3) | copy-start | bytes 786436
  58.4 10.2 %collective-permute-start.11 = (f16[64,2048]{1,0:T(8,128)(2,1)S(1)}, f16[64,2048]{1,0:T(8,128)(2,1)S(1)}, u32[]{:S(2)}, u32[]{:S(2)}) collective-permute-start(f16[64,2048]{1,0:T(8,128)(2,1)S(1)} %get-tuple-element.51), channel_id=1, source_target_pairs={{0,2},{1,3},{2,0},{3,1},{4,6},{5,7},{6,4},{7,5},{8,10},{9,11},{10,... | collective-permute-start | bytes 786440 | tf_op jit(solution)/shard_map/ppermute | solution.py:482
  59.2 14.0 %collective-permute-start.14 = (f16[64,2048]{1,0:T(8,128)(2,1)S(1)}, f16[64,2048]{1,0:T(8,128)(2,1)S(1)}, u32[]{:S(2)}, u32[]{:S(2)}) collective-permute-start(f16[64,2048]{1,0:T(8,128)(2,1)S(1)} %get-tuple-element.50), channel_id=1, source_target_pairs={{0,2},{1,3},{2,0},{3,1},{4,6},{5,7},{6,4},{7,5},{8,10},{9,11},{10,... | collective-permute-start | bytes 786440 | tf_op jit(solution)/shard_map/ppermute | solution.py:482
  68.6 13.2 %collective-permute-start.12 = (f16[64,3072]{1,0:T(8,128)(2,1)S(1)}, f16[64,3072]{1,0:T(8,128)(2,1)}, u32[]{:S(2)}, u32[]{:S(2)}) collective-permute-start(f16[64,3072]{1,0:T(8,128)(2,1)S(1)} %slice.18), channel_id=1, source_target_pairs={{0,2},{1,3},{2,0},{3,1},{4,6},{5,7},{6,4},{7,5},{8,10},{9,11},{10,... | collective-permute-start | bytes 1179656 | tf_op jit(solution)/shard_map/ppermute | solution.py:482
  73.5 1.6 %collective-permute-start.13 = (bf16[64,2048]{1,0:T(8,128)(2,1)S(1)}, bf16[64,2048]{1,0:T(8,128)(2,1)S(1)}, u32[]{:S(2)}, u32[]{:S(2)}) collective-permute-start(bf16[64,2048]{1,0:T(8,128)(2,1)S(1)} %get-tuple-element.49.refs_0_), channel_id=1, source_target_pairs={{0,1},{1,0},{2,3},{3,2},{4,5},{5,4},{6,7},{7,6},{8,9},{9,8},{10,11... | collective-permute-start | bytes 786440 | tf_op jit(solution)/shard_map/ppermute | solution.py:482
  73.6 1.9 %collective-permute-start.15 = (bf16[64,2048]{1,0:T(8,128)(2,1)S(1)}, bf16[64,2048]{1,0:T(8,128)(2,1)S(1)}, u32[]{:S(2)}, u32[]{:S(2)}) collective-permute-start(bf16[64,2048]{1,0:T(8,128)(2,1)S(1)} %get-tuple-element.48.refs_2_), channel_id=1, source_target_pairs={{0,1},{1,0},{2,3},{3,2},{4,5},{5,4},{6,7},{7,6},{8,9},{9,8},{10,11... | collective-permute-start | bytes 786440 | tf_op jit(solution)/shard_map/ppermute | solution.py:482
  74.1 9.7 %collective-permute-start.17 = (f16[64,1024]{1,0:T(8,128)(2,1)}, f16[64,1024]{1,0:T(8,128)(2,1)}, u32[]{:S(2)}, u32[]{:S(2)}) collective-permute-start(f16[64,1024]{1,0:T(8,128)(2,1)} %slice.19), channel_id=1, source_target_pairs={{0,2},{1,3},{2,0},{3,1},{4,6},{5,7},{6,4},{7,5},{8,10},{9,11},{10,... | collective-permute-start | bytes 393224 | tf_op jit(solution)/shard_map/ppermute | solution.py:482
  82.9 3.3 %collective-permute-start.16 = (bf16[64,3072]{1,0:T(8,128)(2,1)S(1)}, bf16[64,3072]{1,0:T(8,128)(2,1)S(1)}, u32[]{:S(2)}, u32[]{:S(2)}) collective-permute-start(bf16[64,3072]{1,0:T(8,128)(2,1)S(1)} %fusion.refs_0_), channel_id=1, source_target_pairs={{0,1},{1,0},{2,3},{3,2},{4,5},{5,4},{6,7},{7,6},{8,9},{9,8},{10,11... | collective-permute-start | bytes 1179656 | tf_op jit(solution)/shard_map/ppermute | solution.py:482
  84.8 1.4 %collective-permute-start.18 = (bf16[64,1024]{1,0:T(8,128)(2,1)S(1)}, bf16[64,1024]{1,0:T(8,128)(2,1)S(1)}, u32[]{:S(2)}, u32[]{:S(2)}) collective-permute-start(bf16[64,1024]{1,0:T(8,128)(2,1)S(1)} %fusion.3.refs_2_), channel_id=1, source_target_pairs={{0,1},{1,0},{2,3},{3,2},{4,5},{5,4},{6,7},{7,6},{8,9},{9,8},{10,11... | collective-permute-start | bytes 393224 | tf_op jit(solution)/shard_map/ppermute | solution.py:482
  (1 other events, 0.7 us)

commit v4 on v3

--- a/solution.py
+++ b/solution.py
@@ -33,41 +33,36 @@
 
 
 def gram_kernel(
-    core_ref, obs_hbm, fac_hbm, flg_hbm, out_ref, send_hbm, obs_ref, fac_ref, flg_ref, sems,
-    send_sems, *, rows
+    obs_hbm, fac_hbm, flg_hbm, out_ref, obs_ref, fac_ref, flg_ref, sems, *, rows
 ):
     series = obs_ref.shape[0]
-    half = send_hbm.shape[0]
     rank, blocks = fac_ref.shape[0], flg_ref.shape[0]
     flg_copy = pltpu.make_async_copy(flg_hbm, flg_ref, sems.at[0])
-    fac_copy = pltpu.make_async_copy(fac_hbm, fac_ref, sems.at[1])
     flg_copy.start()
-    fac_copy.start()
-    first = (1 - core_ref[0]) * half
-    cuts, copies, sends = [], [], []
-    for i in range(series // rows):
-        at = i * rows
-        at = first + at if at < half else half - first + (at - half)
-        cuts.append(pl.ds(pl.multiple_of(at, rows), rows))
-        copies.append(
-            pltpu.make_async_copy(obs_hbm.at[cuts[i]], obs_ref.at[cuts[i]], sems.at[2 + i])
-        )
+    steps = series // rows
+    fac_copies, copies = [], []
+    for i in range(steps):
+        if i % (steps // 2) == 0:
+            cut = pl.ds(i * rows, series // 2)
+            fac_copies.append(
+                pltpu.make_async_copy(
+                    fac_hbm.at[:, cut], fac_ref.at[:, cut], sems.at[1 + len(fac_copies)]
+                )
+            )
+            fac_copies[-1].start()
+        cut = pl.ds(i * rows, rows)
+        copies.append(pltpu.make_async_copy(obs_hbm.at[cut], obs_ref.at[cut], sems.at[3 + i]))
         copies[i].start()
     flg_copy.wait()
-    fac_copy.wait()
-    for i, (cut, copy) in enumerate(zip(cuts, copies)):
+    for i, copy in enumerate(copies):
+        if i % (steps // 2) == 0:
+            fac_copies[i // (steps // 2)].wait()
+        cut = pl.ds(i * rows, rows)
         fac = fac_ref[:, cut]
         flg = flg_ref[:, cut].astype(F32).astype(BF16)
         masked = jnp.concatenate([fac * flg[b : b + 1, :] for b in range(blocks)], axis=0)
         gram_part = nt_dot(fac, masked)
         copy.wait()
-        if i * rows < half:
-            sends.append(
-                pltpu.make_async_copy(
-                    obs_ref.at[cut], send_hbm.at[pl.ds(i * rows, rows)], send_sems.at[i]
-                )
-            )
-            sends[i].start()
         parts = []
         for b in range(0, blocks, 2):
             both = jnp.dot(
@@ -81,39 +76,68 @@
             out_ref[...] = new
         else:
             out_ref[...] += new
-    for send in sends:
-        send.wait()
+
+
+def part_kernel(core_ref, obs_hbm, out_hbm, part_ref, sems, *, first, pieces):
+    rows = out_hbm.shape[0] // pieces
+    base = (1 - core_ref[0]) * (obs_hbm.shape[0] // 2) + first
+    loads, stores = [], []
+    for i in range(pieces):
+        here = pl.ds(i * rows, rows)
+        there = pl.ds(pl.multiple_of(base + i * rows, rows), rows)
+        loads.append(pltpu.make_async_copy(obs_hbm.at[there], part_ref.at[here], sems.at[i, 0]))
+        stores.append(pltpu.make_async_copy(part_ref.at[here], out_hbm.at[here], sems.at[i, 1]))
+    for load in loads:
+        load.start()
+    for load, store in zip(loads, stores):
+        load.wait()
+        store.start()
+    for store in stores:
+        store.wait()
+
+
+def other_part(core, observed, first, rows):
+    hbm = pl.BlockSpec(memory_space=pltpu.HBM)
+    pieces = 8
+    return pl.pallas_call(
+        functools.partial(part_kernel, first=first, pieces=pieces),
+        in_specs=[pl.BlockSpec(memory_space=pltpu.SMEM), hbm],
+        out_specs=hbm,
+        out_shape=pltpu.HBM((rows, observed.shape[1]), observed.dtype),
+        scratch_shapes=[
+            pltpu.VMEM((rows, observed.shape[1]), observed.dtype),
+            pltpu.SemaphoreType.DMA((pieces, 2)),
+        ],
+        compiler_params=pltpu.CompilerParams(vmem_limit_bytes=16 << 20),
+        cost_estimate=kernel_cost(3e-6),
+        name="other_part",
+    )(core, in_hbm(observed))
 
 
 def in_hbm(x):
     return pltpu.with_memory_space_constraint(x, pltpu.HBM)
 
 
-def gram(core, observed, fac_t, flg_t, rows):
+def gram(observed, fac_t, flg_t, rows):
     series, cols = observed.shape
     rank, blocks = fac_t.shape[0], flg_t.shape[0]
     width = cols + blocks * rank
-    half = series // 2
     hbm = pl.BlockSpec(memory_space=pltpu.HBM)
     return pl.pallas_call(
         functools.partial(gram_kernel, rows=rows),
-        in_specs=[pl.BlockSpec(memory_space=pltpu.SMEM), hbm, hbm, hbm],
-        out_specs=[pl.BlockSpec(memory_space=pltpu.VMEM), hbm],
-        out_shape=[
-            jax.ShapeDtypeStruct((rank, width), F32),
-            pltpu.HBM((half, cols), BF16),
-        ],
+        in_specs=[hbm, hbm, hbm],
+        out_specs=pl.BlockSpec(memory_space=pltpu.VMEM),
+        out_shape=jax.ShapeDtypeStruct((rank, width), F32),
         scratch_shapes=[
             pltpu.VMEM((series, cols), BF16),
             pltpu.VMEM(fac_t.shape, BF16),
             pltpu.VMEM(flg_t.shape, jnp.int32),
-            pltpu.SemaphoreType.DMA((2 + series // rows,)),
-            pltpu.SemaphoreType.DMA((half // rows,)),
+            pltpu.SemaphoreType.DMA((3 + series // rows,)),
         ],
         compiler_params=pltpu.CompilerParams(vmem_limit_bytes=32 << 20),
         cost_estimate=kernel_cost(8e-6),
         name="gram",
-    )(core, in_hbm(observed), in_hbm(fac_t), in_hbm(flg_t))
+    )(in_hbm(observed), in_hbm(fac_t), in_hbm(flg_t))
 
 
 def split(x):
@@ -236,20 +260,19 @@
 
 
 def steps_kernel(
-    dil_ref, place_ref, w_hbm, bias_hbm, *refs, slabs, data_scale, entries, series
+    dil_ref, place_ref, last_ref, w_hbm, bias_hbm, *refs, slabs, data_scale, entries, series
 ):
-    sums_hbm, x_hbm, reg_hbm = refs[:slabs], refs[slabs], refs[slabs + 1]
-    own_hbm, sib_hbm, fac_hbm, own_flg_hbm, sib_flg_hbm = refs[slabs + 2 : slabs + 7]
-    basis_out, own_b_out, sib_b_out, pull_ref = refs[slabs + 7 : slabs + 11]
-    x_ref, reg_ref, xb_ref, data_ref, sums_ref, w_ref, bias_ref, fac_ref, flg_ref, sems = refs[
-        slabs + 11 : -2
-    ]
+    sums_hbm, refs = refs[: slabs - 1], refs[slabs - 1 :]
+    x_hbm, reg_hbm, own_hbm, sib_hbm, fac_hbm, own_flg_hbm, sib_flg_hbm = refs[:7]
+    basis_out, own_b_out, sib_b_out, pull_ref = refs[7:11]
+    x_ref, reg_ref, xb_ref, data_ref, sums_ref, w_ref, bias_ref, fac_ref, flg_ref, sems = refs[11:-2]
+    sums = [sums_ref.at[m] for m in range(slabs - 1)] + [last_ref]
     pull_scratch = refs[-2:]
     core = place_ref[0] % 2
     rank, cols = basis_out.shape
     starts = [pl.multiple_of((place_ref[0] ^ m) * cols, cols) for m in range(slabs)]
     mine = pl.ds(pl.multiple_of(core * (fac_hbm.shape[1] // 2), series), series)
-    pairs = [(x_hbm, x_ref)] + [(sums_hbm[m], sums_ref.at[m]) for m in range(slabs)]
+    pairs = [(x_hbm, x_ref)] + list(zip(sums_hbm, sums))
     pairs += [(reg_hbm, reg_ref), (w_hbm, w_ref), (bias_hbm, bias_ref)]
     late = [
         (fac_hbm.at[:, mine], fac_ref),
@@ -271,7 +294,7 @@
         xb_ref[...] = x_ref[...].astype(BF16)
         for m in range(slabs):
             for b in range(0, cols // BLK, 2):
-                high, mid, low = split3(sums_ref[m, :, cols + b * rank : cols + (b + 2) * rank])
+                high, mid, low = split3(sums[m][:, cols + b * rank : cols + (b + 2) * rank])
                 at = pl.multiple_of(starts[m] + b * BLK, 2 * BLK)
                 xb = xb_ref[:, pl.ds(at, 2 * BLK)]
                 zero = jnp.zeros((rank, BLK), BF16)
@@ -286,7 +309,7 @@
                     jnp.concatenate([high, mid, low], axis=0), right, preferred_element_type=F32
                 )
                 got = got[:rank] + (got[rank : 2 * rank] + got[2 * rank :])
-                data_ref[:, pl.ds(at, 2 * BLK)] = got - sums_ref[m, :, b * BLK : (b + 2) * BLK]
+                data_ref[:, pl.ds(at, 2 * BLK)] = got - sums[m][:, b * BLK : (b + 2) * BLK]
         grad = data_ref[...] * data_scale + reg_ref[...]
         square = jnp.sum(grad * grad)
         x_ref[...] -= grad * (0.1 * lax.rsqrt(jnp.full((1, 1), square) / entries + 1e-06))
@@ -320,14 +343,14 @@
     cols = total // slabs
     smem = pl.BlockSpec(memory_space=pltpu.SMEM)
     vmem = pl.BlockSpec(memory_space=pltpu.VMEM)
-    operands = [weights, bias, *sums, *start, observed, sibling, fac_t, *flags]
+    operands = [weights, bias, *sums[:-1], *start, observed, sibling, fac_t, *flags]
     kernel = functools.partial(
         steps_kernel, slabs=slabs, data_scale=data_scale, entries=float(rank * total),
         series=series,
     )
     return pl.pallas_call(
         kernel,
-        in_specs=[smem, smem] + [pl.BlockSpec(memory_space=pltpu.HBM)] * len(operands),
+        in_specs=[smem, smem, vmem] + [pl.BlockSpec(memory_space=pltpu.HBM)] * len(operands),
         out_specs=[vmem] * 4,
         out_shape=[
             jax.ShapeDtypeStruct((rank, cols), F32),
@@ -340,7 +363,7 @@
             pltpu.VMEM((rank, total), F32),
             pltpu.VMEM((rank, total), BF16),
             pltpu.VMEM((rank, total), F32),
-            pltpu.VMEM((slabs, *sums[0].shape), F32),
+            pltpu.VMEM((slabs - 1, *sums[0].shape), F32),
             pltpu.VMEM(weights.shape, F32),
             pltpu.VMEM(bias.shape, F32),
             pltpu.VMEM((rank, series), BF16),
@@ -351,7 +374,10 @@
         compiler_params=pltpu.CompilerParams(vmem_limit_bytes=32 << 20),
         cost_estimate=kernel_cost(8e-6),
         name="basis_steps",
-    )(dilations, place, *[in_hbm(x) for x in operands])
+    )(
+        dilations, place, pltpu.with_memory_space_constraint(sums[-1], pltpu.VMEM),
+        *[in_hbm(x) for x in operands],
+    )
 
 
 def pull_rows(obs, fac, flg, basis):
@@ -392,7 +418,7 @@
             [
                 pltpu.make_async_copy(own_hbm.at[own], obs_ref.at[0, here], sems.at[i, 0]),
                 pltpu.make_async_copy(
-                    sib_hbm.at[pl.ds(first + at, rows)], obs_ref.at[1, here], sems.at[i, 1]
+                    sib_hbm.at[here], obs_ref.at[1, here], sems.at[i, 1]
                 ),
             ]
         )
@@ -515,25 +541,29 @@
     place = place.astype(jnp.int32).reshape(1)
     unit = half // sum(CHUNKS)
 
-    sums, send = gram(core, observed, fac_t, flg_t, 1024)
-    sibling = swap(send, "tm", 1)
-    slabs = {0: basis}
+    slabs, parts, siblings = {0: basis}, [], []
 
     def beside_1(now):
+        parts.append(other_part(after(core, now), observed, 0, CHUNKS[0] * unit))
+        return parts[:]
+
+    def beside_2(now):
+        siblings.append(swap(after(parts[0], now), "tm", 1))
         slabs[2] = swap(after(basis, now), "tm", 2)
-        return [slabs[2]]
-
-    def beside_2(now):
-        return []
+        parts.append(
+            other_part(after(core, now), observed, CHUNKS[0] * unit, CHUNKS[1] * unit)
+        )
+        return [slabs[2], parts[1]]
 
     def beside_3(now):
+        siblings.append(swap(after(parts[1], now), "tm", 1))
         slabs[1] = swap(after(basis, now), "tm", 1)
         slabs[3] = swap(after(slabs[2], now), "tm", 1)
         slabs["flags"] = swap(after(flg_t, now), "tm", 1)
         return [slabs[1], slabs[3]]
 
     beside = [beside_1, beside_2, beside_3]
-    sums = sum_over(sums, "series", beside)
+    sums = sum_over(gram(observed, fac_t, flg_t, 1024), "series", beside)
     for work in beside:
         work(sums)
     flags = (flg_t, slabs["flags"])
@@ -544,7 +574,7 @@
     sums = [sums, swap(sums, "tm", 1), far, swap(far, "tm", 1)]
     new_basis, own_b, sib_b, pull = basis_steps(
         dilations, place, tcn_weights, tcn_bias, start, sums,
-        observed, sibling, fac_t, flags, data_scale, CHUNKS[0] * unit,
+        observed, siblings[0], fac_t, flags, data_scale, CHUNKS[0] * unit,
     )
     sent, arrived, pieces, firsts = [], [], [], []
     first = 0
@@ -553,7 +583,7 @@
         if c > 0:
             own_b = after(own_b, *sent)
             pull = factor_pull(
-                core, observed, sibling, fac_t, flags, (own_b, sib_b), first, width
+                core, observed, siblings[1], fac_t, flags, (own_b, sib_b), first, width
             )
         own = (pull * coef).astype(jnp.float16)
         at = 0

time: 87.6 us -> 85.9 us (0.981)
  waiting for transfers between devices: 30 us -> 23 us
  Pallas kernels: 36.1 us -> 40.3 us
  starting transfers between devices: 16 us -> 17.7 us
    ppermute x19 -> x20, waiting for transfers between devices: 30 us -> 23 us  [swap(): return lax.ppermute(x, axis, [(i, i ^ bit) for i in range(count)])]
    pallas_call x2 -> x4, Pallas kernels: 22.5 us -> 26.7 us  [the longest x1 12.1 us: basis_steps(): pl.pallas_call(kernel, in_specs=[smem, smem, vmem] + [pl.BlockSpec(memory...]
    ppermute x19 -> x20, starting transfers between devices: 16 us -> 17.7 us  [swap(): return lax.ppermute(x, axis, [(i, i ^ bit) for i in range(count)])]
  transfers between devices with their start and end apart: 19 -> 20, of which waited for: 10 -> 9; matrix products, arithmetic and copies ran while one was open for 4% -> 4% of each run, Pallas kernels for 14% -> 37%
where the time goes in v4:
time: 85.9 us; the launch traced here: 85.7 us
  Pallas kernels  40.3 us (47%)
  waiting for transfers between devices  23 us (27%)
  starting transfers between devices  17.7 us (21%)
  other arithmetic  2.66 us (3%)
  between operations  1.1 us (1%)
  local copies, waits for them, and re-layouts  0.93 us (1%)
    ppermute x20, waiting for transfers between devices, swap(): return lax.ppermute(x, axis, [(i, i ^ bit) for i in range(count)])  23 us
    ppermute x20, starting transfers between devices, swap(): return lax.ppermute(x, axis, [(i, i ^ bit) for i in range(count)])  17.7 us
    pallas_call x1, Pallas kernels, basis_steps(): pl.pallas_call(kernel, in_specs=[smem, smem, vmem] + [pl.BlockSpec(memory...  12.1 us
    pallas_call x1, Pallas kernels, gram(): pl.pallas_call(functools.partial(gram_kernel, rows=rows), in_specs=[hbm,...  7.41 us
    pallas_call x2, Pallas kernels, other_part(): pl.pallas_call(functools.partial(part_kernel, first=first, pieces=pieces)...  7.21 us
    pallas_call x1, Pallas kernels, factor_pull(): pl.pallas_call(functools.partial(pull_kernel, first=first, tiles=tiles),...  7.19 us
    pallas_call x1, Pallas kernels, network_start(): pl.pallas_call(functools.partial(network_kernel, slabs=slabs), in_specs=[...  4.37 us
    convert_element_type x3, other arithmetic, shards(): new = (mine.astype(F32) - both).astype(BF16)  2.41 us
  transfers between devices with their start and end apart: 20, of which 9 were waited for; matrix products, arithmetic and copies ran while one was open for 4% of the time, Pallas kernels for 37%

profile of v4, /device:TPU:0, one launch (start us, length us, event | category | flops | bytes accessed | tf_op | source)
XLA Modules:
  0.0 85.7 jit_solution(8509572214951773210)
XLA Ops:
  0.6 7.4 %gram.1 = f32[64,768]{1,0:T(8,128)S(1)} custom-call(bf16[16384,512]{1,0:T(8,128)(2,1)} %own_hbm.1, bf16[64,16384]{1,0:T(8,128)(2,1)} %bitcast.21, s32[4,16384]{1,0:T(4,128)} %bitcast.24), custom_call_target="tpu_custom_call" | custom-call | bytes 29520000 | tf_op jit(solution)/shard_map/gram/pallas_call | solution.py:126
  8.0 3.0 %collective-permute-start = (f32[64,768]{1,0:T(8,128)S(1)}, f32[64,768]{1,0:T(8,128)S(1)}, u32[]{:S(2)}, u32[]{:S(2)}) collective-permute-start(f32[64,768]{1,0:T(8,128)S(1)} %gram.1), channel_id=1, source_target_pairs={{0,4},{4,0},{8,12},{12,8},{16,20},{20,16},{24,28},{28,24},{1,5},{5... | collective-permute-start | bytes 589832 | tf_op jit(solution)/shard_map/ppermute | solution.py:508
  11.1 3.6 %other_part.2 = bf16[4096,512]{1,0:T(8,128)(2,1)} custom-call(s32[1]{0:T(128)} %bitcast.3.core_ref, bf16[16384,512]{1,0:T(8,128)(2,1)} %own_hbm.1), custom_call_target="tpu_custom_call" | custom-call | bytes 11070000 | tf_op jit(solution)/shard_map/other_part/pallas_call | solution.py:102
  14.7 1.3 %collective-permute-done = f32[64,768]{1,0:T(8,128)S(1)} collective-permute-done((f32[64,768]{1,0:T(8,128)S(1)}, f32[64,768]{1,0:T(8,128)S(1)}, u32[]{:S(2)}, u32[]{:S(2)}) %collective-permute-start) | collective-permute-done | bytes 196640 | tf_op jit(solution)/shard_map/ppermute | solution.py:508
  16.1 1.9 %collective-permute-start.1 = (f32[64,768]{1,0:T(8,128)S(1)}, f32[64,768]{1,0:T(8,128)S(1)}, u32[]{:S(2)}, u32[]{:S(2)}) collective-permute-start(f32[64,768]{1,0:T(8,128)S(1)} %add.52), channel_id=1, source_target_pairs={{0,8},{4,12},{8,0},{12,4},{16,24},{20,28},{24,16},{28,20},{1,9},{5... | collective-permute-start | bytes 589832 | tf_op jit(solution)/shard_map/ppermute | solution.py:508
  18.0 1.5 %collective-permute-start.2 = (f32[64,512]{1,0:T(8,128)S(1)}, f32[64,512]{1,0:T(8,128)S(1)}, u32[]{:S(2)}, u32[]{:S(2)}) collective-permute-start(f32[64,512]{1,0:T(8,128)S(1)} %copy-done.9), channel_id=1, source_target_pairs={{0,2},{1,3},{2,0},{3,1},{4,6},{5,7},{6,4},{7,5},{8,10},{9,11},{10,... | collective-permute-start | bytes 393224 | tf_op jit(solution)/shard_map/ppermute | solution.py:508
  19.5 3.6 %other_part.3 = bf16[4096,512]{1,0:T(8,128)(2,1)} custom-call(s32[1]{0:T(128)} %bitcast.3.core_ref, bf16[16384,512]{1,0:T(8,128)(2,1)} %own_hbm.1), custom_call_target="tpu_custom_call" | custom-call | bytes 11070000 | tf_op jit(solution)/shard_map/other_part/pallas_call | solution.py:102
  23.1 0.4 collective-permute-done.1
  23.6 2.8 %collective-permute-start.3 = (f32[64,768]{1,0:T(8,128)S(1)}, f32[64,768]{1,0:T(8,128)S(1)}, u32[]{:S(2)}, u32[]{:S(2)}) collective-permute-start(f32[64,768]{1,0:T(8,128)S(1)} %add.54), channel_id=1, source_target_pairs={{0,16},{4,20},{8,24},{12,28},{16,0},{20,4},{24,8},{28,12},{1,17},{... | collective-permute-start | bytes 589832 | tf_op jit(solution)/shard_map/ppermute | solution.py:508
  26.6 0.3 collective-permute-start.4
  26.9 9.2 %collective-permute-done.3 = f32[64,768]{1,0:T(8,128)S(1)} collective-permute-done((f32[64,768]{1,0:T(8,128)S(1)}, f32[64,768]{1,0:T(8,128)S(1)}, u32[]{:S(2)}, u32[]{:S(2)}) %collective-permute-start.3) | collective-permute-done | bytes 196640 | tf_op jit(solution)/shard_map/ppermute | solution.py:508
  36.2 1.6 %collective-permute-start.6 = (f32[64,768]{1,0:T(8,128)S(1)}, f32[64,768]{1,0:T(8,128)S(1)}, u32[]{:S(2)}, u32[]{:S(2)}) collective-permute-start(f32[64,768]{1,0:T(8,128)S(1)} %add.55.refs_0_), channel_id=1, source_target_pairs={{0,2},{1,3},{2,0},{3,1},{4,6},{5,7},{6,4},{7,5},{8,10},{9,11},{10,... | collective-permute-start | bytes 589832 | tf_op jit(solution)/shard_map/ppermute | solution.py:508
  37.9 0.5 collective-permute-start.8
  38.4 4.4 %network_start.1 = (f32[64,2048]{1,0:T(8,128)}, f32[64,2048]{1,0:T(8,128)}) custom-call(s32[2]{0:T(128)S(1)} %copy-done.5, s32[1]{0:T(128)} %bitcast.place_ref, f32[4,64,64]{2,1,0:T(8,128)} %w_hbm.3, f32[2,64]{1,0:T(2,128)} %bias_hbm.3, f32[64,512]{1,0:T(8,128)} %refs_0_.1, f32[64,512]{1,0:T(8,128)} %copy-done.12, f32[64,512]{1,0:T(8,128)} %copy-done.10, ...), custom_call_target="tpu_custom_call" | custom-call | bytes 11070000 | tf_op jit(solution)/shard_map/network_start/pallas_call | solution.py:244
  42.9 1.4 %collective-permute-done.7.last_ref = f32[64,768]{1,0:T(8,128)S(1)} collective-permute-done((f32[64,768]{1,0:T(8,128)S(1)}, f32[64,768]{1,0:T(8,128)S(1)}, u32[]{:S(2)}, u32[]{:S(2)}) %collective-permute-start.7) | collective-permute-done | bytes 196640 | tf_op jit(solution)/shard_map/ppermute | solution.py:508
  44.4 12.1 %basis_steps.1 = (f32[64,512]{1,0:T(8,128)}, bf16[64,512]{1,0:T(8,128)(2,1)S(1)}, bf16[64,512]{1,0:T(8,128)(2,1)S(1)}, f32[64,4096]{1,0:T(8,128)S(1)}) custom-call(s32[2]{0:T(128)S(1)} %copy-done.5, s32[1]{0:T(128)} %bitcast.place_ref, f32[64,768]{1,0:T(8,128)S(1)} %collective-permute-done.7.last_ref, f32[4,64,64]{2,1,0:T(8,128)} %w_hbm.3, ...), custom_call_target="tpu_custom_call" | custom-call | bytes 29520000 | tf_op jit(solution)/shard_map/basis_steps/pallas_call | solution.py:351
  56.7 1.5 %collective-permute-start.12 = (f16[64,2048]{1,0:T(8,128)(2,1)S(1)}, f16[64,2048]{1,0:T(8,128)(2,1)S(1)}, u32[]{:S(2)}, u32[]{:S(2)}) collective-permute-start(f16[64,2048]{1,0:T(8,128)(2,1)S(1)} %get-tuple-element.57), channel_id=1, source_target_pairs={{0,2},{1,3},{2,0},{3,1},{4,6},{5,7},{6,4},{7,5},{8,10},{9,11},{10,... | collective-permute-start | bytes 786440 | tf_op jit(solution)/shard_map/ppermute | solution.py:508
  58.3 0.6 collective-permute-start.15
  58.9 7.2 %factor_pull.1 = f32[64,4096]{1,0:T(8,128)S(1)} custom-call(s32[1]{0:T(128)} %bitcast.3.core_ref, bf16[16384,512]{1,0:T(8,128)(2,1)} %own_hbm.1, bf16[4096,512]{1,0:T(8,128)(2,1)} %collective-permute-done.11.sib_hbm, bf16[64,16384]{1,0:T(8,128)(2,1)S(1)} %bitcast.23, s32[4,16384]{1,0:T(4,128)S(1)} %bitcast.27, s32[4,16384]{1,0:T(4,128)S(1)} %copy-done.4, ...), custom_call_target="tpu_custom_call" | custom-call | bytes 29520000 | tf_op jit(solution)/shard_map/factor_pull/pallas_call | solution.py:462
  66.2 0.7 slice.19
  66.9 1.5 %collective-permute-start.13 = (f16[64,3072]{1,0:T(8,128)(2,1)S(1)}, f16[64,3072]{1,0:T(8,128)(2,1)}, u32[]{:S(2)}, u32[]{:S(2)}) collective-permute-start(f16[64,3072]{1,0:T(8,128)(2,1)S(1)} %slice.18), channel_id=1, source_target_pairs={{0,2},{1,3},{2,0},{3,1},{4,6},{5,7},{6,4},{7,5},{8,10},{9,11},{10,... | collective-permute-start | bytes 1179656 | tf_op jit(solution)/shard_map/ppermute | solution.py:508
  68.4 3.2 %collective-permute-done.15 = f16[64,2048]{1,0:T(8,128)(2,1)S(1)} collective-permute-done((f16[64,2048]{1,0:T(8,128)(2,1)S(1)}, f16[64,2048]{1,0:T(8,128)(2,1)S(1)}, u32[]{:S(2)}, u32[]{:S(2)}) %collective-permute-start.15) | collective-permute-done | bytes 262176 | tf_op jit(solution)/shard_map/ppermute | solution.py:508
  71.6 0.2 fusion.1
  71.9 0.5 collective-permute-start.16
  72.4 1.4 %collective-permute-start.18 = (f16[64,1024]{1,0:T(8,128)(2,1)}, f16[64,1024]{1,0:T(8,128)(2,1)}, u32[]{:S(2)}, u32[]{:S(2)}) collective-permute-start(f16[64,1024]{1,0:T(8,128)(2,1)} %slice.19), channel_id=1, source_target_pairs={{0,2},{1,3},{2,0},{3,1},{4,6},{5,7},{6,4},{7,5},{8,10},{9,11},{10,... | collective-permute-start | bytes 393224 | tf_op jit(solution)/shard_map/ppermute | solution.py:508
  73.8 1.0 %put.2.refs_4_ = bf16[64,16384]{1,0:T(8,128)(2,1)} custom-call(s32[1]{0:T(128)} %bitcast.3.core_ref, bf16[64,2048]{1,0:T(8,128)(2,1)S(1)} %get-tuple-element.55.refs_0_, bf16[64,2048]{1,0:T(8,128)(2,1)S(1)} %collective-permute-done.14.refs_1_, bf16[64,2048]{1,0:T(8,128)(2,1)S(1)} %get-tuple-element.54.refs_2_, ...), custom_call_target="tpu_custom_call" | custom-call | bytes 3690000 | tf_op jit(solution)/shard_map/put/pallas_call | solution.py:491
  74.9 5.3 %collective-permute-done.13 = f16[64,3072]{1,0:T(8,128)(2,1)} collective-permute-done((f16[64,3072]{1,0:T(8,128)(2,1)S(1)}, f16[64,3072]{1,0:T(8,128)(2,1)}, u32[]{:S(2)}, u32[]{:S(2)}) %collective-permute-start.13) | collective-permute-done | bytes 393248 | tf_op jit(solution)/shard_map/ppermute | solution.py:508
  80.1 1.1 %fusion.refs_0_ = bf16[64,3072]{1,0:T(8,128)(2,1)S(1)} fusion(f16[64,3072]{1,0:T(8,128)(2,1)} %collective-permute-done.13, f16[64,3072]{1,0:T(8,128)(2,1)S(1)} %slice.18, bf16[16384,64]{0,1:T(8,128)(2,1)S(1)} %copy-done, s32[]{:T(128)S(6)} %select_n.20), kind=kLoop, calls=%fused_computation.3 | loop fusion | flops 1179648 | bytes 1572868 | tf_op jit(solution)/shard_map/convert_element_type | solution.py:610
  81.4 0.8 collective-permute-done.18
  82.1 1.0 %fusion.3.refs_2_ = bf16[64,1024]{1,0:T(8,128)(2,1)S(1)} fusion(f16[64,1024]{1,0:T(8,128)(2,1)} %collective-permute-done.18, f16[64,1024]{1,0:T(8,128)(2,1)} %slice.19, bf16[16384,64]{0,1:T(8,128)(2,1)S(1)} %copy-done, s32[]{:T(128)S(6)} %select_n.23), kind=kLoop, calls=%fused_computation.9 | loop fusion | flops 393216 | bytes 524292 | tf_op jit(solution)/shard_map/convert_element_type | solution.py:610
  83.2 1.3 %collective-permute-done.19.refs_3_ = bf16[64,1024]{1,0:T(8,128)(2,1)S(1)} collective-permute-done((bf16[64,1024]{1,0:T(8,128)(2,1)S(1)}, bf16[64,1024]{1,0:T(8,128)(2,1)S(1)}, u32[]{:S(2)}, u32[]{:S(2)}) %collective-permute-start.19) | collective-permute-done | bytes 131104 | tf_op jit(solution)/shard_map/ppermute | solution.py:508
  84.5 1.0 %put.3 = bf16[64,16384]{1,0:T(8,128)(2,1)} custom-call(s32[1]{0:T(128)} %bitcast.3.core_ref, bf16[64,3072]{1,0:T(8,128)(2,1)S(1)} %fusion.refs_0_, bf16[64,3072]{1,0:T(8,128)(2,1)S(1)} %collective-permute-done.17.refs_1_, bf16[64,1024]{1,0:T(8,128)(2,1)S(1)} %fusion.3.refs_2_, ...), custom_call_target="tpu_custom_call", output_to_operand_aliasing={{}: (5, {})} | custom-call | bytes 3690000 | tf_op jit(solution)/shard_map/put/pallas_call | solution.py:491
  (53 shorter events, 1.2 us)
Async XLA Ops:
  8.0 7.9 %collective-permute-start = (f32[64,768]{1,0:T(8,128)S(1)}, f32[64,768]{1,0:T(8,128)S(1)}, u32[]{:S(2)}, u32[]{:S(2)}) collective-permute-start(f32[64,768]{1,0:T(8,128)S(1)} %gram.1), channel_id=1, source_target_pairs={{0,4},{4,0},{8,12},{12,8},{16,20},{20,16},{24,28},{28,24},{1,5},{5... | collective-permute-start | bytes 589832 | tf_op jit(solution)/shard_map/ppermute | solution.py:508
  11.1 6.9 %copy-start.9 = (f32[64,512]{1,0:T(8,128)S(1)}, f32[64,512]{1,0:T(8,128)}, u32[]{:S(2)}) copy-start(f32[64,512]{1,0:T(8,128)} %refs_0_.1) | copy-start | bytes 393220
  16.0 21.8 %copy-start.1 = (s32[16384,4]{0,1:T(4,128)S(1)}, s32[16384,4]{0,1:T(4,128)}, u32[]{:S(2)}) copy-start(s32[16384,4]{0,1:T(4,128)} %param.8) | copy-start | bytes 786436
  16.0 22.3 %copy-start.5 = (s32[2]{0:T(128)S(1)}, s32[2]{0:T(128)}, u32[]{:S(2)}) copy-start(s32[2]{0:T(128)} %dil_ref.3) | copy-start | bytes 28
  16.0 28.3 %collective-permute-start.9 = (bf16[4096,512]{1,0:T(8,128)(2,1)}, bf16[4096,512]{1,0:T(8,128)(2,1)}, u32[]{:S(2)}, u32[]{:S(2)}) collective-permute-start(bf16[4096,512]{1,0:T(8,128)(2,1)} %other_part.2), channel_id=1, source_target_pairs={{0,1},{1,0},{2,3},{3,2},{4,5},{5,4},{6,7},{7,6},{8,9},{9,8},{10,11... | collective-permute-start | bytes 12582920 | tf_op jit(solution)/shard_map/ppermute | solution.py:508
  16.1 7.4 %collective-permute-start.1 = (f32[64,768]{1,0:T(8,128)S(1)}, f32[64,768]{1,0:T(8,128)S(1)}, u32[]{:S(2)}, u32[]{:S(2)}) collective-permute-start(f32[64,768]{1,0:T(8,128)S(1)} %add.52), channel_id=1, source_target_pairs={{0,8},{4,12},{8,0},{12,4},{16,24},{20,28},{24,16},{28,20},{1,9},{5... | collective-permute-start | bytes 589832 | tf_op jit(solution)/shard_map/ppermute | solution.py:508
  18.0 5.6 %collective-permute-start.2 = (f32[64,512]{1,0:T(8,128)S(1)}, f32[64,512]{1,0:T(8,128)S(1)}, u32[]{:S(2)}, u32[]{:S(2)}) collective-permute-start(f32[64,512]{1,0:T(8,128)S(1)} %copy-done.9), channel_id=1, source_target_pairs={{0,2},{1,3},{2,0},{3,1},{4,6},{5,7},{6,4},{7,5},{8,10},{9,11},{10,... | collective-permute-start | bytes 393224 | tf_op jit(solution)/shard_map/ppermute | solution.py:508
  23.6 14.8 %copy-start.10 = (f32[64,512]{1,0:T(8,128)}, f32[64,512]{1,0:T(8,128)S(1)}, u32[]{:S(2)}) copy-start(f32[64,512]{1,0:T(8,128)S(1)} %collective-permute-done.2.refs_2_) | copy-start | bytes 393220
  23.6 35.3 %collective-permute-start.11 = (bf16[4096,512]{1,0:T(8,128)(2,1)}, bf16[4096,512]{1,0:T(8,128)(2,1)}, u32[]{:S(2)}, u32[]{:S(2)}) collective-permute-start(bf16[4096,512]{1,0:T(8,128)(2,1)} %other_part.3), channel_id=1, source_target_pairs={{0,1},{1,0},{2,3},{3,2},{4,5},{5,4},{6,7},{7,6},{8,9},{9,8},{10,11... | collective-permute-start | bytes 12582920 | tf_op jit(solution)/shard_map/ppermute | solution.py:508
  23.6 12.5 %collective-permute-start.3 = (f32[64,768]{1,0:T(8,128)S(1)}, f32[64,768]{1,0:T(8,128)S(1)}, u32[]{:S(2)}, u32[]{:S(2)}) collective-permute-start(f32[64,768]{1,0:T(8,128)S(1)} %add.54), channel_id=1, source_target_pairs={{0,16},{4,20},{8,24},{12,28},{16,0},{20,4},{24,8},{28,12},{1,17},{... | collective-permute-start | bytes 589832 | tf_op jit(solution)/shard_map/ppermute | solution.py:508
  26.4 9.7 %collective-permute-start.5 = (f32[64,512]{1,0:T(8,128)S(1)}, f32[64,512]{1,0:T(8,128)S(1)}, u32[]{:S(2)}, u32[]{:S(2)}) collective-permute-start(f32[64,512]{1,0:T(8,128)S(1)} %collective-permute-done.2.refs_2_), channel_id=1, source_target_pairs={{0,1},{1,0},{2,3},{3,2},{4,5},{5,4},{6,7},{7,6},{8,9},{9,8},{10,11... | collective-permute-start | bytes 393224 | tf_op jit(solution)/shard_map/ppermute | solution.py:508
  26.6 9.6 %collective-permute-start.4 = (f32[64,512]{1,0:T(8,128)S(1)}, f32[64,512]{1,0:T(8,128)S(1)}, u32[]{:S(2)}, u32[]{:S(2)}) collective-permute-start(f32[64,512]{1,0:T(8,128)S(1)} %copy-done.9), channel_id=1, source_target_pairs={{0,1},{1,0},{2,3},{3,2},{4,5},{5,4},{6,7},{7,6},{8,9},{9,8},{10,11... | collective-permute-start | bytes 393224 | tf_op jit(solution)/shard_map/ppermute | solution.py:508
  36.2 8.2 %copy-start.6 = (f32[64,768]{1,0:T(8,128)}, f32[64,768]{1,0:T(8,128)S(1)}, u32[]{:S(2)}) copy-start(f32[64,768]{1,0:T(8,128)S(1)} %add.55.refs_0_) | copy-start | bytes 589828
  36.2 2.2 %copy-start.11 = (f32[64,512]{1,0:T(8,128)}, f32[64,512]{1,0:T(8,128)S(1)}, u32[]{:S(2)}) copy-start(f32[64,512]{1,0:T(8,128)S(1)} %collective-permute-done.5.refs_3_) | copy-start | bytes 393220
  36.2 2.2 %copy-start.12 = (f32[64,512]{1,0:T(8,128)}, f32[64,512]{1,0:T(8,128)S(1)}, u32[]{:S(2)}) copy-start(f32[64,512]{1,0:T(8,128)S(1)} %collective-permute-done.4.refs_1_) | copy-start | bytes 393220
  36.2 6.7 %collective-permute-start.6 = (f32[64,768]{1,0:T(8,128)S(1)}, f32[64,768]{1,0:T(8,128)S(1)}, u32[]{:S(2)}, u32[]{:S(2)}) collective-permute-start(f32[64,768]{1,0:T(8,128)S(1)} %add.55.refs_0_), channel_id=1, source_target_pairs={{0,2},{1,3},{2,0},{3,1},{4,6},{5,7},{6,4},{7,5},{8,10},{9,11},{10,... | collective-permute-start | bytes 589832 | tf_op jit(solution)/shard_map/ppermute | solution.py:508
  37.8 5.0 %collective-permute-start.10 = (s32[4,16384]{1,0:T(4,128)S(1)}, s32[4,16384]{1,0:T(4,128)S(1)}, u32[]{:S(2)}, u32[]{:S(2)}) collective-permute-start(s32[4,16384]{1,0:T(4,128)S(1)} %bitcast.26), channel_id=1, source_target_pairs={{0,1},{1,0},{2,3},{3,2},{4,5},{5,4},{6,7},{7,6},{8,9},{9,8},{10,11... | collective-permute-start | bytes 786440 | tf_op jit(solution)/shard_map/ppermute | solution.py:508
  37.9 5.1 %collective-permute-start.8 = (f32[64,768]{1,0:T(8,128)S(1)}, f32[64,768]{1,0:T(8,128)S(1)}, u32[]{:S(2)}, u32[]{:S(2)}) collective-permute-start(f32[64,768]{1,0:T(8,128)S(1)} %add.55.refs_0_), channel_id=1, source_target_pairs={{0,1},{1,0},{2,3},{3,2},{4,5},{5,4},{6,7},{7,6},{8,9},{9,8},{10,11... | collective-permute-start | bytes 589832 | tf_op jit(solution)/shard_map/ppermute | solution.py:508
  42.9 1.5 %copy-start.7 = (f32[64,768]{1,0:T(8,128)}, f32[64,768]{1,0:T(8,128)S(1)}, u32[]{:S(2)}) copy-start(f32[64,768]{1,0:T(8,128)S(1)} %collective-permute-done.6.refs_2_) | copy-start | bytes 589828
  42.9 1.4 %collective-permute-start.7 = (f32[64,768]{1,0:T(8,128)S(1)}, f32[64,768]{1,0:T(8,128)S(1)}, u32[]{:S(2)}, u32[]{:S(2)}) collective-permute-start(f32[64,768]{1,0:T(8,128)S(1)} %collective-permute-done.6.refs_2_), channel_id=1, source_target_pairs={{0,1},{1,0},{2,3},{3,2},{4,5},{5,4},{6,7},{7,6},{8,9},{9,8},{10,11... | collective-permute-start | bytes 589832 | tf_op jit(solution)/shard_map/ppermute | solution.py:508
  42.9 1.4 %copy-start.3 = (s32[4,16384]{1,0:T(4,128)}, s32[4,16384]{1,0:T(4,128)S(1)}, u32[]{:S(2)}) copy-start(s32[4,16384]{1,0:T(4,128)S(1)} %collective-permute-done.10.refs_9_.sib_flg_ref) | copy-start | bytes 786436
  56.5 2.4 %copy-start = (bf16[16384,64]{0,1:T(8,128)(2,1)S(1)}, bf16[16384,64]{0,1:T(8,128)(2,1)}, u32[]{:S(2)}) copy-start(bf16[16384,64]{0,1:T(8,128)(2,1)} %param.9) | copy-start | bytes 6291460
  56.5 2.3 %copy-start.2 = (s32[16384,4]{0,1:T(4,128)S(1)}, s32[16384,4]{0,1:T(4,128)}, u32[]{:S(2)}) copy-start(s32[16384,4]{0,1:T(4,128)} %param.8) | copy-start | bytes 786436
  56.5 2.3 %copy-start.4 = (s32[4,16384]{1,0:T(4,128)S(1)}, s32[4,16384]{1,0:T(4,128)}, u32[]{:S(2)}) copy-start(s32[4,16384]{1,0:T(4,128)} %copy-done.3) | copy-start | bytes 786436
  56.7 10.2 %collective-permute-start.12 = (f16[64,2048]{1,0:T(8,128)(2,1)S(1)}, f16[64,2048]{1,0:T(8,128)(2,1)S(1)}, u32[]{:S(2)}, u32[]{:S(2)}) collective-permute-start(f16[64,2048]{1,0:T(8,128)(2,1)S(1)} %get-tuple-element.57), channel_id=1, source_target_pairs={{0,2},{1,3},{2,0},{3,1},{4,6},{5,7},{6,4},{7,5},{8,10},{9,11},{10,... | collective-permute-start | bytes 786440 | tf_op jit(solution)/shard_map/ppermute | solution.py:508
  58.3 13.3 %collective-permute-start.15 = (f16[64,2048]{1,0:T(8,128)(2,1)S(1)}, f16[64,2048]{1,0:T(8,128)(2,1)S(1)}, u32[]{:S(2)}, u32[]{:S(2)}) collective-permute-start(f16[64,2048]{1,0:T(8,128)(2,1)S(1)} %get-tuple-element.56), channel_id=1, source_target_pairs={{0,2},{1,3},{2,0},{3,1},{4,6},{5,7},{6,4},{7,5},{8,10},{9,11},{10,... | collective-permute-start | bytes 786440 | tf_op jit(solution)/shard_map/ppermute | solution.py:508
  66.9 13.2 %collective-permute-start.13 = (f16[64,3072]{1,0:T(8,128)(2,1)S(1)}, f16[64,3072]{1,0:T(8,128)(2,1)}, u32[]{:S(2)}, u32[]{:S(2)}) collective-permute-start(f16[64,3072]{1,0:T(8,128)(2,1)S(1)} %slice.18), channel_id=1, source_target_pairs={{0,2},{1,3},{2,0},{3,1},{4,6},{5,7},{6,4},{7,5},{8,10},{9,11},{10,... | collective-permute-start | bytes 1179656 | tf_op jit(solution)/shard_map/ppermute | solution.py:508
  71.8 2.0 %collective-permute-start.14 = (bf16[64,2048]{1,0:T(8,128)(2,1)S(1)}, bf16[64,2048]{1,0:T(8,128)(2,1)S(1)}, u32[]{:S(2)}, u32[]{:S(2)}) collective-permute-start(bf16[64,2048]{1,0:T(8,128)(2,1)S(1)} %get-tuple-element.55.refs_0_), channel_id=1, source_target_pairs={{0,1},{1,0},{2,3},{3,2},{4,5},{5,4},{6,7},{7,6},{8,9},{9,8},{10,11... | collective-permute-start | bytes 786440 | tf_op jit(solution)/shard_map/ppermute | solution.py:508
  71.9 1.9 %collective-permute-start.16 = (bf16[64,2048]{1,0:T(8,128)(2,1)S(1)}, bf16[64,2048]{1,0:T(8,128)(2,1)S(1)}, u32[]{:S(2)}, u32[]{:S(2)}) collective-permute-start(bf16[64,2048]{1,0:T(8,128)(2,1)S(1)} %get-tuple-element.54.refs_2_), channel_id=1, source_target_pairs={{0,1},{1,0},{2,3},{3,2},{4,5},{5,4},{6,7},{7,6},{8,9},{9,8},{10,11... | collective-permute-start | bytes 786440 | tf_op jit(solution)/shard_map/ppermute | solution.py:508
  72.4 9.7 %collective-permute-start.18 = (f16[64,1024]{1,0:T(8,128)(2,1)}, f16[64,1024]{1,0:T(8,128)(2,1)}, u32[]{:S(2)}, u32[]{:S(2)}) collective-permute-start(f16[64,1024]{1,0:T(8,128)(2,1)} %slice.19), channel_id=1, source_target_pairs={{0,2},{1,3},{2,0},{3,1},{4,6},{5,7},{6,4},{7,5},{8,10},{9,11},{10,... | collective-permute-start | bytes 393224 | tf_op jit(solution)/shard_map/ppermute | solution.py:508
  81.3 3.3 %collective-permute-start.17 = (bf16[64,3072]{1,0:T(8,128)(2,1)S(1)}, bf16[64,3072]{1,0:T(8,128)(2,1)S(1)}, u32[]{:S(2)}, u32[]{:S(2)}) collective-permute-start(bf16[64,3072]{1,0:T(8,128)(2,1)S(1)} %fusion.refs_0_), channel_id=1, source_target_pairs={{0,1},{1,0},{2,3},{3,2},{4,5},{5,4},{6,7},{7,6},{8,9},{9,8},{10,11... | collective-permute-start | bytes 1179656 | tf_op jit(solution)/shard_map/ppermute | solution.py:508
  83.1 1.4 %collective-permute-start.19 = (bf16[64,1024]{1,0:T(8,128)(2,1)S(1)}, bf16[64,1024]{1,0:T(8,128)(2,1)S(1)}, u32[]{:S(2)}, u32[]{:S(2)}) collective-permute-start(bf16[64,1024]{1,0:T(8,128)(2,1)S(1)} %fusion.3.refs_2_), channel_id=1, source_target_pairs={{0,1},{1,0},{2,3},{3,2},{4,5},{5,4},{6,7},{7,6},{8,9},{9,8},{10,11... | collective-permute-start | bytes 393224 | tf_op jit(solution)/shard_map/ppermute | solution.py:508
  (1 other events, 1.4 us)

commit v5 on v4

--- a/solution.py
+++ b/solution.py
@@ -14,6 +14,7 @@
 VMEM_BYTES = 40 << 20
 SMALL_BYTES = 24 << 20
 PULL_ROWS = 1024
+SCALE = 4.0
 CHUNKS = (4, 4)
 CUTS = ((2, 2), (3, 1))
 F32 = jnp.float32
@@ -445,30 +446,48 @@
 
 
 def pull_kernel(
-    core_ref, own_hbm, sib_hbm, fac_ref, own_flg_ref, sib_flg_ref, own_basis_ref, sib_basis_ref,
-    out_ref, *scratch, first, tiles
+    core_ref, own_hbm, sib_hbm, fac_hbm, own_flg_hbm, sib_flg_hbm, own_basis_ref, sib_basis_ref,
+    out_ref, fac_ref, flg_ref, sems, *scratch, first, tiles
 ):
+    series = out_ref.shape[1]
+    base = pl.multiple_of(core_ref[0] * (fac_hbm.shape[1] // 2) + first, PULL_ROWS)
+    mine = pl.ds(base, series)
+    loads = [
+        pltpu.make_async_copy(own_flg_hbm.at[:, mine], flg_ref.at[0], sems.at[0]),
+        pltpu.make_async_copy(sib_flg_hbm.at[:, mine], flg_ref.at[1], sems.at[1]),
+        pltpu.make_async_copy(fac_hbm.at[:, mine], fac_ref, sems.at[2]),
+    ]
+    for load in loads:
+        load.start()
     copies = pull_copies(core_ref[0], own_hbm, sib_hbm, scratch, first, tiles)
+    for load in loads:
+        load.wait()
     pull_chunk(
-        core_ref[0] * (fac_ref.shape[1] // 2) + first, tiles, copies, scratch, fac_ref, own_flg_ref,
-        sib_flg_ref, own_basis_ref[...], sib_basis_ref[...], out_ref,
+        0, tiles, copies, scratch, fac_ref, flg_ref.at[0], flg_ref.at[1], own_basis_ref[...],
+        sib_basis_ref[...], out_ref,
     )
 
 
 def factor_pull(core, observed, sibling, fac_t, flags, basis_b, first, series):
+    rank, blocks = fac_t.shape[0], flags[0].shape[0]
     vmem = pl.BlockSpec(memory_space=pltpu.VMEM)
     hbm = pl.BlockSpec(memory_space=pltpu.HBM)
     tiles = pull_tiles(series, False)
     return pl.pallas_call(
         functools.partial(pull_kernel, first=first, tiles=tiles),
-        in_specs=[pl.BlockSpec(memory_space=pltpu.SMEM), hbm, hbm] + [vmem] * 5,
+        in_specs=[pl.BlockSpec(memory_space=pltpu.SMEM)] + [hbm] * 5 + [vmem] * 2,
         out_specs=vmem,
-        out_shape=jax.ShapeDtypeStruct((fac_t.shape[0], series), F32),
-        scratch_shapes=pull_scratch_shapes(observed.shape[1], series, tiles),
+        out_shape=jax.ShapeDtypeStruct((rank, series), F32),
+        scratch_shapes=[
+            pltpu.VMEM((rank, series), BF16),
+            pltpu.VMEM((2, blocks, series), jnp.int32),
+            pltpu.SemaphoreType.DMA((3,)),
+        ]
+        + pull_scratch_shapes(observed.shape[1], series, tiles),
         compiler_params=pltpu.CompilerParams(vmem_limit_bytes=24 << 20),
         cost_estimate=kernel_cost(2e-6 * series / 1024),
         name="factor_pull",
-    )(core, in_hbm(observed), in_hbm(sibling), fac_t, *flags, *basis_b)
+    )(core, *[in_hbm(x) for x in (observed, sibling, fac_t, *flags)], *basis_b)
 
 
 def put_kernel(core_ref, *refs, places):
@@ -585,10 +604,9 @@
             pull = factor_pull(
                 core, observed, siblings[1], fac_t, flags, (own_b, sib_b), first, width
             )
-        own = (pull * coef).astype(jnp.float16)
         at = 0
         for cut in CUTS[c]:
-            piece = own[:, at * unit : (at + cut) * unit]
+            piece = (pull[:, at * unit : (at + cut) * unit] * (SCALE * coef)).astype(jnp.float16)
             if c > 0:
                 piece = after(piece, arrived[0])
             sent.append(piece)
@@ -607,7 +625,7 @@
             got = after(got, new_factors)
         both = own.astype(F32) + got.astype(F32)
         mine = lax.dynamic_slice_in_dim(fac_t, core[0] * half + firsts[c], own.shape[1], 1)
-        new = (mine.astype(F32) - both).astype(BF16)
+        new = (mine.astype(F32) - both * (1.0 / SCALE)).astype(BF16)
         pieces += [new, swap(new, "tm", 1)]
     new_factors = put(core, pieces, firsts[early:], new_factors, fac_t.shape)
     return new_basis, new_factors.T

time: 85.9 us -> 85.8 us (level)
  local copies, waits for them, and re-layouts: 0.93 us -> 0.05 us
    slice x3 -> x0, local copies, waits for them, and re-layouts: 0.87 us -> none  [shards(): piece = own[:, at * unit:(at + cut) * unit]]
    convert_element_type x5 -> x6, other arithmetic: 2.59 us -> 3.32 us  [the longest x3 2.46 us: shards(): new = (mine.astype(F32) - both * (1.0 / SCALE)).astype(BF16)]
  transfers between devices with their start and end apart: 20 -> 20, of which waited for: 9 -> 9; matrix products, arithmetic and copies ran while one was open for 4% -> 4% of each run, Pallas kernels for 37% -> 38%
where the time goes in v5:
time: 85.8 us; the launch traced here: 85.6 us
  Pallas kernels  41.1 us (48%)
  waiting for transfers between devices  22.3 us (26%)
  starting transfers between devices  17.6 us (21%)
  other arithmetic  3.39 us (4%)
  between operations  1.05 us (1%)
    ppermute x20, waiting for transfers between devices, swap(): return lax.ppermute(x, axis, [(i, i ^ bit) for i in range(count)])  22.3 us
    ppermute x20, starting transfers between devices, swap(): return lax.ppermute(x, axis, [(i, i ^ bit) for i in range(count)])  17.6 us
    pallas_call x1, Pallas kernels, basis_steps(): pl.pallas_call(kernel, in_specs=[smem, smem, vmem] + [pl.BlockSpec(memory...  12.1 us
    pallas_call x1, Pallas kernels, factor_pull(): pl.pallas_call(functools.partial(pull_kernel, first=first, tiles=tiles),...  8.02 us
    pallas_call x1, Pallas kernels, gram(): pl.pallas_call(functools.partial(gram_kernel, rows=rows), in_specs=[hbm,...  7.41 us
    pallas_call x2, Pallas kernels, other_part(): pl.pallas_call(functools.partial(part_kernel, first=first, pieces=pieces)...  7.18 us
    pallas_call x1, Pallas kernels, network_start(): pl.pallas_call(functools.partial(network_kernel, slabs=slabs), in_specs=[...  4.37 us
    convert_element_type x3, other arithmetic, shards(): new = (mine.astype(F32) - both * (1.0 / SCALE)).astype(BF16)  2.46 us
  transfers between devices with their start and end apart: 20, of which 9 were waited for; matrix products, arithmetic and copies ran while one was open for 4% of the time, Pallas kernels for 38%

profile of v5, /device:TPU:0, one launch (start us, length us, event | category | flops | bytes accessed | tf_op | source)
XLA Modules:
  0.0 85.6 jit_solution(5869041804914779740)
XLA Ops:
  0.6 7.4 %gram.1 = f32[64,768]{1,0:T(8,128)S(1)} custom-call(bf16[16384,512]{1,0:T(8,128)(2,1)} %own_hbm.1, bf16[64,16384]{1,0:T(8,128)(2,1)} %bitcast.21, s32[4,16384]{1,0:T(4,128)} %bitcast.25), custom_call_target="tpu_custom_call" | custom-call | bytes 29520000 | tf_op jit(solution)/shard_map/gram/pallas_call | solution.py:127
  8.0 3.0 %collective-permute-start = (f32[64,768]{1,0:T(8,128)S(1)}, f32[64,768]{1,0:T(8,128)S(1)}, u32[]{:S(2)}, u32[]{:S(2)}) collective-permute-start(f32[64,768]{1,0:T(8,128)S(1)} %gram.1), channel_id=1, source_target_pairs={{0,4},{4,0},{8,12},{12,8},{16,20},{20,16},{24,28},{28,24},{1,5},{5... | collective-permute-start | bytes 589832 | tf_op jit(solution)/shard_map/ppermute | solution.py:527
  11.1 3.6 %other_part.2 = bf16[4096,512]{1,0:T(8,128)(2,1)} custom-call(s32[1]{0:T(128)} %bitcast.3.core_ref, bf16[16384,512]{1,0:T(8,128)(2,1)} %own_hbm.1), custom_call_target="tpu_custom_call" | custom-call | bytes 11070000 | tf_op jit(solution)/shard_map/other_part/pallas_call | solution.py:103
  14.7 1.3 %collective-permute-done = f32[64,768]{1,0:T(8,128)S(1)} collective-permute-done((f32[64,768]{1,0:T(8,128)S(1)}, f32[64,768]{1,0:T(8,128)S(1)}, u32[]{:S(2)}, u32[]{:S(2)}) %collective-permute-start) | collective-permute-done | bytes 196640 | tf_op jit(solution)/shard_map/ppermute | solution.py:527
  16.1 1.9 %collective-permute-start.1 = (f32[64,768]{1,0:T(8,128)S(1)}, f32[64,768]{1,0:T(8,128)S(1)}, u32[]{:S(2)}, u32[]{:S(2)}) collective-permute-start(f32[64,768]{1,0:T(8,128)S(1)} %add.52), channel_id=1, source_target_pairs={{0,8},{4,12},{8,0},{12,4},{16,24},{20,28},{24,16},{28,20},{1,9},{5... | collective-permute-start | bytes 589832 | tf_op jit(solution)/shard_map/ppermute | solution.py:527
  18.0 1.5 %collective-permute-start.2 = (f32[64,512]{1,0:T(8,128)S(1)}, f32[64,512]{1,0:T(8,128)S(1)}, u32[]{:S(2)}, u32[]{:S(2)}) collective-permute-start(f32[64,512]{1,0:T(8,128)S(1)} %copy-done.7), channel_id=1, source_target_pairs={{0,2},{1,3},{2,0},{3,1},{4,6},{5,7},{6,4},{7,5},{8,10},{9,11},{10,... | collective-permute-start | bytes 393224 | tf_op jit(solution)/shard_map/ppermute | solution.py:527
  19.5 3.6 %other_part.3 = bf16[4096,512]{1,0:T(8,128)(2,1)} custom-call(s32[1]{0:T(128)} %bitcast.3.core_ref, bf16[16384,512]{1,0:T(8,128)(2,1)} %own_hbm.1), custom_call_target="tpu_custom_call" | custom-call | bytes 11070000 | tf_op jit(solution)/shard_map/other_part/pallas_call | solution.py:103
  23.1 0.4 collective-permute-done.1
  23.6 2.8 %collective-permute-start.3 = (f32[64,768]{1,0:T(8,128)S(1)}, f32[64,768]{1,0:T(8,128)S(1)}, u32[]{:S(2)}, u32[]{:S(2)}) collective-permute-start(f32[64,768]{1,0:T(8,128)S(1)} %add.54), channel_id=1, source_target_pairs={{0,16},{4,20},{8,24},{12,28},{16,0},{20,4},{24,8},{28,12},{1,17},{... | collective-permute-start | bytes 589832 | tf_op jit(solution)/shard_map/ppermute | solution.py:527
  26.6 0.3 collective-permute-start.4
  26.9 9.2 %collective-permute-done.3 = f32[64,768]{1,0:T(8,128)S(1)} collective-permute-done((f32[64,768]{1,0:T(8,128)S(1)}, f32[64,768]{1,0:T(8,128)S(1)}, u32[]{:S(2)}, u32[]{:S(2)}) %collective-permute-start.3) | collective-permute-done | bytes 196640 | tf_op jit(solution)/shard_map/ppermute | solution.py:527
  36.2 1.6 %collective-permute-start.6 = (f32[64,768]{1,0:T(8,128)S(1)}, f32[64,768]{1,0:T(8,128)S(1)}, u32[]{:S(2)}, u32[]{:S(2)}) collective-permute-start(f32[64,768]{1,0:T(8,128)S(1)} %add.55.refs_0_), channel_id=1, source_target_pairs={{0,2},{1,3},{2,0},{3,1},{4,6},{5,7},{6,4},{7,5},{8,10},{9,11},{10,... | collective-permute-start | bytes 589832 | tf_op jit(solution)/shard_map/ppermute | solution.py:527
  37.9 0.5 collective-permute-start.8
  38.4 4.4 %network_start.1 = (f32[64,2048]{1,0:T(8,128)}, f32[64,2048]{1,0:T(8,128)}) custom-call(s32[2]{0:T(128)S(1)} %copy-done, s32[1]{0:T(128)} %bitcast.place_ref, f32[4,64,64]{2,1,0:T(8,128)} %w_hbm.3, f32[2,64]{1,0:T(2,128)} %bias_hbm.3, f32[64,512]{1,0:T(8,128)} %refs_0_.1, f32[64,512]{1,0:T(8,128)} %copy-done.10, f32[64,512]{1,0:T(8,128)} %copy-done.8, ...), custom_call_target="tpu_custom_call" | custom-call | bytes 11070000 | tf_op jit(solution)/shard_map/network_start/pallas_call | solution.py:245
  42.9 1.4 %collective-permute-done.7.last_ref = f32[64,768]{1,0:T(8,128)S(1)} collective-permute-done((f32[64,768]{1,0:T(8,128)S(1)}, f32[64,768]{1,0:T(8,128)S(1)}, u32[]{:S(2)}, u32[]{:S(2)}) %collective-permute-start.7) | collective-permute-done | bytes 196640 | tf_op jit(solution)/shard_map/ppermute | solution.py:527
  44.4 12.1 %basis_steps.1 = (f32[64,512]{1,0:T(8,128)}, bf16[64,512]{1,0:T(8,128)(2,1)S(1)}, bf16[64,512]{1,0:T(8,128)(2,1)S(1)}, f32[64,4096]{1,0:T(8,128)S(1)}) custom-call(s32[2]{0:T(128)S(1)} %copy-done, s32[1]{0:T(128)} %bitcast.place_ref, f32[64,768]{1,0:T(8,128)S(1)} %collective-permute-done.7.last_ref, f32[4,64,64]{2,1,0:T(8,128)} %w_hbm.3, f32[2,64]{1,0:T(2,128)} %bias_hbm.3, ...), custom_call_target="tpu_custom_call" | custom-call | bytes 29520000 | tf_op jit(solution)/shard_map/basis_steps/pallas_call | solution.py:352
  56.6 1.5 %collective-permute-start.12 = (f16[64,2048]{1,0:T(8,128)(2,1)S(1)}, f16[64,2048]{1,0:T(8,128)(2,1)S(1)}, u32[]{:S(2)}, u32[]{:S(2)}) collective-permute-start(f16[64,2048]{1,0:T(8,128)(2,1)S(1)} %get-tuple-element.57), channel_id=1, source_target_pairs={{0,2},{1,3},{2,0},{3,1},{4,6},{5,7},{6,4},{7,5},{8,10},{9,11},{10,... | collective-permute-start | bytes 786440 | tf_op jit(solution)/shard_map/ppermute | solution.py:527
  58.1 0.6 collective-permute-start.15
  58.7 8.0 %factor_pull.1 = f32[64,4096]{1,0:T(8,128)S(1)} custom-call(s32[1]{0:T(128)} %bitcast.3.core_ref, bf16[16384,512]{1,0:T(8,128)(2,1)} %own_hbm.1, bf16[4096,512]{1,0:T(8,128)(2,1)} %collective-permute-done.11.sib_hbm, bf16[64,16384]{1,0:T(8,128)(2,1)} %bitcast.23, s32[4,16384]{1,0:T(4,128)} %bitcast.27, s32[4,16384]{1,0:T(4,128)} %copy-done.3, ...), custom_call_target="tpu_custom_call" | custom-call | bytes 29520000 | tf_op jit(solution)/shard_map/factor_pull/pallas_call | solution.py:476
  66.8 0.7 fusion.4
  67.5 1.4 %collective-permute-start.13 = (f16[64,3072]{1,0:T(8,128)(2,1)S(1)}, f16[64,3072]{1,0:T(8,128)(2,1)}, u32[]{:S(2)}, u32[]{:S(2)}) collective-permute-start(f16[64,3072]{1,0:T(8,128)(2,1)S(1)} %fusion), channel_id=1, source_target_pairs={{0,2},{1,3},{2,0},{3,1},{4,6},{5,7},{6,4},{7,5},{8,10},{9,11},{10,... | collective-permute-start | bytes 1179656 | tf_op jit(solution)/shard_map/ppermute | solution.py:527
  68.9 2.5 %collective-permute-done.15 = f16[64,2048]{1,0:T(8,128)(2,1)S(1)} collective-permute-done((f16[64,2048]{1,0:T(8,128)(2,1)S(1)}, f16[64,2048]{1,0:T(8,128)(2,1)S(1)}, u32[]{:S(2)}, u32[]{:S(2)}) %collective-permute-start.15) | collective-permute-done | bytes 262176 | tf_op jit(solution)/shard_map/ppermute | solution.py:527
  71.4 0.3 fusion.2
  71.8 0.5 collective-permute-start.16
  72.3 1.4 %collective-permute-start.18 = (f16[64,1024]{1,0:T(8,128)(2,1)}, f16[64,1024]{1,0:T(8,128)(2,1)}, u32[]{:S(2)}, u32[]{:S(2)}) collective-permute-start(f16[64,1024]{1,0:T(8,128)(2,1)} %fusion.4), channel_id=1, source_target_pairs={{0,2},{1,3},{2,0},{3,1},{4,6},{5,7},{6,4},{7,5},{8,10},{9,11},{10,... | collective-permute-start | bytes 393224 | tf_op jit(solution)/shard_map/ppermute | solution.py:527
  73.7 1.0 %put.2.refs_4_ = bf16[64,16384]{1,0:T(8,128)(2,1)} custom-call(s32[1]{0:T(128)} %bitcast.3.core_ref, bf16[64,2048]{1,0:T(8,128)(2,1)S(1)} %get-tuple-element.55.refs_0_, bf16[64,2048]{1,0:T(8,128)(2,1)S(1)} %collective-permute-done.14.refs_1_, bf16[64,2048]{1,0:T(8,128)(2,1)S(1)} %get-tuple-element.54.refs_2_, ...), custom_call_target="tpu_custom_call" | custom-call | bytes 3690000 | tf_op jit(solution)/shard_map/put/pallas_call | solution.py:510
  74.7 5.2 %collective-permute-done.13 = f16[64,3072]{1,0:T(8,128)(2,1)} collective-permute-done((f16[64,3072]{1,0:T(8,128)(2,1)S(1)}, f16[64,3072]{1,0:T(8,128)(2,1)}, u32[]{:S(2)}, u32[]{:S(2)}) %collective-permute-start.13) | collective-permute-done | bytes 393248 | tf_op jit(solution)/shard_map/ppermute | solution.py:527
  80.0 1.2 %fusion.1.refs_0_ = bf16[64,3072]{1,0:T(8,128)(2,1)S(1)} fusion(f16[64,3072]{1,0:T(8,128)(2,1)} %collective-permute-done.13, f16[64,3072]{1,0:T(8,128)(2,1)S(1)} %fusion, bf16[16384,64]{0,1:T(8,128)(2,1)S(1)} %copy-done.1, s32[]{:T(128)S(6)} %select_n.20), kind=kLoop, calls=%fused_computation.3 | loop fusion | flops 1376256 | bytes 1572868 | tf_op jit(solution)/shard_map/convert_element_type | solution.py:628
  81.2 0.7 collective-permute-done.18
  82.0 1.0 %fusion.5.refs_2_ = bf16[64,1024]{1,0:T(8,128)(2,1)S(1)} fusion(f16[64,1024]{1,0:T(8,128)(2,1)} %collective-permute-done.18, f16[64,1024]{1,0:T(8,128)(2,1)} %fusion.4, bf16[16384,64]{0,1:T(8,128)(2,1)S(1)} %copy-done.1, s32[]{:T(128)S(6)} %select_n.23), kind=kLoop, calls=%fused_computation.13 | loop fusion | flops 458752 | bytes 524292 | tf_op jit(solution)/shard_map/convert_element_type | solution.py:628
  83.1 1.3 %collective-permute-done.19.refs_3_ = bf16[64,1024]{1,0:T(8,128)(2,1)S(1)} collective-permute-done((bf16[64,1024]{1,0:T(8,128)(2,1)S(1)}, bf16[64,1024]{1,0:T(8,128)(2,1)S(1)}, u32[]{:S(2)}, u32[]{:S(2)}) %collective-permute-start.19) | collective-permute-done | bytes 131104 | tf_op jit(solution)/shard_map/ppermute | solution.py:527
  84.4 1.0 %put.3 = bf16[64,16384]{1,0:T(8,128)(2,1)} custom-call(s32[1]{0:T(128)} %bitcast.3.core_ref, bf16[64,3072]{1,0:T(8,128)(2,1)S(1)} %fusion.1.refs_0_, bf16[64,3072]{1,0:T(8,128)(2,1)S(1)} %collective-permute-done.17.refs_1_, bf16[64,1024]{1,0:T(8,128)(2,1)S(1)} %fusion.5.refs_2_, ...), custom_call_target="tpu_custom_call", output_to_operand_aliasing={{}: (5, {})} | custom-call | bytes 3690000 | tf_op jit(solution)/shard_map/put/pallas_call | solution.py:510
  (47 shorter events, 1.0 us)
Async XLA Ops:
  8.0 7.9 %collective-permute-start = (f32[64,768]{1,0:T(8,128)S(1)}, f32[64,768]{1,0:T(8,128)S(1)}, u32[]{:S(2)}, u32[]{:S(2)}) collective-permute-start(f32[64,768]{1,0:T(8,128)S(1)} %gram.1), channel_id=1, source_target_pairs={{0,4},{4,0},{8,12},{12,8},{16,20},{20,16},{24,28},{28,24},{1,5},{5... | collective-permute-start | bytes 589832 | tf_op jit(solution)/shard_map/ppermute | solution.py:527
  11.1 6.9 %copy-start.7 = (f32[64,512]{1,0:T(8,128)S(1)}, f32[64,512]{1,0:T(8,128)}, u32[]{:S(2)}) copy-start(f32[64,512]{1,0:T(8,128)} %refs_0_.1) | copy-start | bytes 393220
  16.0 21.8 %copy-start.2 = (s32[16384,4]{0,1:T(4,128)S(1)}, s32[16384,4]{0,1:T(4,128)}, u32[]{:S(2)}) copy-start(s32[16384,4]{0,1:T(4,128)} %param.8) | copy-start | bytes 786436
  16.0 22.3 %copy-start = (s32[2]{0:T(128)S(1)}, s32[2]{0:T(128)}, u32[]{:S(2)}) copy-start(s32[2]{0:T(128)} %dil_ref.3) | copy-start | bytes 28
  16.0 28.3 %collective-permute-start.9 = (bf16[4096,512]{1,0:T(8,128)(2,1)}, bf16[4096,512]{1,0:T(8,128)(2,1)}, u32[]{:S(2)}, u32[]{:S(2)}) collective-permute-start(bf16[4096,512]{1,0:T(8,128)(2,1)} %other_part.2), channel_id=1, source_target_pairs={{0,1},{1,0},{2,3},{3,2},{4,5},{5,4},{6,7},{7,6},{8,9},{9,8},{10,11... | collective-permute-start | bytes 12582920 | tf_op jit(solution)/shard_map/ppermute | solution.py:527
  16.1 7.4 %collective-permute-start.1 = (f32[64,768]{1,0:T(8,128)S(1)}, f32[64,768]{1,0:T(8,128)S(1)}, u32[]{:S(2)}, u32[]{:S(2)}) collective-permute-start(f32[64,768]{1,0:T(8,128)S(1)} %add.52), channel_id=1, source_target_pairs={{0,8},{4,12},{8,0},{12,4},{16,24},{20,28},{24,16},{28,20},{1,9},{5... | collective-permute-start | bytes 589832 | tf_op jit(solution)/shard_map/ppermute | solution.py:527
  18.0 5.6 %collective-permute-start.2 = (f32[64,512]{1,0:T(8,128)S(1)}, f32[64,512]{1,0:T(8,128)S(1)}, u32[]{:S(2)}, u32[]{:S(2)}) collective-permute-start(f32[64,512]{1,0:T(8,128)S(1)} %copy-done.7), channel_id=1, source_target_pairs={{0,2},{1,3},{2,0},{3,1},{4,6},{5,7},{6,4},{7,5},{8,10},{9,11},{10,... | collective-permute-start | bytes 393224 | tf_op jit(solution)/shard_map/ppermute | solution.py:527
  23.6 14.8 %copy-start.8 = (f32[64,512]{1,0:T(8,128)}, f32[64,512]{1,0:T(8,128)S(1)}, u32[]{:S(2)}) copy-start(f32[64,512]{1,0:T(8,128)S(1)} %collective-permute-done.2.refs_2_) | copy-start | bytes 393220
  23.6 35.1 %collective-permute-start.11 = (bf16[4096,512]{1,0:T(8,128)(2,1)}, bf16[4096,512]{1,0:T(8,128)(2,1)}, u32[]{:S(2)}, u32[]{:S(2)}) collective-permute-start(bf16[4096,512]{1,0:T(8,128)(2,1)} %other_part.3), channel_id=1, source_target_pairs={{0,1},{1,0},{2,3},{3,2},{4,5},{5,4},{6,7},{7,6},{8,9},{9,8},{10,11... | collective-permute-start | bytes 12582920 | tf_op jit(solution)/shard_map/ppermute | solution.py:527
  23.6 12.5 %collective-permute-start.3 = (f32[64,768]{1,0:T(8,128)S(1)}, f32[64,768]{1,0:T(8,128)S(1)}, u32[]{:S(2)}, u32[]{:S(2)}) collective-permute-start(f32[64,768]{1,0:T(8,128)S(1)} %add.54), channel_id=1, source_target_pairs={{0,16},{4,20},{8,24},{12,28},{16,0},{20,4},{24,8},{28,12},{1,17},{... | collective-permute-start | bytes 589832 | tf_op jit(solution)/shard_map/ppermute | solution.py:527
  26.4 9.7 %collective-permute-start.5 = (f32[64,512]{1,0:T(8,128)S(1)}, f32[64,512]{1,0:T(8,128)S(1)}, u32[]{:S(2)}, u32[]{:S(2)}) collective-permute-start(f32[64,512]{1,0:T(8,128)S(1)} %collective-permute-done.2.refs_2_), channel_id=1, source_target_pairs={{0,1},{1,0},{2,3},{3,2},{4,5},{5,4},{6,7},{7,6},{8,9},{9,8},{10,11... | collective-permute-start | bytes 393224 | tf_op jit(solution)/shard_map/ppermute | solution.py:527
  26.6 9.6 %collective-permute-start.4 = (f32[64,512]{1,0:T(8,128)S(1)}, f32[64,512]{1,0:T(8,128)S(1)}, u32[]{:S(2)}, u32[]{:S(2)}) collective-permute-start(f32[64,512]{1,0:T(8,128)S(1)} %copy-done.7), channel_id=1, source_target_pairs={{0,1},{1,0},{2,3},{3,2},{4,5},{5,4},{6,7},{7,6},{8,9},{9,8},{10,11... | collective-permute-start | bytes 393224 | tf_op jit(solution)/shard_map/ppermute | solution.py:527
  36.2 8.2 %copy-start.4 = (f32[64,768]{1,0:T(8,128)}, f32[64,768]{1,0:T(8,128)S(1)}, u32[]{:S(2)}) copy-start(f32[64,768]{1,0:T(8,128)S(1)} %add.55.refs_0_) | copy-start | bytes 589828
  36.2 2.2 %copy-start.9 = (f32[64,512]{1,0:T(8,128)}, f32[64,512]{1,0:T(8,128)S(1)}, u32[]{:S(2)}) copy-start(f32[64,512]{1,0:T(8,128)S(1)} %collective-permute-done.5.refs_3_) | copy-start | bytes 393220
  36.2 2.2 %copy-start.10 = (f32[64,512]{1,0:T(8,128)}, f32[64,512]{1,0:T(8,128)S(1)}, u32[]{:S(2)}) copy-start(f32[64,512]{1,0:T(8,128)S(1)} %collective-permute-done.4.refs_1_) | copy-start | bytes 393220
  36.2 6.7 %collective-permute-start.6 = (f32[64,768]{1,0:T(8,128)S(1)}, f32[64,768]{1,0:T(8,128)S(1)}, u32[]{:S(2)}, u32[]{:S(2)}) collective-permute-start(f32[64,768]{1,0:T(8,128)S(1)} %add.55.refs_0_), channel_id=1, source_target_pairs={{0,2},{1,3},{2,0},{3,1},{4,6},{5,7},{6,4},{7,5},{8,10},{9,11},{10,... | collective-permute-start | bytes 589832 | tf_op jit(solution)/shard_map/ppermute | solution.py:527
  37.8 5.0 %collective-permute-start.10 = (s32[4,16384]{1,0:T(4,128)S(1)}, s32[4,16384]{1,0:T(4,128)S(1)}, u32[]{:S(2)}, u32[]{:S(2)}) collective-permute-start(s32[4,16384]{1,0:T(4,128)S(1)} %bitcast.28), channel_id=1, source_target_pairs={{0,1},{1,0},{2,3},{3,2},{4,5},{5,4},{6,7},{7,6},{8,9},{9,8},{10,11... | collective-permute-start | bytes 786440 | tf_op jit(solution)/shard_map/ppermute | solution.py:527
  37.9 5.1 %collective-permute-start.8 = (f32[64,768]{1,0:T(8,128)S(1)}, f32[64,768]{1,0:T(8,128)S(1)}, u32[]{:S(2)}, u32[]{:S(2)}) collective-permute-start(f32[64,768]{1,0:T(8,128)S(1)} %add.55.refs_0_), channel_id=1, source_target_pairs={{0,1},{1,0},{2,3},{3,2},{4,5},{5,4},{6,7},{7,6},{8,9},{9,8},{10,11... | collective-permute-start | bytes 589832 | tf_op jit(solution)/shard_map/ppermute | solution.py:527
  42.9 1.5 %copy-start.5 = (f32[64,768]{1,0:T(8,128)}, f32[64,768]{1,0:T(8,128)S(1)}, u32[]{:S(2)}) copy-start(f32[64,768]{1,0:T(8,128)S(1)} %collective-permute-done.6.refs_2_) | copy-start | bytes 589828
  42.9 1.4 %collective-permute-start.7 = (f32[64,768]{1,0:T(8,128)S(1)}, f32[64,768]{1,0:T(8,128)S(1)}, u32[]{:S(2)}, u32[]{:S(2)}) collective-permute-start(f32[64,768]{1,0:T(8,128)S(1)} %collective-permute-done.6.refs_2_), channel_id=1, source_target_pairs={{0,1},{1,0},{2,3},{3,2},{4,5},{5,4},{6,7},{7,6},{8,9},{9,8},{10,11... | collective-permute-start | bytes 589832 | tf_op jit(solution)/shard_map/ppermute | solution.py:527
  42.9 1.4 %copy-start.3 = (s32[4,16384]{1,0:T(4,128)}, s32[4,16384]{1,0:T(4,128)S(1)}, u32[]{:S(2)}) copy-start(s32[4,16384]{1,0:T(4,128)S(1)} %collective-permute-done.10.refs_9_.sib_flg_hbm) | copy-start | bytes 786436
  42.9 1.4 %copy-start.6 = (f32[64,768]{1,0:T(8,128)}, f32[64,768]{1,0:T(8,128)S(1)}, u32[]{:S(2)}) copy-start(f32[64,768]{1,0:T(8,128)S(1)} %collective-permute-done.8.refs_1_) | copy-start | bytes 589828
  56.6 10.9 %collective-permute-start.12 = (f16[64,2048]{1,0:T(8,128)(2,1)S(1)}, f16[64,2048]{1,0:T(8,128)(2,1)S(1)}, u32[]{:S(2)}, u32[]{:S(2)}) collective-permute-start(f16[64,2048]{1,0:T(8,128)(2,1)S(1)} %get-tuple-element.57), channel_id=1, source_target_pairs={{0,2},{1,3},{2,0},{3,1},{4,6},{5,7},{6,4},{7,5},{8,10},{9,11},{10,... | collective-permute-start | bytes 786440 | tf_op jit(solution)/shard_map/ppermute | solution.py:527
  58.1 13.3 %collective-permute-start.15 = (f16[64,2048]{1,0:T(8,128)(2,1)S(1)}, f16[64,2048]{1,0:T(8,128)(2,1)S(1)}, u32[]{:S(2)}, u32[]{:S(2)}) collective-permute-start(f16[64,2048]{1,0:T(8,128)(2,1)S(1)} %get-tuple-element.56), channel_id=1, source_target_pairs={{0,2},{1,3},{2,0},{3,1},{4,6},{5,7},{6,4},{7,5},{8,10},{9,11},{10,... | collective-permute-start | bytes 786440 | tf_op jit(solution)/shard_map/ppermute | solution.py:527
  58.7 12.7 %copy-start.1 = (bf16[16384,64]{0,1:T(8,128)(2,1)S(1)}, bf16[16384,64]{0,1:T(8,128)(2,1)}, u32[]{:S(2)}) copy-start(bf16[16384,64]{0,1:T(8,128)(2,1)} %param.9) | copy-start | bytes 6291460
  67.5 12.5 %collective-permute-start.13 = (f16[64,3072]{1,0:T(8,128)(2,1)S(1)}, f16[64,3072]{1,0:T(8,128)(2,1)}, u32[]{:S(2)}, u32[]{:S(2)}) collective-permute-start(f16[64,3072]{1,0:T(8,128)(2,1)S(1)} %fusion), channel_id=1, source_target_pairs={{0,2},{1,3},{2,0},{3,1},{4,6},{5,7},{6,4},{7,5},{8,10},{9,11},{10,... | collective-permute-start | bytes 1179656 | tf_op jit(solution)/shard_map/ppermute | solution.py:527
  71.7 2.0 %collective-permute-start.14 = (bf16[64,2048]{1,0:T(8,128)(2,1)S(1)}, bf16[64,2048]{1,0:T(8,128)(2,1)S(1)}, u32[]{:S(2)}, u32[]{:S(2)}) collective-permute-start(bf16[64,2048]{1,0:T(8,128)(2,1)S(1)} %get-tuple-element.55.refs_0_), channel_id=1, source_target_pairs={{0,1},{1,0},{2,3},{3,2},{4,5},{5,4},{6,7},{7,6},{8,9},{9,8},{10,11... | collective-permute-start | bytes 786440 | tf_op jit(solution)/shard_map/ppermute | solution.py:527
  71.8 1.9 %collective-permute-start.16 = (bf16[64,2048]{1,0:T(8,128)(2,1)S(1)}, bf16[64,2048]{1,0:T(8,128)(2,1)S(1)}, u32[]{:S(2)}, u32[]{:S(2)}) collective-permute-start(bf16[64,2048]{1,0:T(8,128)(2,1)S(1)} %get-tuple-element.54.refs_2_), channel_id=1, source_target_pairs={{0,1},{1,0},{2,3},{3,2},{4,5},{5,4},{6,7},{7,6},{8,9},{9,8},{10,11... | collective-permute-start | bytes 786440 | tf_op jit(solution)/shard_map/ppermute | solution.py:527
  72.3 9.7 %collective-permute-start.18 = (f16[64,1024]{1,0:T(8,128)(2,1)}, f16[64,1024]{1,0:T(8,128)(2,1)}, u32[]{:S(2)}, u32[]{:S(2)}) collective-permute-start(f16[64,1024]{1,0:T(8,128)(2,1)} %fusion.4), channel_id=1, source_target_pairs={{0,2},{1,3},{2,0},{3,1},{4,6},{5,7},{6,4},{7,5},{8,10},{9,11},{10,... | collective-permute-start | bytes 393224 | tf_op jit(solution)/shard_map/ppermute | solution.py:527
  81.1 3.3 %collective-permute-start.17 = (bf16[64,3072]{1,0:T(8,128)(2,1)S(1)}, bf16[64,3072]{1,0:T(8,128)(2,1)S(1)}, u32[]{:S(2)}, u32[]{:S(2)}) collective-permute-start(bf16[64,3072]{1,0:T(8,128)(2,1)S(1)} %fusion.1.refs_0_), channel_id=1, source_target_pairs={{0,1},{1,0},{2,3},{3,2},{4,5},{5,4},{6,7},{7,6},{8,9},{9,8},{10,11... | collective-permute-start | bytes 1179656 | tf_op jit(solution)/shard_map/ppermute | solution.py:527
  83.0 1.4 %collective-permute-start.19 = (bf16[64,1024]{1,0:T(8,128)(2,1)S(1)}, bf16[64,1024]{1,0:T(8,128)(2,1)S(1)}, u32[]{:S(2)}, u32[]{:S(2)}) collective-permute-start(bf16[64,1024]{1,0:T(8,128)(2,1)S(1)} %fusion.5.refs_2_), channel_id=1, source_target_pairs={{0,1},{1,0},{2,3},{3,2},{4,5},{5,4},{6,7},{7,6},{8,9},{9,8},{10,11... | collective-permute-start | bytes 393224 | tf_op jit(solution)/shard_map/ppermute | solution.py:527
